TPU v7x, 32 devices: a whole 2x2x4 slice. The times are simulated.
32 devices in a mesh: src: 4 (over y, core), tgt: 8 (over z, x).
Axes of the slice: x: 2, y: 2, z: 4, core: 2. Of those that a mesh axis runs over, the one named last changes fastest.
Arguments:
- sources: bfloat16 [64, 16384], P(None, ('src', 'tgt')), may hold values from -4 to 4
- targets: bfloat16 [64, 16384], P('src', 'tgt'), may hold values from -1 to 1
- potentials: float32 [16384], P('tgt'), may hold values from -2 to 11
- log_mass: float32 [16384], P('tgt'), may hold values from -3 to 0
Outputs:
- row_potentials: float32 [16384], P(('src', 'tgt'))
All inputs are finite; a program needn't handle non-finite values.
Results may differ from a plain program's by a relative error of at most 0.0003.
Values may be sent and summed in bfloat16 or wider, within the bound.
No kernel may reach another device: no remote copies, remote signals or barrier semaphores. Data moves between devices by JAX's collectives and lax.ppermute only.
A program may use at most 64 MiB of HBM per device.

v0:
```python
import jax
import jax.numpy as jnp
from jax import lax
from jax.sharding import PartitionSpec as P

EPSILON = 0.05


def row_lse(columns, src_sq, tgt_points, tgt_sq, potentials, log_mass):
    crossed = lax.dot_general(
        columns, tgt_points, (((0,), (0,)), ((), ())), preferred_element_type=jnp.float32
    )
    cost = 0.5 * (src_sq[:, None] + tgt_sq[None, :]) - crossed
    scores = (potentials[None, :] - cost) / EPSILON + log_mass[None, :]
    row_top = jnp.max(scores, axis=1)
    row_sum = jnp.sum(jnp.exp(scores - row_top[:, None]), axis=1)
    return (row_top, row_sum)


def on_device(sources, targets, potentials, log_mass):
    full_targets = lax.all_gather(targets, "src", axis=0, tiled=True)
    rows = sources.shape[1]
    width = sources.shape[0]
    wide_targets = full_targets.astype(jnp.float32)
    tgt_sq = jnp.sum(wide_targets * wide_targets, axis=0)

    def block_lse(columns):
        wide = columns.astype(jnp.float32)
        src_sq = jnp.sum(wide * wide, axis=0)
        row_top, row_sum = row_lse(columns, src_sq, full_targets, tgt_sq, potentials, log_mass)
        return row_top + jnp.log(row_sum)

    segment = lax.all_gather(sources, "tgt", axis=1, tiled=True)
    count = segment.shape[1]
    stacked = segment.reshape(width, count // 512, 512).transpose(1, 0, 2)
    partials = lax.map(block_lse, stacked).reshape(count)
    arranged = partials.reshape(lax.axis_size("tgt"), rows)
    arrived = lax.all_to_all(arranged, "tgt", split_axis=0, concat_axis=0, tiled=True)
    row_top = jnp.max(arrived, axis=0)
    owned = row_top + jnp.log(jnp.sum(jnp.exp(arrived - row_top[None, :]), axis=0))
    return -EPSILON * owned


def solution(mesh):
    in_specs = (P(None, ("src", "tgt")), P("src", "tgt"), P("tgt"), P("tgt"))
    out_specs = P(("src", "tgt"))
    return jax.shard_map(
        on_device, mesh=mesh, in_specs=in_specs, out_specs=out_specs, check_vma=False
    )
```

profile of v0, /device:TPU:0, one launch (start us, length us, event | category | flops | bytes accessed | tf_op | source)
XLA Modules:
  0.0 75.5 jit_solution(3011540225558168219)
XLA Ops:
  0.0 7.4 %all_gather.7 = bf16[64,2048]{1,0:T(8,128)(2,1)S(1)} all-gather(bf16[16,2048]{1,0:T(8,128)(2,1)} %param.7), channel_id=1, replica_groups=mesh['src'=4,'tgt'=8] {'src'}, dimensions={0}, use_global_device_ids=true | all-gather | bytes 327680 | tf_op jit(solution)/shard_map/all_gather | solution.py:21
  7.4 0.1 multiply_reduce_fusion.1
  7.5 32.1 %all_gather.6 = bf16[64,4096]{1,0:T(8,128)(2,1)S(1)} all-gather(bf16[64,512]{1,0:T(8,128)(2,1)} %param.6), channel_id=1, replica_groups=mesh['src'=4,'tgt'=8] {'tgt'}, dimensions={1}, use_global_device_ids=true | all-gather | bytes 589824 | tf_op jit(solution)/shard_map/all_gather | solution.py:33
  39.6 0.2 copy.8
  39.8 0.2 copy.6
  39.9 23.2 %while.10 = (s32[]{:T(128)}, f32[8,512]{1,0:T(8,128)S(1)}, f32[2048]{0:T(1024)}, bf16[8,64,512]{2,1,0:T(8,128)(2,1)S(1)}, f32[2048]{0:T(1024)S(1)}, /*index=5*/b...) while((s32[]{:T(128)}, f32[8,512]{1,0:T(8,128)S(1)}, f32[2048]{0:T(1024)}, ...), condition=%wide.region_5.6_spmd, body=%wide.region_1.5_spmd.sunk | while | flops 143752192 | bytes 8826985 | solution.py:36
  40.0 2.1 %fusion.10 = (f32[512]{0:T(512)S(1)}, f32[512,2048]{1,0:T(8,128)S(1)}) fusion(f32[2048]{0:T(1024)} %get-tuple-element.144, bf16[64,2048]{1,0:T(8,128)(2,1)S(1)} %get-tuple-element.143, bf16[8,64,512]{2,1,0:T(8,128)(2,1)S(1)} %get-tuple-element.141, s32[]{:T(128)} %get-tuple-element.129, f32[2048]{0:T(1024)S(1)} %get-tuple-element.142, ...), kind=kOutput, calls=%fused_computation.12.clone.1 | convolution fusion | flops 141557248 | bytes 4550660 | tf_op jit(solution)/shard_map/while/body/eval_jaxpr/dot_general | solution.py:10
  42.0 0.7 exponential_reduce_fusion.2
  42.9 2.1 %fusion.10 = (f32[512]{0:T(512)S(1)}, f32[512,2048]{1,0:T(8,128)S(1)}) fusion(f32[2048]{0:T(1024)} %get-tuple-element.144, bf16[64,2048]{1,0:T(8,128)(2,1)S(1)} %get-tuple-element.143, bf16[8,64,512]{2,1,0:T(8,128)(2,1)S(1)} %get-tuple-element.141, s32[]{:T(128)} %get-tuple-element.129, f32[2048]{0:T(1024)S(1)} %get-tuple-element.142, ...), kind=kOutput, calls=%fused_computation.12.clone.1 | convolution fusion | flops 141557248 | bytes 4550660 | tf_op jit(solution)/shard_map/while/body/eval_jaxpr/dot_general | solution.py:10
  44.9 0.7 exponential_reduce_fusion.2
  45.8 2.1 %fusion.10 = (f32[512]{0:T(512)S(1)}, f32[512,2048]{1,0:T(8,128)S(1)}) fusion(f32[2048]{0:T(1024)} %get-tuple-element.144, bf16[64,2048]{1,0:T(8,128)(2,1)S(1)} %get-tuple-element.143, bf16[8,64,512]{2,1,0:T(8,128)(2,1)S(1)} %get-tuple-element.141, s32[]{:T(128)} %get-tuple-element.129, f32[2048]{0:T(1024)S(1)} %get-tuple-element.142, ...), kind=kOutput, calls=%fused_computation.12.clone.1 | convolution fusion | flops 141557248 | bytes 4550660 | tf_op jit(solution)/shard_map/while/body/eval_jaxpr/dot_general | solution.py:10
  47.8 0.7 exponential_reduce_fusion.2
  48.7 2.1 %fusion.10 = (f32[512]{0:T(512)S(1)}, f32[512,2048]{1,0:T(8,128)S(1)}) fusion(f32[2048]{0:T(1024)} %get-tuple-element.144, bf16[64,2048]{1,0:T(8,128)(2,1)S(1)} %get-tuple-element.143, bf16[8,64,512]{2,1,0:T(8,128)(2,1)S(1)} %get-tuple-element.141, s32[]{:T(128)} %get-tuple-element.129, f32[2048]{0:T(1024)S(1)} %get-tuple-element.142, ...), kind=kOutput, calls=%fused_computation.12.clone.1 | convolution fusion | flops 141557248 | bytes 4550660 | tf_op jit(solution)/shard_map/while/body/eval_jaxpr/dot_general | solution.py:10
  50.7 0.7 exponential_reduce_fusion.2
  51.6 2.1 %fusion.10 = (f32[512]{0:T(512)S(1)}, f32[512,2048]{1,0:T(8,128)S(1)}) fusion(f32[2048]{0:T(1024)} %get-tuple-element.144, bf16[64,2048]{1,0:T(8,128)(2,1)S(1)} %get-tuple-element.143, bf16[8,64,512]{2,1,0:T(8,128)(2,1)S(1)} %get-tuple-element.141, s32[]{:T(128)} %get-tuple-element.129, f32[2048]{0:T(1024)S(1)} %get-tuple-element.142, ...), kind=kOutput, calls=%fused_computation.12.clone.1 | convolution fusion | flops 141557248 | bytes 4550660 | tf_op jit(solution)/shard_map/while/body/eval_jaxpr/dot_general | solution.py:10
  53.6 0.7 exponential_reduce_fusion.2
  54.5 2.1 %fusion.10 = (f32[512]{0:T(512)S(1)}, f32[512,2048]{1,0:T(8,128)S(1)}) fusion(f32[2048]{0:T(1024)} %get-tuple-element.144, bf16[64,2048]{1,0:T(8,128)(2,1)S(1)} %get-tuple-element.143, bf16[8,64,512]{2,1,0:T(8,128)(2,1)S(1)} %get-tuple-element.141, s32[]{:T(128)} %get-tuple-element.129, f32[2048]{0:T(1024)S(1)} %get-tuple-element.142, ...), kind=kOutput, calls=%fused_computation.12.clone.1 | convolution fusion | flops 141557248 | bytes 4550660 | tf_op jit(solution)/shard_map/while/body/eval_jaxpr/dot_general | solution.py:10
  56.5 0.7 exponential_reduce_fusion.2
  57.3 2.1 %fusion.10 = (f32[512]{0:T(512)S(1)}, f32[512,2048]{1,0:T(8,128)S(1)}) fusion(f32[2048]{0:T(1024)} %get-tuple-element.144, bf16[64,2048]{1,0:T(8,128)(2,1)S(1)} %get-tuple-element.143, bf16[8,64,512]{2,1,0:T(8,128)(2,1)S(1)} %get-tuple-element.141, s32[]{:T(128)} %get-tuple-element.129, f32[2048]{0:T(1024)S(1)} %get-tuple-element.142, ...), kind=kOutput, calls=%fused_computation.12.clone.1 | convolution fusion | flops 141557248 | bytes 4550660 | tf_op jit(solution)/shard_map/while/body/eval_jaxpr/dot_general | solution.py:10
  59.4 0.7 exponential_reduce_fusion.2
  60.2 2.1 %fusion.10 = (f32[512]{0:T(512)S(1)}, f32[512,2048]{1,0:T(8,128)S(1)}) fusion(f32[2048]{0:T(1024)} %get-tuple-element.144, bf16[64,2048]{1,0:T(8,128)(2,1)S(1)} %get-tuple-element.143, bf16[8,64,512]{2,1,0:T(8,128)(2,1)S(1)} %get-tuple-element.141, s32[]{:T(128)} %get-tuple-element.129, f32[2048]{0:T(1024)S(1)} %get-tuple-element.142, ...), kind=kOutput, calls=%fused_computation.12.clone.1 | convolution fusion | flops 141557248 | bytes 4550660 | tf_op jit(solution)/shard_map/while/body/eval_jaxpr/dot_general | solution.py:10
  62.3 0.7 exponential_reduce_fusion.2
  63.1 11.8 %all_to_all.12 = f32[8,1,512]{2,1,0:T(1,128)S(1)} all-to-all(f32[8,1,512]{2,1,0:T(1,128)S(1)} %all_to_all.8), channel_id=1, replica_groups=mesh['src'=4,'tgt'=8] {'tgt'}, dimensions={0} | all-to-all | bytes 32768 | tf_op jit(solution)/shard_map/all_to_all | solution.py:38
  74.9 0.6 add_multiply_fusion
  (28 shorter events, 0.9 us)
where the time goes:
time: 76.7 us; the launch traced here: 75.5 us
  blocking collectives  51.3 us (67%)
  matrix products  16.4 us (21%)
  other arithmetic  6.77 us (9%)
  local copies, waits for them, and re-layouts  0.83 us (1%)
    all_gather x1, blocking collectives, on_device(): segment = lax.all_gather(sources, 'tgt', axis=1, tiled=True)  32.1 us
    dot_general x8, matrix products, row_lse(): lax.dot_general(columns, tgt_points, (((0,), (0,)), ((), ())), preferred_...  16.4 us
    all_to_all x1, blocking collectives, on_device(): lax.all_to_all(arranged, 'tgt', split_axis=0, concat_axis=0, tiled=True)  11.8 us
    all_gather x1, blocking collectives, on_device(): full_targets = lax.all_gather(targets, 'src', axis=0, tiled=True)  7.42 us
    reduce_sum x8, other arithmetic, row_lse(): row_sum = jnp.sum(jnp.exp(scores - row_top[:, None]), axis=1)  5.69 us

commit v1 on v0

v1 whole, which is shorter than its diff:
```python
import functools
import math

import jax
import jax.numpy as jnp
from jax import lax
from jax.experimental import pallas as pl
from jax.experimental.pallas import tpu as pltpu
from jax.sharding import PartitionSpec as P

EPSILON = 0.05
RATE = 1.0 / (EPSILON * math.log(2.0))
AXES = ("src", "tgt")
LANES = 128
CHUNK = 128
WIDE = 512


def flip(value, mask):
    n = lax.axis_size("src") * lax.axis_size("tgt")
    return lax.ppermute(value, AXES, [(i, i ^ mask) for i in range(n)])


def split3(value):
    first = value.astype(jnp.bfloat16).astype(jnp.float32)
    rest = value - first
    second = rest.astype(jnp.bfloat16).astype(jnp.float32)
    third = (rest - second).astype(jnp.bfloat16).astype(jnp.float32)
    return first, second, third


def pack_kernel(targets, potentials, log_mass, packed):
    rows, count = targets.shape
    packed[:, :count] = targets[...]
    bias = potentials[...] + EPSILON * log_mass[...]
    parts = split3(bias)
    deep = count // rows
    for k, part in enumerate(parts):
        packed[:, count + k * deep : count + (k + 1) * deep] = part.astype(jnp.bfloat16)


def pack_targets(targets, potentials, log_mass):
    rows, count = targets.shape
    deep = count // rows
    return pl.pallas_call(
        pack_kernel,
        out_shape=jax.ShapeDtypeStruct((rows, count + 3 * deep), jnp.bfloat16),
    )(targets, potentials.reshape(rows, deep), log_mass.reshape(rows, deep))


def score_kernel(src_bits, n_sources, *refs):
    src_refs, (tgt_own, tgt_far, bias_ref) = refs[:n_sources], refs[n_sources : n_sources + 3]
    out_ref, lhs, rhs = refs[n_sources + 3 :]
    count = tgt_own.shape[1]
    width = tgt_own.shape[0] + tgt_far.shape[0]

    step = min(1024, count)
    for start in range(0, count, step):
        cols = slice(start, start + step)
        points = jnp.concatenate([tgt_own[:, cols], tgt_far[:, cols]], axis=0)
        wide = points.astype(jnp.float32)
        half = 0.5 * jnp.sum(wide * wide, axis=0, keepdims=True)
        first, second, third = split3(bias_ref[:, cols] - half)
        place = lax.broadcasted_iota(jnp.int32, (LANES - width, step), 0)
        extra = jnp.where(place == 0, first, jnp.where(place == 1, second, jnp.where(place == 2, third, 0.0)))
        lhs[cols, :] = jnp.concatenate([points, extra.astype(jnp.bfloat16)], axis=0).T

    me = lax.axis_index("src")
    at = 0
    for ref in src_refs:
        points = ref[...].astype(jnp.float32)
        part = width >> src_bits
        blocks = [points[k * part : (k + 1) * part] for k in range(1 << src_bits)]
        for bit in range(src_bits):
            turned = ((me >> bit) & 1) == 1
            blocks = [jnp.where(turned, blocks[k ^ (1 << bit)], blocks[k]) for k in range(1 << src_bits)]
        points = jnp.concatenate(blocks[0::2] + blocks[1::2], axis=0)
        rhs[:width, at : at + ref.shape[1]] = points.astype(jnp.bfloat16)
        at += ref.shape[1]
    rhs[width:, :] = jnp.ones((LANES - width, at), jnp.bfloat16)

    def tile(index, carry):
        cols = pl.ds(pl.multiple_of(index * WIDE, WIDE), WIDE)
        block = rhs[:, cols]

        def product(j):
            found = jnp.dot(lhs[j * CHUNK : (j + 1) * CHUNK, :], block, preferred_element_type=jnp.float32)
            return found.reshape(CHUNK // 8, 8, WIDE)

        scores = product(0)
        top = jnp.max(scores, axis=0) * RATE
        total = jnp.sum(jnp.exp2(scores * RATE - top[None]), axis=0)
        for j in range(1, count // CHUNK):
            scores = product(j)
            higher = jnp.maximum(top, jnp.max(scores, axis=0) * RATE)
            total = total * jnp.exp2(top - higher) + jnp.sum(jnp.exp2(scores * RATE - higher[None]), axis=0)
            top = higher
        row_top = jnp.max(top, axis=0, keepdims=True)
        row_sum = jnp.sum(total * jnp.exp2(top - row_top), axis=0, keepdims=True)
        out_ref[:, cols] = row_top + jnp.log2(row_sum)
        return carry

    lax.fori_loop(0, at // WIDE, tile, 0)


def partial_logs(src_bits, sources, tgt_own, tgt_far, bias):
    count = tgt_own.shape[1]
    rows = sum(s.shape[1] for s in sources)
    return pl.pallas_call(
        functools.partial(score_kernel, src_bits, len(sources)),
        out_shape=jax.ShapeDtypeStruct((1, rows), jnp.float32),
        scratch_shapes=[
            pltpu.VMEM((count, LANES), jnp.bfloat16),
            pltpu.VMEM((LANES, rows), jnp.bfloat16),
        ],
        compiler_params=pltpu.CompilerParams(vmem_limit_bytes=48 << 20),
    )(*sources, tgt_own, tgt_far, bias)


def join(left, right):
    top = jnp.maximum(left, right)
    return top + jnp.log2(1.0 + jnp.exp2(-jnp.abs(left - right)))


def on_device(sources, targets, potentials, log_mass):
    n_src, n_tgt = lax.axis_size("src"), lax.axis_size("tgt")
    src_bits, tgt_bits = n_src.bit_length() - 1, n_tgt.bit_length() - 1
    shared = min(2, tgt_bits)
    count = targets.shape[1]
    owned = sources.shape[1]

    packed = pack_targets(targets, potentials, log_mass)
    held = [sources]
    for bit in range(shared):
        whole = held[0] if len(held) == 1 else jnp.concatenate(held, axis=1)
        held.append(flip(whole, 1 << bit))
    for bit in range(tgt_bits - 1, shared - 1, -1):
        packed = jnp.concatenate([packed, flip(packed, 1 << bit)], axis=1)

    pieces = packed.reshape(packed.shape[0], -1, packed.shape[1] >> (tgt_bits - shared))
    points = pieces[:, :, :count].reshape(targets.shape[0], -1)
    deep = count // targets.shape[0]
    parts = pieces[:, :, count:].astype(jnp.float32).reshape(targets.shape[0], -1, 3, deep)
    bias = (parts[:, :, 0] + parts[:, :, 1]) + parts[:, :, 2]
    bias = bias.transpose(1, 0, 2).reshape(1, -1)

    own = points
    for bit in range(1, src_bits):
        own = jnp.concatenate([own, flip(own, n_tgt << bit)], axis=0)
    far = flip(own, n_tgt)
    logs = partial_logs(src_bits, held, own, far, bias)[0]
    for bit in range(shared - 1, -1, -1):
        half = logs.shape[0] // 2
        logs = join(logs[:half], flip(logs[half:], 1 << bit))
    wide = sources.astype(jnp.float32)
    return 0.5 * jnp.sum(wide * wide, axis=0) - (1.0 / RATE) * logs


def solution(mesh):
    in_specs = (P(None, ("src", "tgt")), P("src", "tgt"), P("tgt"), P("tgt"))
    out_specs = P(("src", "tgt"))
    return jax.shard_map(
        on_device, mesh=mesh, in_specs=in_specs, out_specs=out_specs, check_vma=False
    )
```

time: 76.7 us -> 35.4 us (0.46); the launches traced: 75.5 us -> 35.2 us
  blocking collectives: 51.3 us -> 0 us
  matrix products: 16.4 us -> 0 us
  waiting for transfers between devices: 0 us -> 11.5 us
  starting transfers between devices: 0 us -> 11.4 us
  Pallas kernels: 0 us -> 11.2 us
  other arithmetic: 6.77 us -> 0.7 us
    all_gather x2 -> x0, blocking collectives: 39.5 us -> none  [the longest x1 32.1 us: on_device(): segment = lax.all_gather(sources, 'tgt', axis=1, tiled=True)]
    dot_general x8 -> x0, matrix products: 16.4 us -> none  [row_lse(): lax.dot_general(columns, tgt_points, (((0,), (0,)), ((), ())), preferred_...]
    all_to_all x1 -> x0, blocking collectives: 11.8 us -> none  [on_device(): lax.all_to_all(arranged, 'tgt', split_axis=0, concat_axis=0, tiled=True)]
    ppermute x0 -> x7, waiting for transfers between devices: none -> 11.5 us  [flip(): return lax.ppermute(value, AXES, [(i, i ^ mask) for i in range(n)])]
    ppermute x0 -> x7, starting transfers between devices: none -> 11.4 us  [flip(): return lax.ppermute(value, AXES, [(i, i ^ mask) for i in range(n)])]
    pallas_call x0 -> x2, Pallas kernels: none -> 11.2 us  [the longest x1 9.7 us: partial_logs(): pl.pallas_call(functools.partial(score_kernel, src_bits, len(sources)), o...]
    reduce_sum x18 -> x1, other arithmetic: 6.08 us -> 0.03 us  [on_device(): return 0.5 * jnp.sum(wide * wide, axis=0) - 1.0 / RATE * logs]
  transfers between devices with their start and end apart: 0 -> 7, of which waited for: 0 -> 5; matrix products, arithmetic and copies ran while one was open for 0% -> 1% of each run, Pallas kernels for 0% -> 4%
where the time goes in v1:
time: 35.4 us; the launch traced here: 35.2 us
  waiting for transfers between devices  11.5 us (32%)
  starting transfers between devices  11.4 us (32%)
  Pallas kernels  11.2 us (32%)
  other arithmetic  0.7 us (2%)
    ppermute x7, waiting for transfers between devices, flip(): return lax.ppermute(value, AXES, [(i, i ^ mask) for i in range(n)])  11.5 us
    ppermute x7, starting transfers between devices, flip(): return lax.ppermute(value, AXES, [(i, i ^ mask) for i in range(n)])  11.4 us
    pallas_call x1, Pallas kernels, partial_logs(): pl.pallas_call(functools.partial(score_kernel, src_bits, len(sources)), o...  9.7 us
    pallas_call x1, Pallas kernels, pack_targets(): pl.pallas_call(pack_kernel, out_shape=jax.ShapeDtypeStruct((rows, count +...  1.54 us
  transfers between devices with their start and end apart: 7, of which 5 were waited for; matrix products, arithmetic and copies ran while one was open for 1% of the time, Pallas kernels for 4%

profile of v1, /device:TPU:0, one launch (start us, length us, event | category | flops | bytes accessed | tf_op | source)
XLA Modules:
  0.0 35.2 jit_solution(2367529501426351342)
XLA Ops:
  0.0 2.9 %collective-permute-start = (bf16[64,512]{1,0:T(8,128)(2,1)}, bf16[64,512]{1,0:T(8,128)(2,1)S(1)}, u32[]{:S(2)}, u32[]{:S(2)}) collective-permute-start(bf16[64,512]{1,0:T(8,128)(2,1)} %refs_0_.1), channel_id=1, source_target_pairs={{0,1},{1,0},{2,3},{3,2},{4,5},{5,4},{6,7},{7,6},{8,9},{9,8},{10,11... | collective-permute-start | bytes 196616 | tf_op jit(solution)/shard_map/ppermute | solution.py:21
  2.9 1.5 %shard_map.46 = bf16[16,2432]{1,0:T(8,128)(2,1)} custom-call(bf16[16,2048]{1,0:T(8,128)(2,1)} %targets.1, f32[16,128]{1,0:T(8,128)} %bitcast.18, f32[16,128]{1,0:T(8,128)} %bitcast.19), custom_call_target="tpu_custom_call" | custom-call | tf_op jit(solution)/shard_map/pallas_call | solution.py:45
  4.5 2.6 %collective-permute-start.2 = (bf16[16,2432]{1,0:T(8,128)(2,1)}, bf16[16,2432]{1,0:T(8,128)(2,1)S(1)}, u32[]{:S(2)}, u32[]{:S(2)}) collective-permute-start(bf16[16,2432]{1,0:T(8,128)(2,1)} %shard_map.46), channel_id=1, source_target_pairs={{0,4},{1,5},{2,6},{3,7},{4,0},{5,1},{6,2},{7,3},{8,12},{9,13},{10,... | collective-permute-start | bytes 233480 | tf_op jit(solution)/shard_map/ppermute | solution.py:21
  7.1 0.0 collective-permute-done.refs_1_
  7.1 0.0 copy-done
  7.1 1.6 %collective-permute-start.1 = (bf16[64,1024]{1,0:T(8,128)(2,1)S(1)}, bf16[64,1024]{1,0:T(8,128)(2,1)S(1)}, u32[]{:S(2)}, u32[]{:S(2)}) collective-permute-start(bf16[64,1024]{1,0:T(8,128)(2,1)S(1)} %pad_maximum_fusion.1), channel_id=1, source_target_pairs={{0,2},{1,3},{2,0},{3,1},{4,6},{5,7},{6,4},{7,5},{8,10},{9,11},{10,... | collective-permute-start | bytes 393224 | tf_op jit(solution)/shard_map/ppermute | solution.py:21
  8.7 1.9 %collective-permute-done.2 = bf16[16,2432]{1,0:T(8,128)(2,1)S(1)} collective-permute-done((bf16[16,2432]{1,0:T(8,128)(2,1)}, bf16[16,2432]{1,0:T(8,128)(2,1)S(1)}, u32[]{:S(2)}, u32[]{:S(2)}) %collective-permute-start.2) | collective-permute-done | bytes 77856 | tf_op jit(solution)/shard_map/ppermute | solution.py:21
  10.7 0.0 copy-done.2
  10.7 0.0 copy-start.1
  10.7 0.1 slice.44
  10.9 1.6 %collective-permute-start.3 = (bf16[16,4096]{1,0:T(8,128)(2,1)S(1)}, bf16[16,4096]{1,0:T(8,128)(2,1)S(1)}, u32[]{:S(2)}, u32[]{:S(2)}) collective-permute-start(bf16[16,4096]{1,0:T(8,128)(2,1)S(1)} %bitcast.14), channel_id=1, source_target_pairs={{0,16},{1,17},{2,18},{3,19},{4,20},{5,21},{6,22},{7,23},{8,24},{9,... | collective-permute-start | bytes 393224 | tf_op jit(solution)/shard_map/ppermute | solution.py:21
  12.5 0.0 copy-done.1
  12.5 0.0 slice-start
  12.5 3.4 %collective-permute-done.3 = bf16[16,4096]{1,0:T(8,128)(2,1)S(1)} collective-permute-done((bf16[16,4096]{1,0:T(8,128)(2,1)S(1)}, bf16[16,4096]{1,0:T(8,128)(2,1)S(1)}, u32[]{:S(2)}, u32[]{:S(2)}) %collective-permute-start.3) | collective-permute-done | bytes 131104 | tf_op jit(solution)/shard_map/ppermute | solution.py:21
  15.9 0.1 collective-permute-start.4
  16.0 0.0 slice-done
  16.1 0.0 collective-permute-done.1.refs_2_
  16.1 1.4 %collective-permute-done.4.refs_4_ = bf16[32,4096]{1,0:T(8,128)(2,1)S(1)} collective-permute-done((bf16[32,4096]{1,0:T(8,128)(2,1)S(1)}, bf16[32,4096]{1,0:T(8,128)(2,1)S(1)}, u32[]{:S(2)}, u32[]{:S(2)}) %collective-permute-start.4) | collective-permute-done | bytes 262176 | tf_op jit(solution)/shard_map/ppermute | solution.py:21
  17.5 9.7 %shard_map.47 = f32[1,2048]{1,0:T(1,128)S(1)} custom-call(bf16[64,512]{1,0:T(8,128)(2,1)S(1)} %copy-done, bf16[64,512]{1,0:T(8,128)(2,1)S(1)} %collective-permute-done.refs_1_, bf16[64,1024]{1,0:T(8,128)(2,1)S(1)} %collective-permute-done.1.refs_2_, bf16[32,4096]{1,0:T(8,128)(2,1)S(1)} %constant_dynamic-update-slice_fusion.refs_3_, ...), custom_call_target="tpu_custom_call" | custom-call | tf_op jit(solution)/shard_map/pallas_call | solution.py:109
  27.2 1.8 %collective-permute-start.5 = (f32[1024]{0:T(1024)S(1)}, f32[1024]{0:T(1024)S(1)}, u32[]{:S(2)}, u32[]{:S(2)}) collective-permute-start(f32[1024]{0:T(1024)S(1)} %bitcast.20), channel_id=1, source_target_pairs={{0,2},{1,3},{2,0},{3,1},{4,6},{5,7},{6,4},{7,5},{8,10},{9,11},{10,... | collective-permute-start | bytes 12296 | tf_op jit(solution)/shard_map/ppermute | solution.py:21
  29.1 1.8 %collective-permute-done.5 = f32[1024]{0:T(1024)S(1)} collective-permute-done((f32[1024]{0:T(1024)S(1)}, f32[1024]{0:T(1024)S(1)}, u32[]{:S(2)}, u32[]{:S(2)}) %collective-permute-start.5) | collective-permute-done | bytes 4128 | tf_op jit(solution)/shard_map/ppermute | solution.py:21
  30.9 0.8 %collective-permute-start.6 = (f32[512]{0:T(512)S(1)}, f32[512]{0:T(512)S(1)}, u32[]{:S(2)}, u32[]{:S(2)}) collective-permute-start(f32[512]{0:T(512)S(1)} %slice.43), channel_id=1, source_target_pairs={{0,1},{1,0},{2,3},{3,2},{4,5},{5,4},{6,7},{7,6},{8,9},{9,8},{10,11... | collective-permute-start | bytes 6152 | tf_op jit(solution)/shard_map/ppermute | solution.py:21
  31.7 2.9 %collective-permute-done.6 = f32[512]{0:T(512)S(1)} collective-permute-done((f32[512]{0:T(512)S(1)}, f32[512]{0:T(512)S(1)}, u32[]{:S(2)}, u32[]{:S(2)}) %collective-permute-start.6) | collective-permute-done | bytes 2080 | tf_op jit(solution)/shard_map/ppermute | solution.py:21
  34.6 0.6 %multiply_subtract_fusion = f32[512]{0:T(512)} fusion(f32[512]{0:T(512)S(1)} %collective-permute-done.6, f32[1024]{0:T(1024)S(1)} %multiply_add_fusion, f32[512]{0:T(512)S(1)} %multiply_reduce_fusion), kind=kLoop, calls=%fused_computation.9 | loop fusion | flops 5632 | bytes 8192 | tf_op jit(solution)/shard_map/sub | solution.py:156
  (15 shorter events, 0.2 us)
Async XLA Ops:
  0.0 7.1 %collective-permute-start = (bf16[64,512]{1,0:T(8,128)(2,1)}, bf16[64,512]{1,0:T(8,128)(2,1)S(1)}, u32[]{:S(2)}, u32[]{:S(2)}) collective-permute-start(bf16[64,512]{1,0:T(8,128)(2,1)} %refs_0_.1), channel_id=1, source_target_pairs={{0,1},{1,0},{2,3},{3,2},{4,5},{5,4},{6,7},{7,6},{8,9},{9,8},{10,11... | collective-permute-start | bytes 196616 | tf_op jit(solution)/shard_map/ppermute | solution.py:21
  2.9 4.1 %copy-start = (bf16[64,512]{1,0:T(8,128)(2,1)S(1)}, bf16[64,512]{1,0:T(8,128)(2,1)}, u32[]{:S(2)}) copy-start(bf16[64,512]{1,0:T(8,128)(2,1)} %refs_0_.1) | copy-start | bytes 196612
  4.5 6.2 %copy-start.2 = (bf16[16,2432]{1,0:T(8,128)(2,1)S(1)}, bf16[16,2432]{1,0:T(8,128)(2,1)}, u32[]{:S(2)}) copy-start(bf16[16,2432]{1,0:T(8,128)(2,1)} %shard_map.46) | copy-start | bytes 233476
  4.5 6.2 %collective-permute-start.2 = (bf16[16,2432]{1,0:T(8,128)(2,1)}, bf16[16,2432]{1,0:T(8,128)(2,1)S(1)}, u32[]{:S(2)}, u32[]{:S(2)}) collective-permute-start(bf16[16,2432]{1,0:T(8,128)(2,1)} %shard_map.46), channel_id=1, source_target_pairs={{0,4},{1,5},{2,6},{3,7},{4,0},{5,1},{6,2},{7,3},{8,12},{9,13},{10,... | collective-permute-start | bytes 233480 | tf_op jit(solution)/shard_map/ppermute | solution.py:21
  7.1 9.0 %collective-permute-start.1 = (bf16[64,1024]{1,0:T(8,128)(2,1)S(1)}, bf16[64,1024]{1,0:T(8,128)(2,1)S(1)}, u32[]{:S(2)}, u32[]{:S(2)}) collective-permute-start(bf16[64,1024]{1,0:T(8,128)(2,1)S(1)} %pad_maximum_fusion.1), channel_id=1, source_target_pairs={{0,2},{1,3},{2,0},{3,1},{4,6},{5,7},{6,4},{7,5},{8,10},{9,11},{10,... | collective-permute-start | bytes 393224 | tf_op jit(solution)/shard_map/ppermute | solution.py:21
  10.7 1.8 %copy-start.1 = (bf16[16,2,2432]{2,1,0:T(2,128)(2,1)}, bf16[16,2,2432]{2,1,0:T(2,128)(2,1)S(1)}, u32[]{:S(2)}) copy-start(bf16[16,2,2432]{2,1,0:T(2,128)(2,1)S(1)} %reshape.27) | copy-start | bytes 466948
  10.9 5.0 %collective-permute-start.3 = (bf16[16,4096]{1,0:T(8,128)(2,1)S(1)}, bf16[16,4096]{1,0:T(8,128)(2,1)S(1)}, u32[]{:S(2)}, u32[]{:S(2)}) collective-permute-start(bf16[16,4096]{1,0:T(8,128)(2,1)S(1)} %bitcast.14), channel_id=1, source_target_pairs={{0,16},{1,17},{2,18},{3,19},{4,20},{5,21},{6,22},{7,23},{8,24},{9,... | collective-permute-start | bytes 393224 | tf_op jit(solution)/shard_map/ppermute | solution.py:21
  12.5 3.5 %slice-start = ((bf16[16,2,2432]{2,1,0:T(2,128)(2,1)}), bf16[16,2,384]{2,1,0:T(2,128)(2,1)S(1)}, s32[]{:S(2)}) async-start(bf16[16,2,2432]{2,1,0:T(2,128)(2,1)} %copy-done.1), calls=%async_computation | async-start | bytes 49152 | tf_op jit(solution)/shard_map/slice | solution.py:143
  15.9 1.6 %collective-permute-start.4 = (bf16[32,4096]{1,0:T(8,128)(2,1)S(1)}, bf16[32,4096]{1,0:T(8,128)(2,1)S(1)}, u32[]{:S(2)}, u32[]{:S(2)}) collective-permute-start(bf16[32,4096]{1,0:T(8,128)(2,1)S(1)} %constant_dynamic-update-slice_fusion.refs_3_), channel_id=1, source_target_pairs={{0,8},{1,9},{2,10},{3,11},{4,12},{5,13},{6,14},{7,15},{8,0},{9,1},... | collective-permute-start | bytes 786440 | tf_op jit(solution)/shard_map/ppermute | solution.py:21
  27.2 3.7 %collective-permute-start.5 = (f32[1024]{0:T(1024)S(1)}, f32[1024]{0:T(1024)S(1)}, u32[]{:S(2)}, u32[]{:S(2)}) collective-permute-start(f32[1024]{0:T(1024)S(1)} %bitcast.20), channel_id=1, source_target_pairs={{0,2},{1,3},{2,0},{3,1},{4,6},{5,7},{6,4},{7,5},{8,10},{9,11},{10,... | collective-permute-start | bytes 12296 | tf_op jit(solution)/shard_map/ppermute | solution.py:21
  30.9 3.7 %collective-permute-start.6 = (f32[512]{0:T(512)S(1)}, f32[512]{0:T(512)S(1)}, u32[]{:S(2)}, u32[]{:S(2)}) collective-permute-start(f32[512]{0:T(512)S(1)} %slice.43), channel_id=1, source_target_pairs={{0,1},{1,0},{2,3},{3,2},{4,5},{5,4},{6,7},{7,6},{8,9},{9,8},{10,11... | collective-permute-start | bytes 6152 | tf_op jit(solution)/shard_map/ppermute | solution.py:21

commit v2 on v1

v2 whole, which is shorter than its diff:
```python
import functools
import math

import jax
import jax.numpy as jnp
from jax import lax
from jax.experimental import pallas as pl
from jax.experimental.pallas import tpu as pltpu
from jax.sharding import PartitionSpec as P

EPSILON = 0.05
RATE = 1.0 / (EPSILON * math.log(2.0))
AXES = ("src", "tgt")
LANES = 128
CHUNK = 128
WIDE = 512
VMEM = pl.BlockSpec(memory_space=pltpu.VMEM)
ANY = pl.BlockSpec(memory_space=pl.ANY)


def flip(value, mask):
    n = lax.axis_size("src") * lax.axis_size("tgt")
    return lax.ppermute(value, AXES, [(i, i ^ mask) for i in range(n)])


def split3(value):
    first = value.astype(jnp.bfloat16).astype(jnp.float32)
    rest = value - first
    second = rest.astype(jnp.bfloat16).astype(jnp.float32)
    third = (rest - second).astype(jnp.bfloat16).astype(jnp.float32)
    return first, second, third


def pack_kernel(targets, potentials, log_mass, packed, potentials_here, log_mass_here, sems):
    rows, count = targets.shape
    copies = [
        pltpu.make_async_copy(potentials, potentials_here, sems.at[0]),
        pltpu.make_async_copy(log_mass, log_mass_here, sems.at[1]),
        pltpu.make_async_copy(targets, packed.at[:, pl.ds(0, count)], sems.at[2]),
    ]
    for copy in copies:
        copy.start()
    copies[0].wait()
    copies[1].wait()
    bias = potentials_here[...] + EPSILON * log_mass_here[...]
    deep = count // rows
    for k, part in enumerate(split3(bias)):
        packed[:, count + k * deep : count + (k + 1) * deep] = part.astype(jnp.bfloat16)
    copies[2].wait()


def pack_targets(targets, potentials, log_mass):
    rows, count = targets.shape
    deep = count // rows
    return pl.pallas_call(
        pack_kernel,
        out_shape=jax.ShapeDtypeStruct((rows, count + 3 * deep), jnp.bfloat16),
        in_specs=[ANY] * 3,
        out_specs=VMEM,
        scratch_shapes=[
            pltpu.VMEM((rows, deep), jnp.float32),
            pltpu.VMEM((rows, deep), jnp.float32),
            pltpu.SemaphoreType.DMA((3,)),
        ],
    )(targets, potentials.reshape(rows, deep), log_mass.reshape(rows, deep))


def place_targets(tgt_own, tgt_far, bias_ref, lhs):
    count = tgt_own.shape[1]
    width = tgt_own.shape[0] + tgt_far.shape[0]
    step = min(1024, count)
    for start in range(0, count, step):
        cols = slice(start, start + step)
        points = jnp.concatenate([tgt_own[:, cols], tgt_far[:, cols]], axis=0)
        wide = points.astype(jnp.float32)
        half = 0.5 * jnp.sum(wide * wide, axis=0, keepdims=True)
        first, second, third = split3(bias_ref[:, cols] - half)
        place = lax.broadcasted_iota(jnp.int32, (LANES - width, step), 0)
        extra = jnp.where(place < 6, 1.0, 0.0)
        for k, part in enumerate((first, second, third)):
            extra = jnp.where(place == k, part, extra)
        lhs[cols, :] = jnp.concatenate([points, extra.astype(jnp.bfloat16)], axis=0).T


def place_sources(src_bits, src_ref, rhs):
    width, rows = src_ref.shape
    points = src_ref[...].astype(jnp.float32)
    me = lax.axis_index("src")
    part = width >> src_bits
    blocks = [points[k * part : (k + 1) * part] for k in range(1 << src_bits)]
    for bit in range(src_bits):
        turned = ((me >> bit) & 1) == 1
        blocks = [jnp.where(turned, blocks[k ^ (1 << bit)], blocks[k]) for k in range(1 << src_bits)]
    points = jnp.concatenate(blocks[0::2] + blocks[1::2], axis=0)
    rhs[:width, :] = points.astype(jnp.bfloat16)
    place = lax.broadcasted_iota(jnp.int32, (LANES - width, rows), 0)
    rhs[width:, :] = jnp.where(place < 3, 1.0, 0.0).astype(jnp.bfloat16)


def log_sums(width, lhs, rhs, out_ref):
    count, rows = lhs.shape[0], rhs.shape[1]

    def product(j, block):
        chunk = pl.ds(pl.multiple_of(j * CHUNK, CHUNK), CHUNK)
        found = jnp.dot(lhs[chunk, :], block, preferred_element_type=jnp.float32)
        return found.reshape(CHUNK // 8, 8, found.shape[1])

    place = lax.broadcasted_iota(jnp.int32, (LANES - width, WIDE), 0)
    for start in range(0, rows, WIDE):
        cols = slice(start, start + WIDE)
        high = jnp.max(jnp.max(product(0, rhs[:, cols]), axis=0), axis=0, keepdims=True)
        extra = jnp.where(place < 3, 1.0, 0.0)
        for k, part in enumerate(split3(-high)):
            extra = jnp.where(place == 3 + k, part, extra)
        rhs[width:, cols] = extra.astype(jnp.bfloat16)
        out_ref[:, cols] = high * RATE
    worst = jnp.zeros((1, WIDE), jnp.float32)
    for start in range(0, rows, WIDE):
        cols = slice(start, start + WIDE)
        block = rhs[:, cols]
        total = jnp.zeros((8, WIDE), jnp.float32)
        for j in range(count // CHUNK):
            total = total + jnp.sum(jnp.exp2(product(j, block) * RATE), axis=0)
        row_sum = jnp.sum(total, axis=0, keepdims=True)
        out_ref[:, cols] += jnp.log2(row_sum)
        worst = jnp.maximum(worst, row_sum)

    @pl.when(jnp.logical_not(jnp.max(worst) < jnp.inf))
    def _():
        for start in range(0, rows, WIDE):
            cols = slice(start, start + WIDE)
            extra = jnp.where(place < 3, 1.0, 0.0)
            rhs[width:, cols] = extra.astype(jnp.bfloat16)
            block = rhs[:, cols]

            def step(j, carry):
                top, total = carry
                scores = product(j, block) * RATE
                higher = jnp.maximum(top, jnp.max(scores, axis=0))
                total = total * jnp.exp2(top - higher) + jnp.sum(jnp.exp2(scores - higher[None]), axis=0)
                return higher, total

            first = jnp.max(product(0, block) * RATE, axis=0)
            top, total = lax.fori_loop(0, count // CHUNK, step, (first, jnp.zeros_like(first)))
            row_top = jnp.max(top, axis=0, keepdims=True)
            row_sum = jnp.sum(total * jnp.exp2(top - row_top), axis=0, keepdims=True)
            out_ref[:, cols] = row_top + jnp.log2(row_sum)


def first_kernel(src_bits, src_ref, tgt_own, tgt_far, bias_ref, out_ref, lhs, rhs):
    place_targets(tgt_own, tgt_far, bias_ref, lhs)
    place_sources(src_bits, src_ref, rhs)
    log_sums(src_ref.shape[0], lhs, rhs, out_ref)


def next_kernel(src_bits, src_ref, lhs, out_ref, rhs):
    place_sources(src_bits, src_ref, rhs)
    log_sums(src_ref.shape[0], lhs, rhs, out_ref)


def estimate(rows, count):
    return pl.CostEstimate(flops=2 * rows * count * LANES, bytes_accessed=2 * count * LANES, transcendentals=rows * count)


def first_logs(src_bits, sources, tgt_own, tgt_far, bias):
    count, rows = tgt_own.shape[1], sources.shape[1]
    return pl.pallas_call(
        functools.partial(first_kernel, src_bits),
        out_shape=(
            jax.ShapeDtypeStruct((1, rows), jnp.float32),
            jax.ShapeDtypeStruct((count, LANES), jnp.bfloat16),
        ),
        in_specs=[VMEM] * 4,
        out_specs=(VMEM, VMEM),
        scratch_shapes=[pltpu.VMEM((LANES, rows), jnp.bfloat16)],
        cost_estimate=estimate(rows, count),
        compiler_params=pltpu.CompilerParams(vmem_limit_bytes=48 << 20),
    )(sources, tgt_own, tgt_far, bias)


def next_logs(src_bits, sources, lhs):
    count, rows = lhs.shape[0], sources.shape[1]
    return pl.pallas_call(
        functools.partial(next_kernel, src_bits),
        out_shape=jax.ShapeDtypeStruct((1, rows), jnp.float32),
        in_specs=[VMEM] * 2,
        out_specs=VMEM,
        scratch_shapes=[pltpu.VMEM((LANES, rows), jnp.bfloat16)],
        cost_estimate=estimate(rows, count),
        compiler_params=pltpu.CompilerParams(vmem_limit_bytes=48 << 20),
    )(sources, lhs)


def join(left, right):
    top = jnp.maximum(left, right)
    return top + jnp.log2(1.0 + jnp.exp2(-jnp.abs(left - right)))


def on_device(sources, targets, potentials, log_mass):
    n_src, n_tgt = lax.axis_size("src"), lax.axis_size("tgt")
    src_bits, tgt_bits = n_src.bit_length() - 1, n_tgt.bit_length() - 1
    shared = min(2, tgt_bits)
    masks = [(1 << bit) | n_tgt for bit in range(shared)]
    count = targets.shape[1]

    packed = pack_targets(targets, potentials, log_mass)
    own_sources, packed = lax.optimization_barrier((sources, packed))
    for bit in range(tgt_bits - 1, shared - 1, -1):
        packed = jnp.concatenate([packed, flip(packed, 1 << bit)], axis=1)
    held = [own_sources]
    for mask in masks:
        whole = held[0] if len(held) == 1 else jnp.concatenate(held, axis=1)
        held.append(flip(whole, mask))

    pieces = packed.reshape(packed.shape[0], -1, packed.shape[1] >> (tgt_bits - shared))
    points = pieces[:, :, :count].reshape(targets.shape[0], -1)
    deep = count // targets.shape[0]
    parts = pieces[:, :, count:].astype(jnp.float32).reshape(targets.shape[0], -1, 3, deep)
    bias = (parts[:, :, 0] + parts[:, :, 1]) + parts[:, :, 2]
    bias = bias.transpose(1, 0, 2).reshape(1, -1)

    own = points
    for bit in range(1, src_bits):
        own = jnp.concatenate([own, flip(own, n_tgt << bit)], axis=0)
    far = flip(own, n_tgt)

    owned = sources.shape[1]
    arrived = []
    logs, lhs = first_logs(src_bits, held[-1], own, far, bias)
    for k in range(shared, 0, -1):
        for other in arrived:
            logs = join(logs, other[:, owned << (k - 1) : owned << k])
        arrived.append(flip(logs, masks[k - 1]))
        logs = next_logs(src_bits, held[k - 1], lhs)
    for other in arrived:
        logs = join(logs, other[:, :owned])
    wide = sources.astype(jnp.float32)
    return 0.5 * jnp.sum(wide * wide, axis=0) - (1.0 / RATE) * logs[0]


def solution(mesh):
    in_specs = (P(None, ("src", "tgt")), P("src", "tgt"), P("tgt"), P("tgt"))
    out_specs = P(("src", "tgt"))
    return jax.shard_map(
        on_device, mesh=mesh, in_specs=in_specs, out_specs=out_specs, check_vma=False
    )
```

time: 35.4 us -> 57.5 us (1.62)
  Pallas kernels: 11.2 us -> 38.7 us
  starting transfers between devices: 11.4 us -> 8.1 us
  waiting for transfers between devices: 11.5 us -> 9.37 us
    pallas_call x1 -> x3, Pallas kernels: 9.7 us -> 37.2 us  [the longest x2 18.6 us: next_logs(): pl.pallas_call(functools.partial(next_kernel, src_bits), out_shape=jax.Sh...]
    ppermute x7, starting transfers between devices: 11.4 us -> 8.1 us  [flip(): return lax.ppermute(value, AXES, [(i, i ^ mask) for i in range(n)])]
    ppermute x7, waiting for transfers between devices: 11.5 us -> 9.37 us  [flip(): return lax.ppermute(value, AXES, [(i, i ^ mask) for i in range(n)])]
  transfers between devices with their start and end apart: 7 -> 7, of which waited for: 5 -> 3; matrix products, arithmetic and copies ran while one was open for 1% -> 1% of each run, Pallas kernels for 4% -> 32%
where the time goes in v2:
time: 57.5 us; the launch traced here: 57.4 us
  Pallas kernels  38.7 us (67%)
  waiting for transfers between devices  9.37 us (16%)
  starting transfers between devices  8.1 us (14%)
  other arithmetic  0.73 us (1%)
    pallas_call x2, Pallas kernels, next_logs(): pl.pallas_call(functools.partial(next_kernel, src_bits), out_shape=jax.Sh...  18.6 us
    pallas_call x1, Pallas kernels, first_logs(): pl.pallas_call(functools.partial(first_kernel, src_bits), out_shape=(jax....  18.5 us
    ppermute x7, waiting for transfers between devices, flip(): return lax.ppermute(value, AXES, [(i, i ^ mask) for i in range(n)])  9.37 us
    ppermute x7, starting transfers between devices, flip(): return lax.ppermute(value, AXES, [(i, i ^ mask) for i in range(n)])  8.1 us
    pallas_call x1, Pallas kernels, pack_targets(): pl.pallas_call(pack_kernel, out_shape=jax.ShapeDtypeStruct((rows, count +...  1.56 us
  transfers between devices with their start and end apart: 7, of which 3 were waited for; matrix products, arithmetic and copies ran while one was open for 1% of the time, Pallas kernels for 32%

profile of v2, /device:TPU:0, one launch (start us, length us, event | category | flops | bytes accessed | tf_op | source)
XLA Modules:
  0.0 57.4 jit_solution(11986861325639554217)
XLA Ops:
  0.0 1.6 %shard_map.46 = bf16[16,2432]{1,0:T(8,128)(2,1)} custom-call(bf16[16,2048]{1,0:T(8,128)(2,1)} %targets.1, f32[16,128]{1,0:T(8,128)} %bitcast.16, f32[16,128]{1,0:T(8,128)} %bitcast.17), custom_call_target="tpu_custom_call" | custom-call | tf_op jit(solution)/shard_map/pallas_call | solution.py:55
  1.6 4.1 %collective-permute-start.2 = (bf16[16,2432]{1,0:T(8,128)(2,1)}, bf16[16,2432]{1,0:T(8,128)(2,1)S(1)}, u32[]{:S(2)}, u32[]{:S(2)}) collective-permute-start(bf16[16,2432]{1,0:T(8,128)(2,1)} %shard_map.46), channel_id=1, source_target_pairs={{0,4},{1,5},{2,6},{3,7},{4,0},{5,1},{6,2},{7,3},{8,12},{9,13},{10,... | collective-permute-start | bytes 233480 | tf_op jit(solution)/shard_map/ppermute | solution.py:23
  5.7 0.0 copy-done
  5.7 0.7 %collective-permute-start = (bf16[64,512]{1,0:T(8,128)(2,1)S(1)}, bf16[64,512]{1,0:T(8,128)(2,1)S(1)}, u32[]{:S(2)}, u32[]{:S(2)}) collective-permute-start(bf16[64,512]{1,0:T(8,128)(2,1)S(1)} %copy-done), channel_id=1, source_target_pairs={{0,9},{1,8},{2,11},{3,10},{4,13},{5,12},{6,15},{7,14},{8,1},{9,0},... | collective-permute-start | bytes 196616 | tf_op jit(solution)/shard_map/ppermute | solution.py:23
  6.4 3.7 %collective-permute-done.src_ref = bf16[64,512]{1,0:T(8,128)(2,1)S(1)} collective-permute-done((bf16[64,512]{1,0:T(8,128)(2,1)S(1)}, bf16[64,512]{1,0:T(8,128)(2,1)S(1)}, u32[]{:S(2)}, u32[]{:S(2)}) %collective-permute-start) | collective-permute-done | bytes 65568 | tf_op jit(solution)/shard_map/ppermute | solution.py:23
  10.0 1.4 %collective-permute-start.1 = (bf16[64,1024]{1,0:T(8,128)(2,1)S(1)}, bf16[64,1024]{1,0:T(8,128)(2,1)S(1)}, u32[]{:S(2)}, u32[]{:S(2)}) collective-permute-start(bf16[64,1024]{1,0:T(8,128)(2,1)S(1)} %pad_maximum_fusion.1), channel_id=1, source_target_pairs={{0,10},{1,11},{2,8},{3,9},{4,14},{5,15},{6,12},{7,13},{8,2},{9,3},... | collective-permute-start | bytes 393224 | tf_op jit(solution)/shard_map/ppermute | solution.py:23
  11.4 0.0 collective-permute-done.2
  11.4 0.0 copy-done.2
  11.5 0.0 copy-start.1
  11.5 0.1 slice.28
  11.6 1.6 %collective-permute-start.3 = (bf16[16,4096]{1,0:T(8,128)(2,1)S(1)}, bf16[16,4096]{1,0:T(8,128)(2,1)S(1)}, u32[]{:S(2)}, u32[]{:S(2)}) collective-permute-start(bf16[16,4096]{1,0:T(8,128)(2,1)S(1)} %bitcast.13), channel_id=1, source_target_pairs={{0,16},{1,17},{2,18},{3,19},{4,20},{5,21},{6,22},{7,23},{8,24},{9,... | collective-permute-start | bytes 393224 | tf_op jit(solution)/shard_map/ppermute | solution.py:23
  13.2 0.0 slice-start
  13.3 4.3 %collective-permute-done.3 = bf16[16,4096]{1,0:T(8,128)(2,1)S(1)} collective-permute-done((bf16[16,4096]{1,0:T(8,128)(2,1)S(1)}, bf16[16,4096]{1,0:T(8,128)(2,1)S(1)}, u32[]{:S(2)}, u32[]{:S(2)}) %collective-permute-start.3) | collective-permute-done | bytes 131104 | tf_op jit(solution)/shard_map/ppermute | solution.py:23
  17.5 0.1 collective-permute-start.4
  17.7 0.0 collective-permute-done.1.src_ref
  17.7 1.4 %collective-permute-done.4.tgt_far = bf16[32,4096]{1,0:T(8,128)(2,1)S(1)} collective-permute-done((bf16[32,4096]{1,0:T(8,128)(2,1)S(1)}, bf16[32,4096]{1,0:T(8,128)(2,1)S(1)}, u32[]{:S(2)}, u32[]{:S(2)}) %collective-permute-start.4) | collective-permute-done | bytes 262176 | tf_op jit(solution)/shard_map/ppermute | solution.py:23
  19.1 18.5 %shard_map.47 = (f32[1,1024]{1,0:T(1,128)S(1)}, bf16[4096,128]{1,0:T(8,128)(2,1)S(1)}) custom-call(bf16[64,1024]{1,0:T(8,128)(2,1)S(1)} %collective-permute-done.1.src_ref, bf16[32,4096]{1,0:T(8,128)(2,1)S(1)} %constant_dynamic-update-slice_fusion.tgt_own, bf16[32,4096]{1,0:T(8,128)(2,1)S(1)} %collective-permute-done.4.tgt_far, f32[1,4096]{1,0:T(1,128)S(1)} %bitcast.12), custom_call_target="tpu_custom_call" | custom-call | flops 1073741824 | bytes 1048576 | tf_op jit(solution)/shard_map/pallas_call | solution.py:167
  37.7 0.3 collective-permute-start.5
  38.0 9.3 %shard_map.49 = f32[1,512]{1,0:T(1,128)S(1)} custom-call(bf16[64,512]{1,0:T(8,128)(2,1)S(1)} %collective-permute-done.src_ref, bf16[4096,128]{1,0:T(8,128)(2,1)S(1)} %get-tuple-element.11.lhs), custom_call_target="tpu_custom_call" | custom-call | flops 536870912 | bytes 1048576 | tf_op jit(solution)/shard_map/pallas_call | solution.py:183
  47.3 0.0 collective-permute-done.5
  47.3 0.1 collective-permute-start.6
  47.4 9.3 %shard_map.48 = f32[1,512]{1,0:T(1,128)S(1)} custom-call(bf16[64,512]{1,0:T(8,128)(2,1)S(1)} %copy-done, bf16[4096,128]{1,0:T(8,128)(2,1)S(1)} %get-tuple-element.11.lhs), custom_call_target="tpu_custom_call" | custom-call | flops 536870912 | bytes 1048576 | tf_op jit(solution)/shard_map/pallas_call | solution.py:183
  56.7 0.0 collective-permute-done.6
  56.8 0.6 %multiply_subtract_fusion = f32[512]{0:T(512)} fusion(f32[512]{0:T(512)S(1)} %bitcast.18, f32[512]{0:T(512)S(1)} %multiply_reduce_fusion), kind=kLoop, calls=%fused_computation.10 | loop fusion | flops 1024 | bytes 6144 | tf_op jit(solution)/shard_map/sub | solution.py:238
  (16 shorter events, 0.3 us)
Async XLA Ops:
  0.0 5.7 %copy-start = (bf16[64,512]{1,0:T(8,128)(2,1)S(1)}, bf16[64,512]{1,0:T(8,128)(2,1)}, u32[]{:S(2)}) copy-start(bf16[64,512]{1,0:T(8,128)(2,1)} %src_ref) | copy-start | bytes 196612
  1.6 9.8 %collective-permute-start.2 = (bf16[16,2432]{1,0:T(8,128)(2,1)}, bf16[16,2432]{1,0:T(8,128)(2,1)S(1)}, u32[]{:S(2)}, u32[]{:S(2)}) collective-permute-start(bf16[16,2432]{1,0:T(8,128)(2,1)} %shard_map.46), channel_id=1, source_target_pairs={{0,4},{1,5},{2,6},{3,7},{4,0},{5,1},{6,2},{7,3},{8,12},{9,13},{10,... | collective-permute-start | bytes 233480 | tf_op jit(solution)/shard_map/ppermute | solution.py:23
  5.7 4.3 %collective-permute-start = (bf16[64,512]{1,0:T(8,128)(2,1)S(1)}, bf16[64,512]{1,0:T(8,128)(2,1)S(1)}, u32[]{:S(2)}, u32[]{:S(2)}) collective-permute-start(bf16[64,512]{1,0:T(8,128)(2,1)S(1)} %copy-done), channel_id=1, source_target_pairs={{0,9},{1,8},{2,11},{3,10},{4,13},{5,12},{6,15},{7,14},{8,1},{9,0},... | collective-permute-start | bytes 196616 | tf_op jit(solution)/shard_map/ppermute | solution.py:23
  6.4 5.0 %copy-start.2 = (bf16[16,2432]{1,0:T(8,128)(2,1)S(1)}, bf16[16,2432]{1,0:T(8,128)(2,1)}, u32[]{:S(2)}) copy-start(bf16[16,2432]{1,0:T(8,128)(2,1)} %shard_map.46) | copy-start | bytes 233476
  10.0 7.7 %collective-permute-start.1 = (bf16[64,1024]{1,0:T(8,128)(2,1)S(1)}, bf16[64,1024]{1,0:T(8,128)(2,1)S(1)}, u32[]{:S(2)}, u32[]{:S(2)}) collective-permute-start(bf16[64,1024]{1,0:T(8,128)(2,1)S(1)} %pad_maximum_fusion.1), channel_id=1, source_target_pairs={{0,10},{1,11},{2,8},{3,9},{4,14},{5,15},{6,12},{7,13},{8,2},{9,3},... | collective-permute-start | bytes 393224 | tf_op jit(solution)/shard_map/ppermute | solution.py:23
  11.5 1.8 %copy-start.1 = (bf16[16,2,2432]{2,1,0:T(2,128)(2,1)}, bf16[16,2,2432]{2,1,0:T(2,128)(2,1)S(1)}, u32[]{:S(2)}) copy-start(bf16[16,2,2432]{2,1,0:T(2,128)(2,1)S(1)} %reshape.27) | copy-start | bytes 466948
  11.6 5.9 %collective-permute-start.3 = (bf16[16,4096]{1,0:T(8,128)(2,1)S(1)}, bf16[16,4096]{1,0:T(8,128)(2,1)S(1)}, u32[]{:S(2)}, u32[]{:S(2)}) collective-permute-start(bf16[16,4096]{1,0:T(8,128)(2,1)S(1)} %bitcast.13), channel_id=1, source_target_pairs={{0,16},{1,17},{2,18},{3,19},{4,20},{5,21},{6,22},{7,23},{8,24},{9,... | collective-permute-start | bytes 393224 | tf_op jit(solution)/shard_map/ppermute | solution.py:23
  13.2 4.4 %slice-start = ((bf16[16,2,2432]{2,1,0:T(2,128)(2,1)}), bf16[16,2,384]{2,1,0:T(2,128)(2,1)S(1)}, s32[]{:S(2)}) async-start(bf16[16,2,2432]{2,1,0:T(2,128)(2,1)} %copy-done.1), calls=%async_computation | async-start | bytes 49152 | tf_op jit(solution)/shard_map/slice | solution.py:218
  17.5 1.6 %collective-permute-start.4 = (bf16[32,4096]{1,0:T(8,128)(2,1)S(1)}, bf16[32,4096]{1,0:T(8,128)(2,1)S(1)}, u32[]{:S(2)}, u32[]{:S(2)}) collective-permute-start(bf16[32,4096]{1,0:T(8,128)(2,1)S(1)} %constant_dynamic-update-slice_fusion.tgt_own), channel_id=1, source_target_pairs={{0,8},{1,9},{2,10},{3,11},{4,12},{5,13},{6,14},{7,15},{8,0},{9,1},... | collective-permute-start | bytes 786440 | tf_op jit(solution)/shard_map/ppermute | solution.py:23
  37.7 9.6 %collective-permute-start.5 = (f32[1,1024]{1,0:T(1,128)S(1)}, f32[1,1024]{1,0:T(1,128)S(1)}, u32[]{:S(2)}, u32[]{:S(2)}) collective-permute-start(f32[1,1024]{1,0:T(1,128)S(1)} %get-tuple-element.12), channel_id=1, source_target_pairs={{0,10},{1,11},{2,8},{3,9},{4,14},{5,15},{6,12},{7,13},{8,2},{9,3},... | collective-permute-start | bytes 12296 | tf_op jit(solution)/shard_map/ppermute | solution.py:23
  47.3 9.4 %collective-permute-start.6 = (f32[1,512]{1,0:T(1,128)S(1)}, f32[1,512]{1,0:T(1,128)S(1)}, u32[]{:S(2)}, u32[]{:S(2)}) collective-permute-start(f32[1,512]{1,0:T(1,128)S(1)} %multiply_add_fusion), channel_id=1, source_target_pairs={{0,9},{1,8},{2,11},{3,10},{4,13},{5,12},{6,15},{7,14},{8,1},{9,0},... | collective-permute-start | bytes 6152 | tf_op jit(solution)/shard_map/ppermute | solution.py:23

commit v3 on v2

--- a/solution.py
+++ b/solution.py
@@ -31,38 +31,30 @@
     return first, second, third
 
 
-def pack_kernel(targets, potentials, log_mass, packed, potentials_here, log_mass_here, sems):
-    rows, count = targets.shape
+def load_kernel(targets, potentials, log_mass, targets_here, bias, scratch, sems):
     copies = [
-        pltpu.make_async_copy(potentials, potentials_here, sems.at[0]),
-        pltpu.make_async_copy(log_mass, log_mass_here, sems.at[1]),
-        pltpu.make_async_copy(targets, packed.at[:, pl.ds(0, count)], sems.at[2]),
+        pltpu.make_async_copy(potentials, scratch.at[0], sems.at[0]),
+        pltpu.make_async_copy(log_mass, scratch.at[1], sems.at[1]),
+        pltpu.make_async_copy(targets, targets_here, sems.at[2]),
     ]
     for copy in copies:
         copy.start()
     copies[0].wait()
     copies[1].wait()
-    bias = potentials_here[...] + EPSILON * log_mass_here[...]
-    deep = count // rows
-    for k, part in enumerate(split3(bias)):
-        packed[:, count + k * deep : count + (k + 1) * deep] = part.astype(jnp.bfloat16)
+    bias[...] = scratch[0] + EPSILON * scratch[1]
     copies[2].wait()
 
 
-def pack_targets(targets, potentials, log_mass):
-    rows, count = targets.shape
-    deep = count // rows
-    return pl.pallas_call(
-        pack_kernel,
-        out_shape=jax.ShapeDtypeStruct((rows, count + 3 * deep), jnp.bfloat16),
+def load(targets, potentials, log_mass):
+    rows = potentials.shape[0] // LANES
+    return pl.pallas_call(
+        load_kernel,
+        out_shape=(pltpu.VMEM(targets.shape, targets.dtype), pltpu.VMEM((rows, LANES), jnp.float32)),
         in_specs=[ANY] * 3,
-        out_specs=VMEM,
-        scratch_shapes=[
-            pltpu.VMEM((rows, deep), jnp.float32),
-            pltpu.VMEM((rows, deep), jnp.float32),
-            pltpu.SemaphoreType.DMA((3,)),
-        ],
-    )(targets, potentials.reshape(rows, deep), log_mass.reshape(rows, deep))
+        out_specs=(VMEM,) * 2,
+        scratch_shapes=[pltpu.VMEM((2, rows, LANES), jnp.float32), pltpu.SemaphoreType.DMA((3,))],
+        compiler_params=pltpu.CompilerParams(vmem_limit_bytes=8 << 20),
+    )(targets, potentials.reshape(rows, LANES), log_mass.reshape(rows, LANES))
 
 
 def place_targets(tgt_own, tgt_far, bias_ref, lhs):
@@ -95,6 +87,23 @@
     rhs[:width, :] = points.astype(jnp.bfloat16)
     place = lax.broadcasted_iota(jnp.int32, (LANES - width, rows), 0)
     rhs[width:, :] = jnp.where(place < 3, 1.0, 0.0).astype(jnp.bfloat16)
+
+
+def sources_kernel(src_bits, *refs):
+    count = len(refs) // 2
+    for src_ref, rhs in zip(refs[:count], refs[count:], strict=True):
+        place_sources(src_bits, src_ref, rhs)
+
+
+def placed_sources(src_bits, held):
+    return pl.pallas_call(
+        functools.partial(sources_kernel, src_bits),
+        out_shape=tuple(pltpu.VMEM((LANES, piece.shape[1]), jnp.bfloat16) for piece in held),
+        in_specs=[VMEM] * len(held),
+        out_specs=(VMEM,) * len(held),
+        cost_estimate=pl.CostEstimate(flops=4 << 30, bytes_accessed=0, transcendentals=0),
+        compiler_params=pltpu.CompilerParams(vmem_limit_bytes=8 << 20),
+    )(*held)
 
 
 def log_sums(width, lhs, rhs, out_ref):
@@ -147,53 +156,56 @@
             out_ref[:, cols] = row_top + jnp.log2(row_sum)
 
 
-def first_kernel(src_bits, src_ref, tgt_own, tgt_far, bias_ref, out_ref, lhs, rhs):
+def first_kernel(placed, tgt_own, tgt_far, bias_ref, out_ref, lhs, rhs):
     place_targets(tgt_own, tgt_far, bias_ref, lhs)
-    place_sources(src_bits, src_ref, rhs)
-    log_sums(src_ref.shape[0], lhs, rhs, out_ref)
-
-
-def next_kernel(src_bits, src_ref, lhs, out_ref, rhs):
-    place_sources(src_bits, src_ref, rhs)
-    log_sums(src_ref.shape[0], lhs, rhs, out_ref)
+    rhs[...] = placed[...]
+    log_sums(tgt_own.shape[0] + tgt_far.shape[0], lhs, rhs, out_ref)
+
+
+def next_kernel(width, placed, lhs, out_ref, rhs):
+    rhs[...] = placed[...]
+    log_sums(width, lhs, rhs, out_ref)
 
 
 def estimate(rows, count):
     return pl.CostEstimate(flops=2 * rows * count * LANES, bytes_accessed=2 * count * LANES, transcendentals=rows * count)
 
 
-def first_logs(src_bits, sources, tgt_own, tgt_far, bias):
-    count, rows = tgt_own.shape[1], sources.shape[1]
-    return pl.pallas_call(
-        functools.partial(first_kernel, src_bits),
-        out_shape=(
-            jax.ShapeDtypeStruct((1, rows), jnp.float32),
-            jax.ShapeDtypeStruct((count, LANES), jnp.bfloat16),
-        ),
+def first_logs(placed, tgt_own, tgt_far, bias):
+    count, rows = tgt_own.shape[1], placed.shape[1]
+    return pl.pallas_call(
+        first_kernel,
+        out_shape=(pltpu.VMEM((1, rows), jnp.float32), pltpu.VMEM((count, LANES), jnp.bfloat16)),
         in_specs=[VMEM] * 4,
         out_specs=(VMEM, VMEM),
         scratch_shapes=[pltpu.VMEM((LANES, rows), jnp.bfloat16)],
         cost_estimate=estimate(rows, count),
         compiler_params=pltpu.CompilerParams(vmem_limit_bytes=48 << 20),
-    )(sources, tgt_own, tgt_far, bias)
-
-
-def next_logs(src_bits, sources, lhs):
-    count, rows = lhs.shape[0], sources.shape[1]
-    return pl.pallas_call(
-        functools.partial(next_kernel, src_bits),
-        out_shape=jax.ShapeDtypeStruct((1, rows), jnp.float32),
+    )(placed, tgt_own, tgt_far, bias)
+
+
+def next_logs(width, placed, lhs):
+    count, rows = lhs.shape[0], placed.shape[1]
+    return pl.pallas_call(
+        functools.partial(next_kernel, width),
+        out_shape=pltpu.VMEM((1, rows), jnp.float32),
         in_specs=[VMEM] * 2,
         out_specs=VMEM,
         scratch_shapes=[pltpu.VMEM((LANES, rows), jnp.bfloat16)],
         cost_estimate=estimate(rows, count),
         compiler_params=pltpu.CompilerParams(vmem_limit_bytes=48 << 20),
-    )(sources, lhs)
+    )(placed, lhs)
 
 
 def join(left, right):
     top = jnp.maximum(left, right)
     return top + jnp.log2(1.0 + jnp.exp2(-jnp.abs(left - right)))
+
+
+def gather(value, masks, axis):
+    for mask in masks:
+        value = jnp.concatenate([value, flip(value, mask)], axis=axis)
+    return value
 
 
 def on_device(sources, targets, potentials, log_mass):
@@ -201,37 +213,36 @@
     src_bits, tgt_bits = n_src.bit_length() - 1, n_tgt.bit_length() - 1
     shared = min(2, tgt_bits)
     masks = [(1 << bit) | n_tgt for bit in range(shared)]
-    count = targets.shape[1]
-
-    packed = pack_targets(targets, potentials, log_mass)
-    own_sources, packed = lax.optimization_barrier((sources, packed))
-    for bit in range(tgt_bits - 1, shared - 1, -1):
-        packed = jnp.concatenate([packed, flip(packed, 1 << bit)], axis=1)
-    held = [own_sources]
+    col_masks = [1 << bit for bit in range(tgt_bits - 1, shared - 1, -1)]
+    row_masks = [n_tgt << bit for bit in range(1, src_bits)]
+
+    targets_here, bias = load(targets, potentials, log_mass)
+    held = [sources]
     for mask in masks:
         whole = held[0] if len(held) == 1 else jnp.concatenate(held, axis=1)
         held.append(flip(whole, mask))
-
-    pieces = packed.reshape(packed.shape[0], -1, packed.shape[1] >> (tgt_bits - shared))
-    points = pieces[:, :, :count].reshape(targets.shape[0], -1)
-    deep = count // targets.shape[0]
-    parts = pieces[:, :, count:].astype(jnp.float32).reshape(targets.shape[0], -1, 3, deep)
-    bias = (parts[:, :, 0] + parts[:, :, 1]) + parts[:, :, 2]
-    bias = bias.transpose(1, 0, 2).reshape(1, -1)
-
-    own = points
-    for bit in range(1, src_bits):
-        own = jnp.concatenate([own, flip(own, n_tgt << bit)], axis=0)
+    if len(col_masks) == 1 and len(row_masks) == 1:
+        beside = flip(targets, col_masks[0])
+        beside, bias = lax.optimization_barrier((beside, bias))
+        below = flip(targets, row_masks[0])
+        corner = flip(beside, row_masks[0])
+        upper = jnp.concatenate([targets_here, beside], axis=1)
+        lower = jnp.concatenate([below, corner], axis=1)
+        own = jnp.concatenate([upper, lower], axis=0)
+    else:
+        own = gather(gather(targets_here, col_masks, 1), row_masks, 0)
+    bias = gather(bias, col_masks, 0).reshape(1, -1)
     far = flip(own, n_tgt)
+    placed = placed_sources(src_bits, held)
 
     owned = sources.shape[1]
     arrived = []
-    logs, lhs = first_logs(src_bits, held[-1], own, far, bias)
+    logs, lhs = first_logs(placed[-1], own, far, bias)
     for k in range(shared, 0, -1):
         for other in arrived:
             logs = join(logs, other[:, owned << (k - 1) : owned << k])
         arrived.append(flip(logs, masks[k - 1]))
-        logs = next_logs(src_bits, held[k - 1], lhs)
+        logs = next_logs(sources.shape[0], placed[k - 1], lhs)
     for other in arrived:
         logs = join(logs, other[:, :owned])
     wide = sources.astype(jnp.float32)

time: 57.5 us -> 56.5 us (0.983); the launches traced: 57.4 us -> 55.6 us
  waiting for transfers between devices: 9.37 us -> 3.74 us
  starting transfers between devices: 8.1 us -> 11.5 us
  local copies, waits for them, and re-layouts: 0.23 us -> 2.24 us
  Pallas kernels: 38.7 us -> 37.3 us
    ppermute x7 -> x9, waiting for transfers between devices: 9.37 us -> 3.74 us  [flip(): return lax.ppermute(value, AXES, [(i, i ^ mask) for i in range(n)])]
    ppermute x7 -> x9, starting transfers between devices: 8.1 us -> 11.5 us  [flip(): return lax.ppermute(value, AXES, [(i, i ^ mask) for i in range(n)])]
    unnamed x8, local copies, waits for them, and re-layouts: 0.06 us -> 2.24 us
    pallas_call x4 -> x5, Pallas kernels: 38.7 us -> 37.3 us  [the longest x2 18.6 us: next_logs(): pl.pallas_call(functools.partial(next_kernel, width), out_shape=pltpu.VME...]
  transfers between devices with their start and end apart: 7 -> 9, of which waited for: 3 -> 2; matrix products, arithmetic and copies ran while one was open for 1% -> 0% of each run, Pallas kernels for 32% -> 34%
where the time goes in v3:
time: 56.5 us; the launch traced here: 55.6 us
  Pallas kernels  37.3 us (66%)
  starting transfers between devices  11.5 us (20%)
  waiting for transfers between devices  3.74 us (7%)
  local copies, waits for them, and re-layouts  2.24 us (4%)
  other arithmetic  0.71 us (1%)
    pallas_call x2, Pallas kernels, next_logs(): pl.pallas_call(functools.partial(next_kernel, width), out_shape=pltpu.VME...  18.6 us
    pallas_call x1, Pallas kernels, first_logs(): pl.pallas_call(first_kernel, out_shape=(pltpu.VMEM((1, rows), jnp.float32...  18.5 us
    ppermute x9, starting transfers between devices, flip(): return lax.ppermute(value, AXES, [(i, i ^ mask) for i in range(n)])  11.5 us
    ppermute x9, waiting for transfers between devices, flip(): return lax.ppermute(value, AXES, [(i, i ^ mask) for i in range(n)])  3.74 us
    unnamed x8, local copies, waits for them, and re-layouts  2.24 us
  transfers between devices with their start and end apart: 9, of which 2 were waited for; matrix products, arithmetic and copies ran while one was open for 0% of the time, Pallas kernels for 34%

profile of v3, /device:TPU:0, one launch (start us, length us, event | category | flops | bytes accessed | tf_op | source)
XLA Modules:
  0.0 55.6 jit_solution(8593917756579174482)
XLA Ops:
  0.0 4.0 %collective-permute-start.2 = (bf16[16,2048]{1,0:T(8,128)(2,1)}, bf16[16,2048]{1,0:T(8,128)(2,1)S(1)}, u32[]{:S(2)}, u32[]{:S(2)}) collective-permute-start(bf16[16,2048]{1,0:T(8,128)(2,1)} %targets.1), channel_id=1, source_target_pairs={{0,4},{1,5},{2,6},{3,7},{4,0},{5,1},{6,2},{7,3},{8,12},{9,13},{10,... | collective-permute-start | bytes 196616 | tf_op jit(solution)/shard_map/ppermute | solution.py:23
  4.0 1.5 %collective-permute-start.3 = (bf16[16,2048]{1,0:T(8,128)(2,1)}, bf16[16,2048]{1,0:T(8,128)(2,1)S(1)}, u32[]{:S(2)}, u32[]{:S(2)}) collective-permute-start(bf16[16,2048]{1,0:T(8,128)(2,1)} %targets.1), channel_id=1, source_target_pairs={{0,16},{1,17},{2,18},{3,19},{4,20},{5,21},{6,22},{7,23},{8,24},{9,... | collective-permute-start | bytes 196616 | tf_op jit(solution)/shard_map/ppermute | solution.py:23
  5.6 0.4 collective-permute-start
  5.9 0.8 %copy-done.1 = bf16[16,2048]{1,0:T(8,128)(2,1)S(1)} copy-done((bf16[16,2048]{1,0:T(8,128)(2,1)S(1)}, bf16[16,2048]{1,0:T(8,128)(2,1)}, u32[]{:S(2)}) %copy-start.1) | copy-done | bytes 65560
  6.8 0.7 %copy-done.2 = f32[2048]{0:T(1024)S(1)} copy-done((f32[2048]{0:T(1024)S(1)}, f32[2048]{0:T(1024)}, u32[]{:S(2)}) %copy-start.2) | copy-done | bytes 8216
  7.5 0.7 %copy-done.3 = f32[2048]{0:T(1024)S(1)} copy-done((f32[2048]{0:T(1024)S(1)}, f32[2048]{0:T(1024)}, u32[]{:S(2)}) %copy-start.3) | copy-done | bytes 8216
  8.2 0.1 shard_map.47
  8.3 0.0 collective-permute-done.2
  8.3 1.3 %collective-permute-start.4 = (bf16[16,2048]{1,0:T(8,128)(2,1)S(1)}, bf16[16,2048]{1,0:T(8,128)(2,1)S(1)}, u32[]{:S(2)}, u32[]{:S(2)}) collective-permute-start(bf16[16,2048]{1,0:T(8,128)(2,1)S(1)} %collective-permute-done.2), channel_id=1, source_target_pairs={{0,16},{1,17},{2,18},{3,19},{4,20},{5,21},{6,22},{7,23},{8,24},{9,... | collective-permute-start | bytes 196616 | tf_op jit(solution)/shard_map/ppermute | solution.py:23
  9.6 1.3 %collective-permute-start.6 = (f32[16,128]{1,0:T(8,128)S(1)}, f32[16,128]{1,0:T(8,128)S(1)}, u32[]{:S(2)}, u32[]{:S(2)}) collective-permute-start(f32[16,128]{1,0:T(8,128)S(1)} %get-tuple-element.19), channel_id=1, source_target_pairs={{0,4},{1,5},{2,6},{3,7},{4,0},{5,1},{6,2},{7,3},{8,12},{9,13},{10,... | collective-permute-start | bytes 24584 | tf_op jit(solution)/shard_map/ppermute | solution.py:23
  11.0 1.2 %collective-permute-start.1 = (bf16[64,1024]{1,0:T(8,128)(2,1)S(1)}, bf16[64,1024]{1,0:T(8,128)(2,1)S(1)}, u32[]{:S(2)}, u32[]{:S(2)}) collective-permute-start(bf16[64,1024]{1,0:T(8,128)(2,1)S(1)} %pad_maximum_fusion), channel_id=1, source_target_pairs={{0,10},{1,11},{2,8},{3,9},{4,14},{5,15},{6,12},{7,13},{8,2},{9,3},... | collective-permute-start | bytes 393224 | tf_op jit(solution)/shard_map/ppermute | solution.py:23
  12.2 2.1 %collective-permute-done.6 = f32[16,128]{1,0:T(8,128)S(1)} collective-permute-done((f32[16,128]{1,0:T(8,128)S(1)}, f32[16,128]{1,0:T(8,128)S(1)}, u32[]{:S(2)}, u32[]{:S(2)}) %collective-permute-start.6) | collective-permute-done | bytes 8224 | tf_op jit(solution)/shard_map/ppermute | solution.py:23
  14.3 0.1 collective-permute-start.5
  14.4 1.6 %collective-permute-done.1.refs_2_ = bf16[64,1024]{1,0:T(8,128)(2,1)S(1)} collective-permute-done((bf16[64,1024]{1,0:T(8,128)(2,1)S(1)}, bf16[64,1024]{1,0:T(8,128)(2,1)S(1)}, u32[]{:S(2)}, u32[]{:S(2)}) %collective-permute-start.1) | collective-permute-done | bytes 131104 | tf_op jit(solution)/shard_map/ppermute | solution.py:23
  16.0 0.1 shard_map.46
  16.1 0.0 collective-permute-done.5.tgt_far
  16.1 18.5 %shard_map.48 = (f32[1,1024]{1,0:T(1,128)S(1)}, bf16[4096,128]{1,0:T(8,128)(2,1)S(1)}) custom-call(bf16[128,1024]{1,0:T(8,128)(2,1)S(1)} %get-tuple-element.15.placed, bf16[32,4096]{1,0:T(8,128)(2,1)S(1)} %maximum_maximum_fusion.tgt_own, bf16[32,4096]{1,0:T(8,128)(2,1)S(1)} %collective-permute-done.5.tgt_far, f32[1,4096]{1,0:T(1,128)S(1)} %bitcast.4), custom_call_target="tpu_custom_call" | custom-call | flops 1073741824 | bytes 1048576 | tf_op jit(solution)/shard_map/pallas_call | solution.py:176
  34.7 1.6 %collective-permute-start.7 = (f32[1,1024]{1,0:T(1,128)S(1)}, f32[1,1024]{1,0:T(1,128)S(1)}, u32[]{:S(2)}, u32[]{:S(2)}) collective-permute-start(f32[1,1024]{1,0:T(1,128)S(1)} %get-tuple-element.21), channel_id=1, source_target_pairs={{0,10},{1,11},{2,8},{3,9},{4,14},{5,15},{6,12},{7,13},{8,2},{9,3},... | collective-permute-start | bytes 12296 | tf_op jit(solution)/shard_map/ppermute | solution.py:23
  36.3 9.3 %shard_map.50 = f32[1,512]{1,0:T(1,128)S(1)} custom-call(bf16[128,512]{1,0:T(8,128)(2,1)S(1)} %get-tuple-element.22.placed, bf16[4096,128]{1,0:T(8,128)(2,1)S(1)} %get-tuple-element.20.lhs), custom_call_target="tpu_custom_call" | custom-call | flops 536870912 | bytes 1048576 | tf_op jit(solution)/shard_map/pallas_call | solution.py:189
  45.6 0.0 collective-permute-done.7
  45.6 0.1 collective-permute-start.8
  45.7 9.3 %shard_map.49 = f32[1,512]{1,0:T(1,128)S(1)} custom-call(bf16[128,512]{1,0:T(8,128)(2,1)S(1)} %get-tuple-element.14.placed, bf16[4096,128]{1,0:T(8,128)(2,1)S(1)} %get-tuple-element.20.lhs), custom_call_target="tpu_custom_call" | custom-call | flops 536870912 | bytes 1048576 | tf_op jit(solution)/shard_map/pallas_call | solution.py:189
  55.0 0.0 collective-permute-done.8
  55.1 0.6 %multiply_subtract_fusion = f32[512]{0:T(512)} fusion(f32[512]{0:T(512)S(1)} %bitcast.7, f32[512]{0:T(512)S(1)} %multiply_reduce_fusion), kind=kLoop, calls=%fused_computation.6 | loop fusion | flops 1024 | bytes 6144 | tf_op jit(solution)/shard_map/sub | solution.py:249
  (14 shorter events, 0.1 us)
Async XLA Ops:
  0.0 8.3 %copy-start = (bf16[64,512]{1,0:T(8,128)(2,1)S(1)}, bf16[64,512]{1,0:T(8,128)(2,1)}, u32[]{:S(2)}) copy-start(bf16[64,512]{1,0:T(8,128)(2,1)} %refs_0_.1) | copy-start | bytes 196612
  0.0 8.3 %collective-permute-start.2 = (bf16[16,2048]{1,0:T(8,128)(2,1)}, bf16[16,2048]{1,0:T(8,128)(2,1)S(1)}, u32[]{:S(2)}, u32[]{:S(2)}) collective-permute-start(bf16[16,2048]{1,0:T(8,128)(2,1)} %targets.1), channel_id=1, source_target_pairs={{0,4},{1,5},{2,6},{3,7},{4,0},{5,1},{6,2},{7,3},{8,12},{9,13},{10,... | collective-permute-start | bytes 196616 | tf_op jit(solution)/shard_map/ppermute | solution.py:23
  4.0 10.3 %collective-permute-start.3 = (bf16[16,2048]{1,0:T(8,128)(2,1)}, bf16[16,2048]{1,0:T(8,128)(2,1)S(1)}, u32[]{:S(2)}, u32[]{:S(2)}) collective-permute-start(bf16[16,2048]{1,0:T(8,128)(2,1)} %targets.1), channel_id=1, source_target_pairs={{0,16},{1,17},{2,18},{3,19},{4,20},{5,21},{6,22},{7,23},{8,24},{9,... | collective-permute-start | bytes 196616 | tf_op jit(solution)/shard_map/ppermute | solution.py:23
  5.6 5.4 %collective-permute-start = (bf16[64,512]{1,0:T(8,128)(2,1)}, bf16[64,512]{1,0:T(8,128)(2,1)S(1)}, u32[]{:S(2)}, u32[]{:S(2)}) collective-permute-start(bf16[64,512]{1,0:T(8,128)(2,1)} %refs_0_.1), channel_id=1, source_target_pairs={{0,9},{1,8},{2,11},{3,10},{4,13},{5,12},{6,15},{7,14},{8,1},{9,0},... | collective-permute-start | bytes 196616 | tf_op jit(solution)/shard_map/ppermute | solution.py:23
  5.9 0.8 %copy-start.1 = (bf16[16,2048]{1,0:T(8,128)(2,1)S(1)}, bf16[16,2048]{1,0:T(8,128)(2,1)}, u32[]{:S(2)}) copy-start(bf16[16,2048]{1,0:T(8,128)(2,1)} %targets.1) | copy-start | bytes 196612
  6.8 0.7 %copy-start.2 = (f32[2048]{0:T(1024)S(1)}, f32[2048]{0:T(1024)}, u32[]{:S(2)}) copy-start(f32[2048]{0:T(1024)} %param.6) | copy-start | bytes 24580
  7.5 0.7 %copy-start.3 = (f32[2048]{0:T(1024)S(1)}, f32[2048]{0:T(1024)}, u32[]{:S(2)}) copy-start(f32[2048]{0:T(1024)} %param.7) | copy-start | bytes 24580
  8.3 6.0 %collective-permute-start.4 = (bf16[16,2048]{1,0:T(8,128)(2,1)S(1)}, bf16[16,2048]{1,0:T(8,128)(2,1)S(1)}, u32[]{:S(2)}, u32[]{:S(2)}) collective-permute-start(bf16[16,2048]{1,0:T(8,128)(2,1)S(1)} %collective-permute-done.2), channel_id=1, source_target_pairs={{0,16},{1,17},{2,18},{3,19},{4,20},{5,21},{6,22},{7,23},{8,24},{9,... | collective-permute-start | bytes 196616 | tf_op jit(solution)/shard_map/ppermute | solution.py:23
  9.6 4.7 %collective-permute-start.6 = (f32[16,128]{1,0:T(8,128)S(1)}, f32[16,128]{1,0:T(8,128)S(1)}, u32[]{:S(2)}, u32[]{:S(2)}) collective-permute-start(f32[16,128]{1,0:T(8,128)S(1)} %get-tuple-element.19), channel_id=1, source_target_pairs={{0,4},{1,5},{2,6},{3,7},{4,0},{5,1},{6,2},{7,3},{8,12},{9,13},{10,... | collective-permute-start | bytes 24584 | tf_op jit(solution)/shard_map/ppermute | solution.py:23
  11.0 5.1 %collective-permute-start.1 = (bf16[64,1024]{1,0:T(8,128)(2,1)S(1)}, bf16[64,1024]{1,0:T(8,128)(2,1)S(1)}, u32[]{:S(2)}, u32[]{:S(2)}) collective-permute-start(bf16[64,1024]{1,0:T(8,128)(2,1)S(1)} %pad_maximum_fusion), channel_id=1, source_target_pairs={{0,10},{1,11},{2,8},{3,9},{4,14},{5,15},{6,12},{7,13},{8,2},{9,3},... | collective-permute-start | bytes 393224 | tf_op jit(solution)/shard_map/ppermute | solution.py:23
  14.3 1.8 %collective-permute-start.5 = (bf16[32,4096]{1,0:T(8,128)(2,1)S(1)}, bf16[32,4096]{1,0:T(8,128)(2,1)S(1)}, u32[]{:S(2)}, u32[]{:S(2)}) collective-permute-start(bf16[32,4096]{1,0:T(8,128)(2,1)S(1)} %maximum_maximum_fusion.tgt_own), channel_id=1, source_target_pairs={{0,8},{1,9},{2,10},{3,11},{4,12},{5,13},{6,14},{7,15},{8,0},{9,1},... | collective-permute-start | bytes 786440 | tf_op jit(solution)/shard_map/ppermute | solution.py:23
  34.7 10.9 %collective-permute-start.7 = (f32[1,1024]{1,0:T(1,128)S(1)}, f32[1,1024]{1,0:T(1,128)S(1)}, u32[]{:S(2)}, u32[]{:S(2)}) collective-permute-start(f32[1,1024]{1,0:T(1,128)S(1)} %get-tuple-element.21), channel_id=1, source_target_pairs={{0,10},{1,11},{2,8},{3,9},{4,14},{5,15},{6,12},{7,13},{8,2},{9,3},... | collective-permute-start | bytes 12296 | tf_op jit(solution)/shard_map/ppermute | solution.py:23
  45.6 9.4 %collective-permute-start.8 = (f32[1,512]{1,0:T(1,128)S(1)}, f32[1,512]{1,0:T(1,128)S(1)}, u32[]{:S(2)}, u32[]{:S(2)}) collective-permute-start(f32[1,512]{1,0:T(1,128)S(1)} %multiply_add_fusion), channel_id=1, source_target_pairs={{0,9},{1,8},{2,11},{3,10},{4,13},{5,12},{6,15},{7,14},{8,1},{9,0},... | collective-permute-start | bytes 6152 | tf_op jit(solution)/shard_map/ppermute | solution.py:23

commit v4 on v3

--- a/solution.py
+++ b/solution.py
@@ -31,7 +31,7 @@
     return first, second, third
 
 
-def load_kernel(targets, potentials, log_mass, targets_here, bias, scratch, sems):
+def load_kernel(targets, potentials, log_mass, targets_here, bias, parts, scratch, sems):
     copies = [
         pltpu.make_async_copy(potentials, scratch.at[0], sems.at[0]),
         pltpu.make_async_copy(log_mass, scratch.at[1], sems.at[1]),
@@ -42,19 +42,26 @@
     copies[0].wait()
     copies[1].wait()
     bias[...] = scratch[0] + EPSILON * scratch[1]
+    deep = bias.shape[1]
+    for k, part in enumerate(split3(bias[...])):
+        parts[:, k * deep : (k + 1) * deep] = part.astype(jnp.bfloat16)
     copies[2].wait()
 
 
 def load(targets, potentials, log_mass):
-    rows = potentials.shape[0] // LANES
+    rows, count = targets.shape
+    deep = count // rows
     return pl.pallas_call(
         load_kernel,
-        out_shape=(pltpu.VMEM(targets.shape, targets.dtype), pltpu.VMEM((rows, LANES), jnp.float32)),
+        out_shape=(
+            pltpu.VMEM((rows, count), targets.dtype),
+            pltpu.VMEM((rows, deep), jnp.float32),
+            pltpu.VMEM((rows, 3 * deep), jnp.bfloat16),
+        ),
         in_specs=[ANY] * 3,
-        out_specs=(VMEM,) * 2,
-        scratch_shapes=[pltpu.VMEM((2, rows, LANES), jnp.float32), pltpu.SemaphoreType.DMA((3,))],
-        compiler_params=pltpu.CompilerParams(vmem_limit_bytes=8 << 20),
-    )(targets, potentials.reshape(rows, LANES), log_mass.reshape(rows, LANES))
+        out_specs=(VMEM,) * 3,
+        scratch_shapes=[pltpu.VMEM((2, rows, deep), jnp.float32), pltpu.SemaphoreType.DMA((3,))],
+    )(targets, potentials.reshape(rows, deep), log_mass.reshape(rows, deep))
 
 
 def place_targets(tgt_own, tgt_far, bias_ref, lhs):
@@ -212,26 +219,30 @@
     n_src, n_tgt = lax.axis_size("src"), lax.axis_size("tgt")
     src_bits, tgt_bits = n_src.bit_length() - 1, n_tgt.bit_length() - 1
     shared = min(2, tgt_bits)
-    masks = [(1 << bit) | n_tgt for bit in range(shared)]
+    masks = [(1 << bit) | n_tgt for bit in range(shared - 1, -1, -1)]
     col_masks = [1 << bit for bit in range(tgt_bits - 1, shared - 1, -1)]
     row_masks = [n_tgt << bit for bit in range(1, src_bits)]
 
-    targets_here, bias = load(targets, potentials, log_mass)
+    targets_here, bias, parts = load(targets, potentials, log_mass)
     held = [sources]
     for mask in masks:
         whole = held[0] if len(held) == 1 else jnp.concatenate(held, axis=1)
         held.append(flip(whole, mask))
     if len(col_masks) == 1 and len(row_masks) == 1:
+        count, deep = targets.shape[1], bias.shape[1]
         beside = flip(targets, col_masks[0])
-        beside, bias = lax.optimization_barrier((beside, bias))
         below = flip(targets, row_masks[0])
-        corner = flip(beside, row_masks[0])
+        corner = flip(jnp.concatenate([below, parts], axis=1), col_masks[0])
+        parts = corner[:, count:].astype(jnp.float32)
+        there = (parts[:, :deep] + parts[:, deep : 2 * deep]) + parts[:, 2 * deep :]
+        bias = jnp.concatenate([bias, there], axis=0)
         upper = jnp.concatenate([targets_here, beside], axis=1)
-        lower = jnp.concatenate([below, corner], axis=1)
+        lower = jnp.concatenate([below, corner[:, :count]], axis=1)
         own = jnp.concatenate([upper, lower], axis=0)
     else:
         own = gather(gather(targets_here, col_masks, 1), row_masks, 0)
-    bias = gather(bias, col_masks, 0).reshape(1, -1)
+        bias = gather(bias, col_masks, 0)
+    bias = bias.reshape(1, -1)
     far = flip(own, n_tgt)
     placed = placed_sources(src_bits, held)
 

time: 56.5 us -> 56.8 us (level); the launches traced: 55.6 us -> 56.6 us
  waiting for transfers between devices: 3.74 us -> 6.1 us
  local copies, waits for them, and re-layouts: 2.24 us -> 0.01 us
  Pallas kernels: 37.3 us -> 38.1 us
    ppermute x9 -> x8, waiting for transfers between devices: 3.74 us -> 6.1 us  [flip(): return lax.ppermute(value, AXES, [(i, i ^ mask) for i in range(n)])]
    unnamed x8 -> x2, local copies, waits for them, and re-layouts: 2.24 us -> 0.01 us
    pallas_call x1, Pallas kernels: 0.11 us -> 0.9 us  [load(): pl.pallas_call(load_kernel, out_shape=(pltpu.VMEM((rows, count), targets....]
    ppermute x9 -> x8, starting transfers between devices: 11.5 us -> 11.5 us  [flip(): return lax.ppermute(value, AXES, [(i, i ^ mask) for i in range(n)])]
  transfers between devices with their start and end apart: 9 -> 8, of which waited for: 2 -> 4; matrix products, arithmetic and copies ran while one was open for 0% -> 0% of each run, Pallas kernels for 34% -> 35%
where the time goes in v4:
time: 56.8 us; the launch traced here: 56.6 us
  Pallas kernels  38.1 us (67%)
  starting transfers between devices  11.5 us (20%)
  waiting for transfers between devices  6.1 us (11%)
  other arithmetic  0.73 us (1%)
    pallas_call x2, Pallas kernels, next_logs(): pl.pallas_call(functools.partial(next_kernel, width), out_shape=pltpu.VME...  18.6 us
    pallas_call x1, Pallas kernels, first_logs(): pl.pallas_call(first_kernel, out_shape=(pltpu.VMEM((1, rows), jnp.float32...  18.5 us
    ppermute x8, starting transfers between devices, flip(): return lax.ppermute(value, AXES, [(i, i ^ mask) for i in range(n)])  11.5 us
    ppermute x8, waiting for transfers between devices, flip(): return lax.ppermute(value, AXES, [(i, i ^ mask) for i in range(n)])  6.1 us
  transfers between devices with their start and end apart: 8, of which 4 were waited for; matrix products, arithmetic and copies ran while one was open for 0% of the time, Pallas kernels for 35%

profile of v4, /device:TPU:0, one launch (start us, length us, event | category | flops | bytes accessed | tf_op | source)
XLA Modules:
  0.0 56.6 jit_solution(16148900620667153931)
XLA Ops:
  0.0 0.0 copy-start
  0.0 3.0 %collective-permute-start.3 = (bf16[16,2048]{1,0:T(8,128)(2,1)}, bf16[16,2048]{1,0:T(8,128)(2,1)S(1)}, u32[]{:S(2)}, u32[]{:S(2)}) collective-permute-start(bf16[16,2048]{1,0:T(8,128)(2,1)} %targets.1), channel_id=1, source_target_pairs={{0,16},{1,17},{2,18},{3,19},{4,20},{5,21},{6,22},{7,23},{8,24},{9,... | collective-permute-start | bytes 196616 | tf_op jit(solution)/shard_map/ppermute | solution.py:23
  3.0 2.6 %collective-permute-start.2 = (bf16[16,2048]{1,0:T(8,128)(2,1)}, bf16[16,2048]{1,0:T(8,128)(2,1)S(1)}, u32[]{:S(2)}, u32[]{:S(2)}) collective-permute-start(bf16[16,2048]{1,0:T(8,128)(2,1)} %targets.1), channel_id=1, source_target_pairs={{0,4},{1,5},{2,6},{3,7},{4,0},{5,1},{6,2},{7,3},{8,12},{9,13},{10,... | collective-permute-start | bytes 196616 | tf_op jit(solution)/shard_map/ppermute | solution.py:23
  5.6 0.5 collective-permute-start
  6.0 0.9 %shard_map.47 = (bf16[16,2048]{1,0:T(8,128)(2,1)S(1)}, f32[16,128]{1,0:T(8,128)S(1)}, bf16[16,384]{1,0:T(8,128)(2,1)S(1)}) custom-call(bf16[16,2048]{1,0:T(8,128)(2,1)} %targets.1, f32[16,128]{1,0:T(8,128)} %bitcast.5, f32[16,128]{1,0:T(8,128)} %bitcast.6), custom_call_target="tpu_custom_call" | custom-call | tf_op jit(solution)/shard_map/pallas_call | solution.py:54
  6.9 0.0 copy-done
  7.0 0.0 collective-permute-done.3
  7.0 1.5 %collective-permute-start.4 = (bf16[16,2432]{1,0:T(8,128)(2,1)S(1)}, bf16[16,2432]{1,0:T(8,128)(2,1)S(1)}, u32[]{:S(2)}, u32[]{:S(2)}) collective-permute-start(bf16[16,2432]{1,0:T(8,128)(2,1)S(1)} %pad_maximum_fusion.1), channel_id=1, source_target_pairs={{0,4},{1,5},{2,6},{3,7},{4,0},{5,1},{6,2},{7,3},{8,12},{9,13},{10,... | collective-permute-start | bytes 233480 | tf_op jit(solution)/shard_map/ppermute | solution.py:23
  8.5 1.5 %collective-permute-done.refs_1_ = bf16[64,512]{1,0:T(8,128)(2,1)S(1)} collective-permute-done((bf16[64,512]{1,0:T(8,128)(2,1)}, bf16[64,512]{1,0:T(8,128)(2,1)S(1)}, u32[]{:S(2)}, u32[]{:S(2)}) %collective-permute-start) | collective-permute-done | bytes 65568 | tf_op jit(solution)/shard_map/ppermute | solution.py:23
  10.0 1.3 %collective-permute-start.1 = (bf16[64,1024]{1,0:T(8,128)(2,1)S(1)}, bf16[64,1024]{1,0:T(8,128)(2,1)S(1)}, u32[]{:S(2)}, u32[]{:S(2)}) collective-permute-start(bf16[64,1024]{1,0:T(8,128)(2,1)S(1)} %pad_maximum_fusion), channel_id=1, source_target_pairs={{0,9},{1,8},{2,11},{3,10},{4,13},{5,12},{6,15},{7,14},{8,1},{9,0},... | collective-permute-start | bytes 393224 | tf_op jit(solution)/shard_map/ppermute | solution.py:23
  11.3 3.3 %collective-permute-done.4 = bf16[16,2432]{1,0:T(8,128)(2,1)S(1)} collective-permute-done((bf16[16,2432]{1,0:T(8,128)(2,1)S(1)}, bf16[16,2432]{1,0:T(8,128)(2,1)S(1)}, u32[]{:S(2)}, u32[]{:S(2)}) %collective-permute-start.4) | collective-permute-done | bytes 77856 | tf_op jit(solution)/shard_map/ppermute | solution.py:23
  14.6 0.0 collective-permute-done.2
  14.6 0.2 collective-permute-start.5
  14.8 0.8 %collective-permute-done.1.refs_2_ = bf16[64,1024]{1,0:T(8,128)(2,1)S(1)} collective-permute-done((bf16[64,1024]{1,0:T(8,128)(2,1)S(1)}, bf16[64,1024]{1,0:T(8,128)(2,1)S(1)}, u32[]{:S(2)}, u32[]{:S(2)}) %collective-permute-start.1) | collective-permute-done | bytes 131104 | tf_op jit(solution)/shard_map/ppermute | solution.py:23
  15.6 0.1 shard_map.46
  15.7 0.5 collective-permute-done.5.tgt_far
  16.2 18.5 %shard_map.48 = (f32[1,1024]{1,0:T(1,128)S(1)}, bf16[4096,128]{1,0:T(8,128)(2,1)S(1)}) custom-call(bf16[128,1024]{1,0:T(8,128)(2,1)S(1)} %get-tuple-element.14.placed, bf16[32,4096]{1,0:T(8,128)(2,1)S(1)} %maximum_maximum_fusion.tgt_own, bf16[32,4096]{1,0:T(8,128)(2,1)S(1)} %collective-permute-done.5.tgt_far, f32[1,4096]{1,0:T(1,128)S(1)} %bitcast.4), custom_call_target="tpu_custom_call" | custom-call | flops 1073741824 | bytes 1048576 | tf_op jit(solution)/shard_map/pallas_call | solution.py:183
  34.8 0.1 collective-permute-start.6
  34.9 9.3 %shard_map.50 = f32[1,512]{1,0:T(1,128)S(1)} custom-call(bf16[128,512]{1,0:T(8,128)(2,1)S(1)} %get-tuple-element.20.placed, bf16[4096,128]{1,0:T(8,128)(2,1)S(1)} %get-tuple-element.18.lhs), custom_call_target="tpu_custom_call" | custom-call | flops 536870912 | bytes 1048576 | tf_op jit(solution)/shard_map/pallas_call | solution.py:196
  44.2 0.0 collective-permute-done.6
  44.2 2.5 %collective-permute-start.7 = (f32[1,512]{1,0:T(1,128)S(1)}, f32[1,512]{1,0:T(1,128)S(1)}, u32[]{:S(2)}, u32[]{:S(2)}) collective-permute-start(f32[1,512]{1,0:T(1,128)S(1)} %multiply_add_fusion), channel_id=1, source_target_pairs={{0,10},{1,11},{2,8},{3,9},{4,14},{5,15},{6,12},{7,13},{8,2},{9,3},... | collective-permute-start | bytes 6152 | tf_op jit(solution)/shard_map/ppermute | solution.py:23
  46.7 9.3 %shard_map.49 = f32[1,512]{1,0:T(1,128)S(1)} custom-call(bf16[128,512]{1,0:T(8,128)(2,1)S(1)} %get-tuple-element.13.placed, bf16[4096,128]{1,0:T(8,128)(2,1)S(1)} %get-tuple-element.18.lhs), custom_call_target="tpu_custom_call" | custom-call | flops 536870912 | bytes 1048576 | tf_op jit(solution)/shard_map/pallas_call | solution.py:196
  56.0 0.0 collective-permute-done.7
  56.0 0.6 %multiply_subtract_fusion = f32[512]{0:T(512)} fusion(f32[512]{0:T(512)S(1)} %bitcast.7, f32[512]{0:T(512)S(1)} %multiply_reduce_fusion), kind=kLoop, calls=%fused_computation.10 | loop fusion | flops 1024 | bytes 6144 | tf_op jit(solution)/shard_map/sub | solution.py:260
  (10 shorter events, 0.2 us)
Async XLA Ops:
  0.0 6.9 %copy-start = (bf16[64,512]{1,0:T(8,128)(2,1)S(1)}, bf16[64,512]{1,0:T(8,128)(2,1)}, u32[]{:S(2)}) copy-start(bf16[64,512]{1,0:T(8,128)(2,1)} %refs_0_.1) | copy-start | bytes 196612
  0.0 7.0 %collective-permute-start.3 = (bf16[16,2048]{1,0:T(8,128)(2,1)}, bf16[16,2048]{1,0:T(8,128)(2,1)S(1)}, u32[]{:S(2)}, u32[]{:S(2)}) collective-permute-start(bf16[16,2048]{1,0:T(8,128)(2,1)} %targets.1), channel_id=1, source_target_pairs={{0,16},{1,17},{2,18},{3,19},{4,20},{5,21},{6,22},{7,23},{8,24},{9,... | collective-permute-start | bytes 196616 | tf_op jit(solution)/shard_map/ppermute | solution.py:23
  3.0 11.6 %collective-permute-start.2 = (bf16[16,2048]{1,0:T(8,128)(2,1)}, bf16[16,2048]{1,0:T(8,128)(2,1)S(1)}, u32[]{:S(2)}, u32[]{:S(2)}) collective-permute-start(bf16[16,2048]{1,0:T(8,128)(2,1)} %targets.1), channel_id=1, source_target_pairs={{0,4},{1,5},{2,6},{3,7},{4,0},{5,1},{6,2},{7,3},{8,12},{9,13},{10,... | collective-permute-start | bytes 196616 | tf_op jit(solution)/shard_map/ppermute | solution.py:23
  5.6 4.5 %collective-permute-start = (bf16[64,512]{1,0:T(8,128)(2,1)}, bf16[64,512]{1,0:T(8,128)(2,1)S(1)}, u32[]{:S(2)}, u32[]{:S(2)}) collective-permute-start(bf16[64,512]{1,0:T(8,128)(2,1)} %refs_0_.1), channel_id=1, source_target_pairs={{0,10},{1,11},{2,8},{3,9},{4,14},{5,15},{6,12},{7,13},{8,2},{9,3},... | collective-permute-start | bytes 196616 | tf_op jit(solution)/shard_map/ppermute | solution.py:23
  7.0 7.6 %collective-permute-start.4 = (bf16[16,2432]{1,0:T(8,128)(2,1)S(1)}, bf16[16,2432]{1,0:T(8,128)(2,1)S(1)}, u32[]{:S(2)}, u32[]{:S(2)}) collective-permute-start(bf16[16,2432]{1,0:T(8,128)(2,1)S(1)} %pad_maximum_fusion.1), channel_id=1, source_target_pairs={{0,4},{1,5},{2,6},{3,7},{4,0},{5,1},{6,2},{7,3},{8,12},{9,13},{10,... | collective-permute-start | bytes 233480 | tf_op jit(solution)/shard_map/ppermute | solution.py:23
  10.0 5.6 %collective-permute-start.1 = (bf16[64,1024]{1,0:T(8,128)(2,1)S(1)}, bf16[64,1024]{1,0:T(8,128)(2,1)S(1)}, u32[]{:S(2)}, u32[]{:S(2)}) collective-permute-start(bf16[64,1024]{1,0:T(8,128)(2,1)S(1)} %pad_maximum_fusion), channel_id=1, source_target_pairs={{0,9},{1,8},{2,11},{3,10},{4,13},{5,12},{6,15},{7,14},{8,1},{9,0},... | collective-permute-start | bytes 393224 | tf_op jit(solution)/shard_map/ppermute | solution.py:23
  14.6 1.6 %collective-permute-start.5 = (bf16[32,4096]{1,0:T(8,128)(2,1)S(1)}, bf16[32,4096]{1,0:T(8,128)(2,1)S(1)}, u32[]{:S(2)}, u32[]{:S(2)}) collective-permute-start(bf16[32,4096]{1,0:T(8,128)(2,1)S(1)} %maximum_maximum_fusion.tgt_own), channel_id=1, source_target_pairs={{0,8},{1,9},{2,10},{3,11},{4,12},{5,13},{6,14},{7,15},{8,0},{9,1},... | collective-permute-start | bytes 786440 | tf_op jit(solution)/shard_map/ppermute | solution.py:23
  34.8 9.4 %collective-permute-start.6 = (f32[1,1024]{1,0:T(1,128)S(1)}, f32[1,1024]{1,0:T(1,128)S(1)}, u32[]{:S(2)}, u32[]{:S(2)}) collective-permute-start(f32[1,1024]{1,0:T(1,128)S(1)} %get-tuple-element.19), channel_id=1, source_target_pairs={{0,9},{1,8},{2,11},{3,10},{4,13},{5,12},{6,15},{7,14},{8,1},{9,0},... | collective-permute-start | bytes 12296 | tf_op jit(solution)/shard_map/ppermute | solution.py:23
  44.2 11.8 %collective-permute-start.7 = (f32[1,512]{1,0:T(1,128)S(1)}, f32[1,512]{1,0:T(1,128)S(1)}, u32[]{:S(2)}, u32[]{:S(2)}) collective-permute-start(f32[1,512]{1,0:T(1,128)S(1)} %multiply_add_fusion), channel_id=1, source_target_pairs={{0,10},{1,11},{2,8},{3,9},{4,14},{5,15},{6,12},{7,13},{8,2},{9,3},... | collective-permute-start | bytes 6152 | tf_op jit(solution)/shard_map/ppermute | solution.py:23

commit v5 on v3

--- a/solution.py
+++ b/solution.py
@@ -31,11 +31,12 @@
     return first, second, third
 
 
-def load_kernel(targets, potentials, log_mass, targets_here, bias, scratch, sems):
+def load_kernel(sources, targets, potentials, log_mass, sources_here, targets_here, bias, scratch, sems):
     copies = [
         pltpu.make_async_copy(potentials, scratch.at[0], sems.at[0]),
         pltpu.make_async_copy(log_mass, scratch.at[1], sems.at[1]),
-        pltpu.make_async_copy(targets, targets_here, sems.at[2]),
+        pltpu.make_async_copy(sources, sources_here, sems.at[2]),
+        pltpu.make_async_copy(targets, targets_here, sems.at[3]),
     ]
     for copy in copies:
         copy.start()
@@ -43,27 +44,32 @@
     copies[1].wait()
     bias[...] = scratch[0] + EPSILON * scratch[1]
     copies[2].wait()
-
-
-def load(targets, potentials, log_mass):
+    copies[3].wait()
+
+
+def load(sources, targets, potentials, log_mass):
     rows = potentials.shape[0] // LANES
     return pl.pallas_call(
         load_kernel,
-        out_shape=(pltpu.VMEM(targets.shape, targets.dtype), pltpu.VMEM((rows, LANES), jnp.float32)),
-        in_specs=[ANY] * 3,
-        out_specs=(VMEM,) * 2,
-        scratch_shapes=[pltpu.VMEM((2, rows, LANES), jnp.float32), pltpu.SemaphoreType.DMA((3,))],
-        compiler_params=pltpu.CompilerParams(vmem_limit_bytes=8 << 20),
-    )(targets, potentials.reshape(rows, LANES), log_mass.reshape(rows, LANES))
-
-
-def place_targets(tgt_own, tgt_far, bias_ref, lhs):
+        out_shape=(
+            pltpu.VMEM(sources.shape, sources.dtype),
+            pltpu.VMEM(targets.shape, targets.dtype),
+            pltpu.VMEM((rows, LANES), jnp.float32),
+        ),
+        in_specs=[ANY] * 4,
+        out_specs=(VMEM,) * 3,
+        scratch_shapes=[pltpu.VMEM((2, rows, LANES), jnp.float32), pltpu.SemaphoreType.DMA((4,))],
+    )(sources, targets, potentials.reshape(rows, LANES), log_mass.reshape(rows, LANES))
+
+
+def place_targets(turn, tgt_own, tgt_far, bias_ref, lhs):
     count = tgt_own.shape[1]
     width = tgt_own.shape[0] + tgt_far.shape[0]
     step = min(1024, count)
     for start in range(0, count, step):
         cols = slice(start, start + step)
-        points = jnp.concatenate([tgt_own[:, cols], tgt_far[:, cols]], axis=0)
+        halves = [tgt_own[:, cols], tgt_far[:, cols]]
+        points = jnp.concatenate(halves if start < turn else halves[::-1], axis=0)
         wide = points.astype(jnp.float32)
         half = 0.5 * jnp.sum(wide * wide, axis=0, keepdims=True)
         first, second, third = split3(bias_ref[:, cols] - half)
@@ -74,30 +80,31 @@
         lhs[cols, :] = jnp.concatenate([points, extra.astype(jnp.bfloat16)], axis=0).T
 
 
-def place_sources(src_bits, src_ref, rhs):
+def place_sources(order, src_ref, rhs):
     width, rows = src_ref.shape
     points = src_ref[...].astype(jnp.float32)
     me = lax.axis_index("src")
-    part = width >> src_bits
-    blocks = [points[k * part : (k + 1) * part] for k in range(1 << src_bits)]
-    for bit in range(src_bits):
+    n_src = len(order)
+    part = width // n_src
+    blocks = [points[k * part : (k + 1) * part] for k in range(n_src)]
+    for bit in range(n_src.bit_length() - 1):
         turned = ((me >> bit) & 1) == 1
-        blocks = [jnp.where(turned, blocks[k ^ (1 << bit)], blocks[k]) for k in range(1 << src_bits)]
-    points = jnp.concatenate(blocks[0::2] + blocks[1::2], axis=0)
+        blocks = [jnp.where(turned, blocks[k ^ (1 << bit)], blocks[k]) for k in range(n_src)]
+    points = jnp.concatenate([blocks[k] for k in order], axis=0)
     rhs[:width, :] = points.astype(jnp.bfloat16)
     place = lax.broadcasted_iota(jnp.int32, (LANES - width, rows), 0)
     rhs[width:, :] = jnp.where(place < 3, 1.0, 0.0).astype(jnp.bfloat16)
 
 
-def sources_kernel(src_bits, *refs):
+def sources_kernel(order, *refs):
     count = len(refs) // 2
     for src_ref, rhs in zip(refs[:count], refs[count:], strict=True):
-        place_sources(src_bits, src_ref, rhs)
-
-
-def placed_sources(src_bits, held):
-    return pl.pallas_call(
-        functools.partial(sources_kernel, src_bits),
+        place_sources(order, src_ref, rhs)
+
+
+def placed_sources(order, held):
+    return pl.pallas_call(
+        functools.partial(sources_kernel, order),
         out_shape=tuple(pltpu.VMEM((LANES, piece.shape[1]), jnp.bfloat16) for piece in held),
         in_specs=[VMEM] * len(held),
         out_specs=(VMEM,) * len(held),
@@ -156,8 +163,8 @@
             out_ref[:, cols] = row_top + jnp.log2(row_sum)
 
 
-def first_kernel(placed, tgt_own, tgt_far, bias_ref, out_ref, lhs, rhs):
-    place_targets(tgt_own, tgt_far, bias_ref, lhs)
+def first_kernel(turn, placed, tgt_own, tgt_far, bias_ref, out_ref, lhs, rhs):
+    place_targets(turn, tgt_own, tgt_far, bias_ref, lhs)
     rhs[...] = placed[...]
     log_sums(tgt_own.shape[0] + tgt_far.shape[0], lhs, rhs, out_ref)
 
@@ -171,10 +178,10 @@
     return pl.CostEstimate(flops=2 * rows * count * LANES, bytes_accessed=2 * count * LANES, transcendentals=rows * count)
 
 
-def first_logs(placed, tgt_own, tgt_far, bias):
+def first_logs(turn, placed, tgt_own, tgt_far, bias):
     count, rows = tgt_own.shape[1], placed.shape[1]
     return pl.pallas_call(
-        first_kernel,
+        functools.partial(first_kernel, turn),
         out_shape=(pltpu.VMEM((1, rows), jnp.float32), pltpu.VMEM((count, LANES), jnp.bfloat16)),
         in_specs=[VMEM] * 4,
         out_specs=(VMEM, VMEM),
@@ -212,32 +219,40 @@
     n_src, n_tgt = lax.axis_size("src"), lax.axis_size("tgt")
     src_bits, tgt_bits = n_src.bit_length() - 1, n_tgt.bit_length() - 1
     shared = min(2, tgt_bits)
-    masks = [(1 << bit) | n_tgt for bit in range(shared)]
+    masks = [(1 << bit) | n_tgt for bit in range(shared - 1, -1, -1)]
     col_masks = [1 << bit for bit in range(tgt_bits - 1, shared - 1, -1)]
     row_masks = [n_tgt << bit for bit in range(1, src_bits)]
 
-    targets_here, bias = load(targets, potentials, log_mass)
+    sources_here, targets_here, bias = load(sources, targets, potentials, log_mass)
     held = [sources]
     for mask in masks:
-        whole = held[0] if len(held) == 1 else jnp.concatenate(held, axis=1)
+        whole = sources if len(held) == 1 else jnp.concatenate([sources_here, *held[1:]], axis=1)
         held.append(flip(whole, mask))
+    held[0] = sources_here
     if len(col_masks) == 1 and len(row_masks) == 1:
-        beside = flip(targets, col_masks[0])
-        beside, bias = lax.optimization_barrier((beside, bias))
-        below = flip(targets, row_masks[0])
-        corner = flip(beside, row_masks[0])
+        col_mask, row_mask = col_masks[0] | n_tgt, row_masks[0] | n_tgt
+        beside = flip(targets, col_mask)
+        below = flip(targets, row_mask)
+        corner = flip(beside, row_mask)
+        bias, _ = lax.optimization_barrier((bias, whole))
+        there = flip(bias, col_mask)
+        there, held[-1] = lax.optimization_barrier((there, held[-1]))
+        bias = jnp.concatenate([bias, there], axis=0)
         upper = jnp.concatenate([targets_here, beside], axis=1)
         lower = jnp.concatenate([below, corner], axis=1)
         own = jnp.concatenate([upper, lower], axis=0)
+        order, turn = (0, 3, 1, 2), targets.shape[1]
     else:
         own = gather(gather(targets_here, col_masks, 1), row_masks, 0)
-    bias = gather(bias, col_masks, 0).reshape(1, -1)
+        bias = gather(bias, col_masks, 0)
+        order, turn = (*range(0, n_src, 2), *range(1, n_src, 2)), own.shape[1]
+    bias = bias.reshape(1, -1)
     far = flip(own, n_tgt)
-    placed = placed_sources(src_bits, held)
+    placed = placed_sources(order, held)
 
     owned = sources.shape[1]
     arrived = []
-    logs, lhs = first_logs(placed[-1], own, far, bias)
+    logs, lhs = first_logs(turn, placed[-1], own, far, bias)
     for k in range(shared, 0, -1):
         for other in arrived:
             logs = join(logs, other[:, owned << (k - 1) : owned << k])

time: 56.5 us -> 56.4 us (level); the launches traced: 55.6 us -> 56.2 us
  starting transfers between devices: 11.5 us -> 13.8 us
  local copies, waits for them, and re-layouts: 2.24 us -> 0.01 us
  waiting for transfers between devices: 3.74 us -> 2.63 us
  Pallas kernels: 37.3 us -> 38.2 us
  other arithmetic: 0.71 us -> 1.56 us
    ppermute x9, starting transfers between devices: 11.5 us -> 13.8 us  [flip(): return lax.ppermute(value, AXES, [(i, i ^ mask) for i in range(n)])]
    unnamed x8 -> x1, local copies, waits for them, and re-layouts: 2.24 us -> 0.01 us
    ppermute x9, waiting for transfers between devices: 3.74 us -> 2.63 us  [flip(): return lax.ppermute(value, AXES, [(i, i ^ mask) for i in range(n)])]
    reduce_sum x1, other arithmetic: 0.03 us -> 0.9 us  [on_device(): return 0.5 * jnp.sum(wide * wide, axis=0) - 1.0 / RATE * logs[0]]
    pallas_call x3, Pallas kernels: 18.8 us -> 19.6 us  [the longest x1 18.5 us: first_logs(): pl.pallas_call(functools.partial(first_kernel, turn), out_shape=(pltpu.VM...]
  transfers between devices with their start and end apart: 9 -> 9, of which waited for: 2 -> 3; matrix products, arithmetic and copies ran while one was open for 0% -> 2% of each run, Pallas kernels for 34% -> 35%
where the time goes in v5:
time: 56.4 us; the launch traced here: 56.2 us
  Pallas kernels  38.2 us (68%)
  starting transfers between devices  13.8 us (24%)
  waiting for transfers between devices  2.63 us (5%)
  other arithmetic  1.56 us (3%)
    pallas_call x2, Pallas kernels, next_logs(): pl.pallas_call(functools.partial(next_kernel, width), out_shape=pltpu.VME...  18.6 us
    pallas_call x1, Pallas kernels, first_logs(): pl.pallas_call(functools.partial(first_kernel, turn), out_shape=(pltpu.VM...  18.5 us
    ppermute x9, starting transfers between devices, flip(): return lax.ppermute(value, AXES, [(i, i ^ mask) for i in range(n)])  13.8 us
    ppermute x9, waiting for transfers between devices, flip(): return lax.ppermute(value, AXES, [(i, i ^ mask) for i in range(n)])  2.63 us
  transfers between devices with their start and end apart: 9, of which 3 were waited for; matrix products, arithmetic and copies ran while one was open for 2% of the time, Pallas kernels for 35%

profile of v5, /device:TPU:0, one launch (start us, length us, event | category | flops | bytes accessed | tf_op | source)
XLA Modules:
  0.0 56.2 jit_solution(8387857558581513384)
XLA Ops:
  0.0 3.5 %collective-permute-start.3 = (bf16[16,2048]{1,0:T(8,128)(2,1)}, bf16[16,2048]{1,0:T(8,128)(2,1)S(1)}, u32[]{:S(2)}, u32[]{:S(2)}) collective-permute-start(bf16[16,2048]{1,0:T(8,128)(2,1)} %targets.1), channel_id=1, source_target_pairs={{0,12},{1,13},{2,14},{3,15},{4,8},{5,9},{6,10},{7,11},{8,4},{9,5},... | collective-permute-start | bytes 196616 | tf_op jit(solution)/shard_map/ppermute | solution.py:23
  3.5 1.8 %collective-permute-start.4 = (bf16[16,2048]{1,0:T(8,128)(2,1)}, bf16[16,2048]{1,0:T(8,128)(2,1)S(1)}, u32[]{:S(2)}, u32[]{:S(2)}) collective-permute-start(bf16[16,2048]{1,0:T(8,128)(2,1)} %targets.1), channel_id=1, source_target_pairs={{0,24},{1,25},{2,26},{3,27},{4,28},{5,29},{6,30},{7,31},{8,16},{9,... | collective-permute-start | bytes 196616 | tf_op jit(solution)/shard_map/ppermute | solution.py:23
  5.3 1.0 %collective-permute-start = (bf16[64,512]{1,0:T(8,128)(2,1)}, bf16[64,512]{1,0:T(8,128)(2,1)S(1)}, u32[]{:S(2)}, u32[]{:S(2)}) collective-permute-start(bf16[64,512]{1,0:T(8,128)(2,1)} %sources.1), channel_id=1, source_target_pairs={{0,10},{1,11},{2,8},{3,9},{4,14},{5,15},{6,12},{7,13},{8,2},{9,3},... | collective-permute-start | bytes 196616 | tf_op jit(solution)/shard_map/ppermute | solution.py:23
  6.3 0.9 %multiply_reduce_fusion = f32[512]{0:T(512)S(1)} fusion(bf16[64,512]{1,0:T(8,128)(2,1)} %sources.1), kind=kLoop, calls=%fused_computation.1 | loop fusion | flops 97792 | bytes 67584 | tf_op jit(solution)/shard_map/reduce_sum | solution.py:264
  7.2 0.9 %shard_map.46 = (bf16[64,512]{1,0:T(8,128)(2,1)S(1)}, bf16[16,2048]{1,0:T(8,128)(2,1)S(1)}, f32[16,128]{1,0:T(8,128)S(1)}) custom-call(bf16[64,512]{1,0:T(8,128)(2,1)} %sources.1, bf16[16,2048]{1,0:T(8,128)(2,1)} %targets.1, f32[16,128]{1,0:T(8,128)} %bitcast.5, f32[16,128]{1,0:T(8,128)} %bitcast.6), custom_call_target="tpu_custom_call" | custom-call | tf_op jit(solution)/shard_map/pallas_call | solution.py:52
  8.2 0.0 collective-permute-done.3
  8.2 1.2 %collective-permute-start.5 = (bf16[16,2048]{1,0:T(8,128)(2,1)S(1)}, bf16[16,2048]{1,0:T(8,128)(2,1)S(1)}, u32[]{:S(2)}, u32[]{:S(2)}) collective-permute-start(bf16[16,2048]{1,0:T(8,128)(2,1)S(1)} %collective-permute-done.3), channel_id=1, source_target_pairs={{0,24},{1,25},{2,26},{3,27},{4,28},{5,29},{6,30},{7,31},{8,16},{9,... | collective-permute-start | bytes 196616 | tf_op jit(solution)/shard_map/ppermute | solution.py:23
  9.4 0.3 collective-permute-done.refs_1_
  9.8 1.2 %collective-permute-start.2 = (bf16[64,1024]{1,0:T(8,128)(2,1)S(1)}, bf16[64,1024]{1,0:T(8,128)(2,1)S(1)}, u32[]{:S(2)}, u32[]{:S(2)}) collective-permute-start(bf16[64,1024]{1,0:T(8,128)(2,1)S(1)} %constant_dynamic-update-slice_fusion), channel_id=1, source_target_pairs={{0,9},{1,8},{2,11},{3,10},{4,13},{5,12},{6,15},{7,14},{8,1},{9,0},... | collective-permute-start | bytes 393224 | tf_op jit(solution)/shard_map/ppermute | solution.py:23
  11.0 1.1 %collective-permute-start.1 = (f32[16,128]{1,0:T(8,128)S(1)}, f32[16,128]{1,0:T(8,128)S(1)}, u32[]{:S(2)}, u32[]{:S(2)}) collective-permute-start(f32[16,128]{1,0:T(8,128)S(1)} %get-tuple-element.18), channel_id=1, source_target_pairs={{0,12},{1,13},{2,14},{3,15},{4,8},{5,9},{6,10},{7,11},{8,4},{9,5},... | collective-permute-start | bytes 24584 | tf_op jit(solution)/shard_map/ppermute | solution.py:23
  12.1 0.0 collective-permute-done.4
  12.1 0.0 collective-permute-done.5
  12.1 0.9 %collective-permute-start.6 = (bf16[32,4096]{1,0:T(8,128)(2,1)S(1)}, bf16[32,4096]{1,0:T(8,128)(2,1)S(1)}, u32[]{:S(2)}, u32[]{:S(2)}) collective-permute-start(bf16[32,4096]{1,0:T(8,128)(2,1)S(1)} %maximum_maximum_fusion.tgt_own), channel_id=1, source_target_pairs={{0,8},{1,9},{2,10},{3,11},{4,12},{5,13},{6,14},{7,15},{8,0},{9,1},... | collective-permute-start | bytes 786440 | tf_op jit(solution)/shard_map/ppermute | solution.py:23
  13.0 2.0 %collective-permute-done.1 = f32[16,128]{1,0:T(8,128)S(1)} collective-permute-done((f32[16,128]{1,0:T(8,128)S(1)}, f32[16,128]{1,0:T(8,128)S(1)}, u32[]{:S(2)}, u32[]{:S(2)}) %collective-permute-start.1) | collective-permute-done | bytes 8224 | tf_op jit(solution)/shard_map/ppermute | solution.py:23
  14.9 0.3 collective-permute-done.2.refs_2_
  15.3 0.1 shard_map.47
  15.4 0.0 collective-permute-done.6.tgt_far
  15.4 18.5 %shard_map.48 = (f32[1,1024]{1,0:T(1,128)S(1)}, bf16[4096,128]{1,0:T(8,128)(2,1)S(1)}) custom-call(bf16[128,1024]{1,0:T(8,128)(2,1)S(1)} %get-tuple-element.21.placed, bf16[32,4096]{1,0:T(8,128)(2,1)S(1)} %maximum_maximum_fusion.tgt_own, bf16[32,4096]{1,0:T(8,128)(2,1)S(1)} %collective-permute-done.6.tgt_far, f32[1,4096]{1,0:T(1,128)S(1)} %bitcast.4), custom_call_target="tpu_custom_call" | custom-call | flops 1073741824 | bytes 1048576 | tf_op jit(solution)/shard_map/pallas_call | solution.py:183
  33.9 0.1 collective-permute-start.7
  34.0 9.3 %shard_map.50 = f32[1,512]{1,0:T(1,128)S(1)} custom-call(bf16[128,512]{1,0:T(8,128)(2,1)S(1)} %get-tuple-element.26.placed, bf16[4096,128]{1,0:T(8,128)(2,1)S(1)} %get-tuple-element.24.lhs), custom_call_target="tpu_custom_call" | custom-call | flops 536870912 | bytes 1048576 | tf_op jit(solution)/shard_map/pallas_call | solution.py:196
  43.3 3.0 %collective-permute-start.8 = (f32[1,512]{1,0:T(1,128)S(1)}, f32[1,512]{1,0:T(1,128)S(1)}, u32[]{:S(2)}, u32[]{:S(2)}) collective-permute-start(f32[1,512]{1,0:T(1,128)S(1)} %multiply_add_fusion), channel_id=1, source_target_pairs={{0,10},{1,11},{2,8},{3,9},{4,14},{5,15},{6,12},{7,13},{8,2},{9,3},... | collective-permute-start | bytes 6152 | tf_op jit(solution)/shard_map/ppermute | solution.py:23
  46.3 9.3 %shard_map.49 = f32[1,512]{1,0:T(1,128)S(1)} custom-call(bf16[128,512]{1,0:T(8,128)(2,1)S(1)} %get-tuple-element.20.placed, bf16[4096,128]{1,0:T(8,128)(2,1)S(1)} %get-tuple-element.24.lhs), custom_call_target="tpu_custom_call" | custom-call | flops 536870912 | bytes 1048576 | tf_op jit(solution)/shard_map/pallas_call | solution.py:196
  55.6 0.0 collective-permute-done.8
  55.6 0.6 %multiply_subtract_fusion = f32[512]{0:T(512)} fusion(f32[512]{0:T(512)S(1)} %bitcast.7, f32[512]{0:T(512)S(1)} %multiply_reduce_fusion), kind=kLoop, calls=%fused_computation.7 | loop fusion | flops 1024 | bytes 6144 | tf_op jit(solution)/shard_map/sub | solution.py:264
  (7 shorter events, 0.1 us)
Async XLA Ops:
  0.0 8.2 %collective-permute-start.3 = (bf16[16,2048]{1,0:T(8,128)(2,1)}, bf16[16,2048]{1,0:T(8,128)(2,1)S(1)}, u32[]{:S(2)}, u32[]{:S(2)}) collective-permute-start(bf16[16,2048]{1,0:T(8,128)(2,1)} %targets.1), channel_id=1, source_target_pairs={{0,12},{1,13},{2,14},{3,15},{4,8},{5,9},{6,10},{7,11},{8,4},{9,5},... | collective-permute-start | bytes 196616 | tf_op jit(solution)/shard_map/ppermute | solution.py:23
  3.5 8.6 %collective-permute-start.4 = (bf16[16,2048]{1,0:T(8,128)(2,1)}, bf16[16,2048]{1,0:T(8,128)(2,1)S(1)}, u32[]{:S(2)}, u32[]{:S(2)}) collective-permute-start(bf16[16,2048]{1,0:T(8,128)(2,1)} %targets.1), channel_id=1, source_target_pairs={{0,24},{1,25},{2,26},{3,27},{4,28},{5,29},{6,30},{7,31},{8,16},{9,... | collective-permute-start | bytes 196616 | tf_op jit(solution)/shard_map/ppermute | solution.py:23
  5.3 4.5 %collective-permute-start = (bf16[64,512]{1,0:T(8,128)(2,1)}, bf16[64,512]{1,0:T(8,128)(2,1)S(1)}, u32[]{:S(2)}, u32[]{:S(2)}) collective-permute-start(bf16[64,512]{1,0:T(8,128)(2,1)} %sources.1), channel_id=1, source_target_pairs={{0,10},{1,11},{2,8},{3,9},{4,14},{5,15},{6,12},{7,13},{8,2},{9,3},... | collective-permute-start | bytes 196616 | tf_op jit(solution)/shard_map/ppermute | solution.py:23
  8.2 3.9 %collective-permute-start.5 = (bf16[16,2048]{1,0:T(8,128)(2,1)S(1)}, bf16[16,2048]{1,0:T(8,128)(2,1)S(1)}, u32[]{:S(2)}, u32[]{:S(2)}) collective-permute-start(bf16[16,2048]{1,0:T(8,128)(2,1)S(1)} %collective-permute-done.3), channel_id=1, source_target_pairs={{0,24},{1,25},{2,26},{3,27},{4,28},{5,29},{6,30},{7,31},{8,16},{9,... | collective-permute-start | bytes 196616 | tf_op jit(solution)/shard_map/ppermute | solution.py:23
  9.8 5.5 %collective-permute-start.2 = (bf16[64,1024]{1,0:T(8,128)(2,1)S(1)}, bf16[64,1024]{1,0:T(8,128)(2,1)S(1)}, u32[]{:S(2)}, u32[]{:S(2)}) collective-permute-start(bf16[64,1024]{1,0:T(8,128)(2,1)S(1)} %constant_dynamic-update-slice_fusion), channel_id=1, source_target_pairs={{0,9},{1,8},{2,11},{3,10},{4,13},{5,12},{6,15},{7,14},{8,1},{9,0},... | collective-permute-start | bytes 393224 | tf_op jit(solution)/shard_map/ppermute | solution.py:23
  11.0 4.0 %collective-permute-start.1 = (f32[16,128]{1,0:T(8,128)S(1)}, f32[16,128]{1,0:T(8,128)S(1)}, u32[]{:S(2)}, u32[]{:S(2)}) collective-permute-start(f32[16,128]{1,0:T(8,128)S(1)} %get-tuple-element.18), channel_id=1, source_target_pairs={{0,12},{1,13},{2,14},{3,15},{4,8},{5,9},{6,10},{7,11},{8,4},{9,5},... | collective-permute-start | bytes 24584 | tf_op jit(solution)/shard_map/ppermute | solution.py:23
  12.1 3.3 %collective-permute-start.6 = (bf16[32,4096]{1,0:T(8,128)(2,1)S(1)}, bf16[32,4096]{1,0:T(8,128)(2,1)S(1)}, u32[]{:S(2)}, u32[]{:S(2)}) collective-permute-start(bf16[32,4096]{1,0:T(8,128)(2,1)S(1)} %maximum_maximum_fusion.tgt_own), channel_id=1, source_target_pairs={{0,8},{1,9},{2,10},{3,11},{4,12},{5,13},{6,14},{7,15},{8,0},{9,1},... | collective-permute-start | bytes 786440 | tf_op jit(solution)/shard_map/ppermute | solution.py:23
  33.9 9.4 %collective-permute-start.7 = (f32[1,1024]{1,0:T(1,128)S(1)}, f32[1,1024]{1,0:T(1,128)S(1)}, u32[]{:S(2)}, u32[]{:S(2)}) collective-permute-start(f32[1,1024]{1,0:T(1,128)S(1)} %get-tuple-element.25), channel_id=1, source_target_pairs={{0,9},{1,8},{2,11},{3,10},{4,13},{5,12},{6,15},{7,14},{8,1},{9,0},... | collective-permute-start | bytes 12296 | tf_op jit(solution)/shard_map/ppermute | solution.py:23
  43.3 12.2 %collective-permute-start.8 = (f32[1,512]{1,0:T(1,128)S(1)}, f32[1,512]{1,0:T(1,128)S(1)}, u32[]{:S(2)}, u32[]{:S(2)}) collective-permute-start(f32[1,512]{1,0:T(1,128)S(1)} %multiply_add_fusion), channel_id=1, source_target_pairs={{0,10},{1,11},{2,8},{3,9},{4,14},{5,15},{6,12},{7,13},{8,2},{9,3},... | collective-permute-start | bytes 6152 | tf_op jit(solution)/shard_map/ppermute | solution.py:23

commit v6 on v5

--- a/solution.py
+++ b/solution.py
@@ -108,7 +108,7 @@
         out_shape=tuple(pltpu.VMEM((LANES, piece.shape[1]), jnp.bfloat16) for piece in held),
         in_specs=[VMEM] * len(held),
         out_specs=(VMEM,) * len(held),
-        cost_estimate=pl.CostEstimate(flops=4 << 30, bytes_accessed=0, transcendentals=0),
+        cost_estimate=pl.CostEstimate(flops=1 << 30, bytes_accessed=0, transcendentals=0),
         compiler_params=pltpu.CompilerParams(vmem_limit_bytes=8 << 20),
     )(*held)
 
@@ -234,7 +234,7 @@
         beside = flip(targets, col_mask)
         below = flip(targets, row_mask)
         corner = flip(beside, row_mask)
-        bias, _ = lax.optimization_barrier((bias, whole))
+        bias, _ = lax.optimization_barrier((bias, held[1]))
         there = flip(bias, col_mask)
         there, held[-1] = lax.optimization_barrier((there, held[-1]))
         bias = jnp.concatenate([bias, there], axis=0)

time: 56.4 us -> 55.3 us (0.980)
  other arithmetic: 1.56 us -> 0.71 us
    reduce_sum x1, other arithmetic: 0.9 us -> 0.03 us  [on_device(): return 0.5 * jnp.sum(wide * wide, axis=0) - 1.0 / RATE * logs[0]]
  transfers between devices with their start and end apart: 9 -> 9, of which waited for: 3 -> 2; matrix products, arithmetic and copies ran while one was open for 2% -> 0% of each run, Pallas kernels for 35% -> 36%
where the time goes in v6:
time: 55.3 us; the launch traced here: 55.1 us
  Pallas kernels  38.2 us (69%)
  starting transfers between devices  13.8 us (25%)
  waiting for transfers between devices  2.08 us (4%)
  other arithmetic  0.71 us (1%)
    pallas_call x2, Pallas kernels, next_logs(): pl.pallas_call(functools.partial(next_kernel, width), out_shape=pltpu.VME...  18.6 us
    pallas_call x1, Pallas kernels, first_logs(): pl.pallas_call(functools.partial(first_kernel, turn), out_shape=(pltpu.VM...  18.5 us
    ppermute x9, starting transfers between devices, flip(): return lax.ppermute(value, AXES, [(i, i ^ mask) for i in range(n)])  13.8 us
    ppermute x9, waiting for transfers between devices, flip(): return lax.ppermute(value, AXES, [(i, i ^ mask) for i in range(n)])  2.08 us
  transfers between devices with their start and end apart: 9, of which 2 were waited for; matrix products, arithmetic and copies ran while one was open for 0% of the time, Pallas kernels for 36%

profile of v6, /device:TPU:0, one launch (start us, length us, event | category | flops | bytes accessed | tf_op | source)
XLA Modules:
  0.0 55.1 jit_solution(15933924775660379310)
XLA Ops:
  0.0 3.5 %collective-permute-start.3 = (bf16[16,2048]{1,0:T(8,128)(2,1)}, bf16[16,2048]{1,0:T(8,128)(2,1)S(1)}, u32[]{:S(2)}, u32[]{:S(2)}) collective-permute-start(bf16[16,2048]{1,0:T(8,128)(2,1)} %targets.1), channel_id=1, source_target_pairs={{0,12},{1,13},{2,14},{3,15},{4,8},{5,9},{6,10},{7,11},{8,4},{9,5},... | collective-permute-start | bytes 196616 | tf_op jit(solution)/shard_map/ppermute | solution.py:23
  3.5 1.9 %collective-permute-start = (bf16[64,512]{1,0:T(8,128)(2,1)}, bf16[64,512]{1,0:T(8,128)(2,1)S(1)}, u32[]{:S(2)}, u32[]{:S(2)}) collective-permute-start(bf16[64,512]{1,0:T(8,128)(2,1)} %sources.1), channel_id=1, source_target_pairs={{0,10},{1,11},{2,8},{3,9},{4,14},{5,15},{6,12},{7,13},{8,2},{9,3},... | collective-permute-start | bytes 196616 | tf_op jit(solution)/shard_map/ppermute | solution.py:23
  5.3 1.0 %collective-permute-start.4 = (bf16[16,2048]{1,0:T(8,128)(2,1)}, bf16[16,2048]{1,0:T(8,128)(2,1)S(1)}, u32[]{:S(2)}, u32[]{:S(2)}) collective-permute-start(bf16[16,2048]{1,0:T(8,128)(2,1)} %targets.1), channel_id=1, source_target_pairs={{0,24},{1,25},{2,26},{3,27},{4,28},{5,29},{6,30},{7,31},{8,16},{9,... | collective-permute-start | bytes 196616 | tf_op jit(solution)/shard_map/ppermute | solution.py:23
  6.3 0.9 %shard_map.46 = (bf16[64,512]{1,0:T(8,128)(2,1)S(1)}, bf16[16,2048]{1,0:T(8,128)(2,1)S(1)}, f32[16,128]{1,0:T(8,128)S(1)}) custom-call(bf16[64,512]{1,0:T(8,128)(2,1)} %sources.1, bf16[16,2048]{1,0:T(8,128)(2,1)} %targets.1, f32[16,128]{1,0:T(8,128)} %bitcast.5, f32[16,128]{1,0:T(8,128)} %bitcast.6), custom_call_target="tpu_custom_call" | custom-call | tf_op jit(solution)/shard_map/pallas_call | solution.py:52
  7.2 0.0 collective-permute-done.3
  7.3 2.1 %collective-permute-start.5 = (bf16[16,2048]{1,0:T(8,128)(2,1)S(1)}, bf16[16,2048]{1,0:T(8,128)(2,1)S(1)}, u32[]{:S(2)}, u32[]{:S(2)}) collective-permute-start(bf16[16,2048]{1,0:T(8,128)(2,1)S(1)} %collective-permute-done.3), channel_id=1, source_target_pairs={{0,24},{1,25},{2,26},{3,27},{4,28},{5,29},{6,30},{7,31},{8,16},{9,... | collective-permute-start | bytes 196616 | tf_op jit(solution)/shard_map/ppermute | solution.py:23
  9.4 0.0 collective-permute-done.refs_1_
  9.4 1.4 %collective-permute-start.2 = (bf16[64,1024]{1,0:T(8,128)(2,1)S(1)}, bf16[64,1024]{1,0:T(8,128)(2,1)S(1)}, u32[]{:S(2)}, u32[]{:S(2)}) collective-permute-start(bf16[64,1024]{1,0:T(8,128)(2,1)S(1)} %pad_maximum_fusion), channel_id=1, source_target_pairs={{0,9},{1,8},{2,11},{3,10},{4,13},{5,12},{6,15},{7,14},{8,1},{9,0},... | collective-permute-start | bytes 393224 | tf_op jit(solution)/shard_map/ppermute | solution.py:23
  10.8 1.3 %collective-permute-start.1 = (f32[16,128]{1,0:T(8,128)S(1)}, f32[16,128]{1,0:T(8,128)S(1)}, u32[]{:S(2)}, u32[]{:S(2)}) collective-permute-start(f32[16,128]{1,0:T(8,128)S(1)} %get-tuple-element.18), channel_id=1, source_target_pairs={{0,12},{1,13},{2,14},{3,15},{4,8},{5,9},{6,10},{7,11},{8,4},{9,5},... | collective-permute-start | bytes 24584 | tf_op jit(solution)/shard_map/ppermute | solution.py:23
  12.1 0.0 collective-permute-done.4
  12.1 0.0 collective-permute-done.5
  12.1 0.6 %collective-permute-start.6 = (bf16[32,4096]{1,0:T(8,128)(2,1)S(1)}, bf16[32,4096]{1,0:T(8,128)(2,1)S(1)}, u32[]{:S(2)}, u32[]{:S(2)}) collective-permute-start(bf16[32,4096]{1,0:T(8,128)(2,1)S(1)} %maximum_maximum_fusion.tgt_own), channel_id=1, source_target_pairs={{0,8},{1,9},{2,10},{3,11},{4,12},{5,13},{6,14},{7,15},{8,0},{9,1},... | collective-permute-start | bytes 786440 | tf_op jit(solution)/shard_map/ppermute | solution.py:23
  12.7 0.2 copy-done
  12.9 1.8 %collective-permute-done.1 = f32[16,128]{1,0:T(8,128)S(1)} collective-permute-done((f32[16,128]{1,0:T(8,128)S(1)}, f32[16,128]{1,0:T(8,128)S(1)}, u32[]{:S(2)}, u32[]{:S(2)}) %collective-permute-start.1) | collective-permute-done | bytes 8224 | tf_op jit(solution)/shard_map/ppermute | solution.py:23
  14.8 0.2 collective-permute-done.2.refs_2_
  15.0 0.1 shard_map.47
  15.1 0.0 collective-permute-done.6.tgt_far
  15.1 18.5 %shard_map.48 = (f32[1,1024]{1,0:T(1,128)S(1)}, bf16[4096,128]{1,0:T(8,128)(2,1)S(1)}) custom-call(bf16[128,1024]{1,0:T(8,128)(2,1)S(1)} %get-tuple-element.21.placed, bf16[32,4096]{1,0:T(8,128)(2,1)S(1)} %maximum_maximum_fusion.tgt_own, bf16[32,4096]{1,0:T(8,128)(2,1)S(1)} %collective-permute-done.6.tgt_far, f32[1,4096]{1,0:T(1,128)S(1)} %bitcast.4), custom_call_target="tpu_custom_call" | custom-call | flops 1073741824 | bytes 1048576 | tf_op jit(solution)/shard_map/pallas_call | solution.py:183
  33.7 0.1 collective-permute-start.7
  33.8 9.3 %shard_map.50 = f32[1,512]{1,0:T(1,128)S(1)} custom-call(bf16[128,512]{1,0:T(8,128)(2,1)S(1)} %get-tuple-element.26.placed, bf16[4096,128]{1,0:T(8,128)(2,1)S(1)} %get-tuple-element.24.lhs), custom_call_target="tpu_custom_call" | custom-call | flops 536870912 | bytes 1048576 | tf_op jit(solution)/shard_map/pallas_call | solution.py:196
  43.1 0.0 collective-permute-done.7
  43.1 2.1 %collective-permute-start.8 = (f32[1,512]{1,0:T(1,128)S(1)}, f32[1,512]{1,0:T(1,128)S(1)}, u32[]{:S(2)}, u32[]{:S(2)}) collective-permute-start(f32[1,512]{1,0:T(1,128)S(1)} %multiply_add_fusion), channel_id=1, source_target_pairs={{0,10},{1,11},{2,8},{3,9},{4,14},{5,15},{6,12},{7,13},{8,2},{9,3},... | collective-permute-start | bytes 6152 | tf_op jit(solution)/shard_map/ppermute | solution.py:23
  45.2 9.3 %shard_map.49 = f32[1,512]{1,0:T(1,128)S(1)} custom-call(bf16[128,512]{1,0:T(8,128)(2,1)S(1)} %get-tuple-element.20.placed, bf16[4096,128]{1,0:T(8,128)(2,1)S(1)} %get-tuple-element.24.lhs), custom_call_target="tpu_custom_call" | custom-call | flops 536870912 | bytes 1048576 | tf_op jit(solution)/shard_map/pallas_call | solution.py:196
  54.5 0.6 %multiply_subtract_fusion = f32[512]{0:T(512)} fusion(f32[512]{0:T(512)S(1)} %bitcast.7, f32[512]{0:T(512)S(1)} %multiply_reduce_fusion), kind=kLoop, calls=%fused_computation.6 | loop fusion | flops 1024 | bytes 6144 | tf_op jit(solution)/shard_map/sub | solution.py:264
  (8 shorter events, 0.1 us)
Async XLA Ops:
  0.0 7.3 %collective-permute-start.3 = (bf16[16,2048]{1,0:T(8,128)(2,1)}, bf16[16,2048]{1,0:T(8,128)(2,1)S(1)}, u32[]{:S(2)}, u32[]{:S(2)}) collective-permute-start(bf16[16,2048]{1,0:T(8,128)(2,1)} %targets.1), channel_id=1, source_target_pairs={{0,12},{1,13},{2,14},{3,15},{4,8},{5,9},{6,10},{7,11},{8,4},{9,5},... | collective-permute-start | bytes 196616 | tf_op jit(solution)/shard_map/ppermute | solution.py:23
  3.5 5.9 %collective-permute-start = (bf16[64,512]{1,0:T(8,128)(2,1)}, bf16[64,512]{1,0:T(8,128)(2,1)S(1)}, u32[]{:S(2)}, u32[]{:S(2)}) collective-permute-start(bf16[64,512]{1,0:T(8,128)(2,1)} %sources.1), channel_id=1, source_target_pairs={{0,10},{1,11},{2,8},{3,9},{4,14},{5,15},{6,12},{7,13},{8,2},{9,3},... | collective-permute-start | bytes 196616 | tf_op jit(solution)/shard_map/ppermute | solution.py:23
  5.3 6.7 %collective-permute-start.4 = (bf16[16,2048]{1,0:T(8,128)(2,1)}, bf16[16,2048]{1,0:T(8,128)(2,1)S(1)}, u32[]{:S(2)}, u32[]{:S(2)}) collective-permute-start(bf16[16,2048]{1,0:T(8,128)(2,1)} %targets.1), channel_id=1, source_target_pairs={{0,24},{1,25},{2,26},{3,27},{4,28},{5,29},{6,30},{7,31},{8,16},{9,... | collective-permute-start | bytes 196616 | tf_op jit(solution)/shard_map/ppermute | solution.py:23
  7.3 4.8 %collective-permute-start.5 = (bf16[16,2048]{1,0:T(8,128)(2,1)S(1)}, bf16[16,2048]{1,0:T(8,128)(2,1)S(1)}, u32[]{:S(2)}, u32[]{:S(2)}) collective-permute-start(bf16[16,2048]{1,0:T(8,128)(2,1)S(1)} %collective-permute-done.3), channel_id=1, source_target_pairs={{0,24},{1,25},{2,26},{3,27},{4,28},{5,29},{6,30},{7,31},{8,16},{9,... | collective-permute-start | bytes 196616 | tf_op jit(solution)/shard_map/ppermute | solution.py:23
  9.4 5.6 %collective-permute-start.2 = (bf16[64,1024]{1,0:T(8,128)(2,1)S(1)}, bf16[64,1024]{1,0:T(8,128)(2,1)S(1)}, u32[]{:S(2)}, u32[]{:S(2)}) collective-permute-start(bf16[64,1024]{1,0:T(8,128)(2,1)S(1)} %pad_maximum_fusion), channel_id=1, source_target_pairs={{0,9},{1,8},{2,11},{3,10},{4,13},{5,12},{6,15},{7,14},{8,1},{9,0},... | collective-permute-start | bytes 393224 | tf_op jit(solution)/shard_map/ppermute | solution.py:23
  10.8 4.0 %collective-permute-start.1 = (f32[16,128]{1,0:T(8,128)S(1)}, f32[16,128]{1,0:T(8,128)S(1)}, u32[]{:S(2)}, u32[]{:S(2)}) collective-permute-start(f32[16,128]{1,0:T(8,128)S(1)} %get-tuple-element.18), channel_id=1, source_target_pairs={{0,12},{1,13},{2,14},{3,15},{4,8},{5,9},{6,10},{7,11},{8,4},{9,5},... | collective-permute-start | bytes 24584 | tf_op jit(solution)/shard_map/ppermute | solution.py:23
  12.1 0.8 %copy-start = (bf16[64,512]{1,0:T(8,128)(2,1)S(1)}, bf16[64,512]{1,0:T(8,128)(2,1)}, u32[]{:S(2)}) copy-start(bf16[64,512]{1,0:T(8,128)(2,1)} %sources.1) | copy-start | bytes 196612
  12.1 3.0 %collective-permute-start.6 = (bf16[32,4096]{1,0:T(8,128)(2,1)S(1)}, bf16[32,4096]{1,0:T(8,128)(2,1)S(1)}, u32[]{:S(2)}, u32[]{:S(2)}) collective-permute-start(bf16[32,4096]{1,0:T(8,128)(2,1)S(1)} %maximum_maximum_fusion.tgt_own), channel_id=1, source_target_pairs={{0,8},{1,9},{2,10},{3,11},{4,12},{5,13},{6,14},{7,15},{8,0},{9,1},... | collective-permute-start | bytes 786440 | tf_op jit(solution)/shard_map/ppermute | solution.py:23
  33.7 9.4 %collective-permute-start.7 = (f32[1,1024]{1,0:T(1,128)S(1)}, f32[1,1024]{1,0:T(1,128)S(1)}, u32[]{:S(2)}, u32[]{:S(2)}) collective-permute-start(f32[1,1024]{1,0:T(1,128)S(1)} %get-tuple-element.25), channel_id=1, source_target_pairs={{0,9},{1,8},{2,11},{3,10},{4,13},{5,12},{6,15},{7,14},{8,1},{9,0},... | collective-permute-start | bytes 12296 | tf_op jit(solution)/shard_map/ppermute | solution.py:23
  43.1 11.4 %collective-permute-start.8 = (f32[1,512]{1,0:T(1,128)S(1)}, f32[1,512]{1,0:T(1,128)S(1)}, u32[]{:S(2)}, u32[]{:S(2)}) collective-permute-start(f32[1,512]{1,0:T(1,128)S(1)} %multiply_add_fusion), channel_id=1, source_target_pairs={{0,10},{1,11},{2,8},{3,9},{4,14},{5,15},{6,12},{7,13},{8,2},{9,3},... | collective-permute-start | bytes 6152 | tf_op jit(solution)/shard_map/ppermute | solution.py:23

commit v7 on v6

--- a/solution.py
+++ b/solution.py
@@ -62,14 +62,13 @@
     )(sources, targets, potentials.reshape(rows, LANES), log_mass.reshape(rows, LANES))
 
 
-def place_targets(turn, tgt_own, tgt_far, bias_ref, lhs):
+def place_targets(tgt_own, tgt_far, bias_ref, lhs):
     count = tgt_own.shape[1]
     width = tgt_own.shape[0] + tgt_far.shape[0]
     step = min(1024, count)
     for start in range(0, count, step):
         cols = slice(start, start + step)
-        halves = [tgt_own[:, cols], tgt_far[:, cols]]
-        points = jnp.concatenate(halves if start < turn else halves[::-1], axis=0)
+        points = jnp.concatenate([tgt_own[:, cols], tgt_far[:, cols]], axis=0)
         wide = points.astype(jnp.float32)
         half = 0.5 * jnp.sum(wide * wide, axis=0, keepdims=True)
         first, second, third = split3(bias_ref[:, cols] - half)
@@ -163,8 +162,8 @@
             out_ref[:, cols] = row_top + jnp.log2(row_sum)
 
 
-def first_kernel(turn, placed, tgt_own, tgt_far, bias_ref, out_ref, lhs, rhs):
-    place_targets(turn, tgt_own, tgt_far, bias_ref, lhs)
+def first_kernel(placed, tgt_own, tgt_far, bias_ref, out_ref, lhs, rhs):
+    place_targets(tgt_own, tgt_far, bias_ref, lhs)
     rhs[...] = placed[...]
     log_sums(tgt_own.shape[0] + tgt_far.shape[0], lhs, rhs, out_ref)
 
@@ -178,10 +177,10 @@
     return pl.CostEstimate(flops=2 * rows * count * LANES, bytes_accessed=2 * count * LANES, transcendentals=rows * count)
 
 
-def first_logs(turn, placed, tgt_own, tgt_far, bias):
+def first_logs(placed, tgt_own, tgt_far, bias):
     count, rows = tgt_own.shape[1], placed.shape[1]
     return pl.pallas_call(
-        functools.partial(first_kernel, turn),
+        first_kernel,
         out_shape=(pltpu.VMEM((1, rows), jnp.float32), pltpu.VMEM((count, LANES), jnp.bfloat16)),
         in_specs=[VMEM] * 4,
         out_specs=(VMEM, VMEM),
@@ -230,29 +229,27 @@
         held.append(flip(whole, mask))
     held[0] = sources_here
     if len(col_masks) == 1 and len(row_masks) == 1:
-        col_mask, row_mask = col_masks[0] | n_tgt, row_masks[0] | n_tgt
-        beside = flip(targets, col_mask)
-        below = flip(targets, row_mask)
-        corner = flip(beside, row_mask)
+        beside = flip(targets, col_masks[0])
+        below = flip(targets, row_masks[0])
+        corner = flip(beside, row_masks[0])
         bias, _ = lax.optimization_barrier((bias, held[1]))
-        there = flip(bias, col_mask)
+        there = flip(bias, col_masks[0])
         there, held[-1] = lax.optimization_barrier((there, held[-1]))
         bias = jnp.concatenate([bias, there], axis=0)
         upper = jnp.concatenate([targets_here, beside], axis=1)
         lower = jnp.concatenate([below, corner], axis=1)
         own = jnp.concatenate([upper, lower], axis=0)
-        order, turn = (0, 3, 1, 2), targets.shape[1]
     else:
         own = gather(gather(targets_here, col_masks, 1), row_masks, 0)
         bias = gather(bias, col_masks, 0)
-        order, turn = (*range(0, n_src, 2), *range(1, n_src, 2)), own.shape[1]
     bias = bias.reshape(1, -1)
     far = flip(own, n_tgt)
+    order = (*range(0, n_src, 2), *range(1, n_src, 2))
     placed = placed_sources(order, held)
 
     owned = sources.shape[1]
     arrived = []
-    logs, lhs = first_logs(turn, placed[-1], own, far, bias)
+    logs, lhs = first_logs(placed[-1], own, far, bias)
     for k in range(shared, 0, -1):
         for other in arrived:
             logs = join(logs, other[:, owned << (k - 1) : owned << k])

time: 55.3 us -> 55.3 us (level)
  starting transfers between devices: 13.8 us -> 12.7 us
  waiting for transfers between devices: 2.08 us -> 3.06 us
    ppermute x9, starting transfers between devices: 13.8 us -> 12.7 us  [flip(): return lax.ppermute(value, AXES, [(i, i ^ mask) for i in range(n)])]
    ppermute x9, waiting for transfers between devices: 2.08 us -> 3.06 us  [flip(): return lax.ppermute(value, AXES, [(i, i ^ mask) for i in range(n)])]
  transfers between devices with their start and end apart: 9 -> 9, of which waited for: 2 -> 3; matrix products, arithmetic and copies ran while one was open for 0% -> 0% of each run, Pallas kernels for 36% -> 36%
where the time goes in v7:
time: 55.3 us; the launch traced here: 55.1 us
  Pallas kernels  38.2 us (69%)
  starting transfers between devices  12.7 us (23%)
  waiting for transfers between devices  3.06 us (6%)
  other arithmetic  0.7 us (1%)
    pallas_call x2, Pallas kernels, next_logs(): pl.pallas_call(functools.partial(next_kernel, width), out_shape=pltpu.VME...  18.6 us
    pallas_call x1, Pallas kernels, first_logs(): pl.pallas_call(first_kernel, out_shape=(pltpu.VMEM((1, rows), jnp.float32...  18.5 us
    ppermute x9, starting transfers between devices, flip(): return lax.ppermute(value, AXES, [(i, i ^ mask) for i in range(n)])  12.7 us
    ppermute x9, waiting for transfers between devices, flip(): return lax.ppermute(value, AXES, [(i, i ^ mask) for i in range(n)])  3.06 us
  transfers between devices with their start and end apart: 9, of which 3 were waited for; matrix products, arithmetic and copies ran while one was open for 0% of the time, Pallas kernels for 36%

profile of v7, /device:TPU:0, one launch (start us, length us, event | category | flops | bytes accessed | tf_op | source)
XLA Modules:
  0.0 55.1 jit_solution(9439418069098725133)
XLA Ops:
  0.0 4.0 %collective-permute-start.3 = (bf16[16,2048]{1,0:T(8,128)(2,1)}, bf16[16,2048]{1,0:T(8,128)(2,1)S(1)}, u32[]{:S(2)}, u32[]{:S(2)}) collective-permute-start(bf16[16,2048]{1,0:T(8,128)(2,1)} %targets.1), channel_id=1, source_target_pairs={{0,4},{1,5},{2,6},{3,7},{4,0},{5,1},{6,2},{7,3},{8,12},{9,13},{10,... | collective-permute-start | bytes 196616 | tf_op jit(solution)/shard_map/ppermute | solution.py:23
  4.0 0.7 %collective-permute-start = (bf16[64,512]{1,0:T(8,128)(2,1)}, bf16[64,512]{1,0:T(8,128)(2,1)S(1)}, u32[]{:S(2)}, u32[]{:S(2)}) collective-permute-start(bf16[64,512]{1,0:T(8,128)(2,1)} %sources.1), channel_id=1, source_target_pairs={{0,10},{1,11},{2,8},{3,9},{4,14},{5,15},{6,12},{7,13},{8,2},{9,3},... | collective-permute-start | bytes 196616 | tf_op jit(solution)/shard_map/ppermute | solution.py:23
  4.8 1.5 %collective-permute-start.4 = (bf16[16,2048]{1,0:T(8,128)(2,1)}, bf16[16,2048]{1,0:T(8,128)(2,1)S(1)}, u32[]{:S(2)}, u32[]{:S(2)}) collective-permute-start(bf16[16,2048]{1,0:T(8,128)(2,1)} %targets.1), channel_id=1, source_target_pairs={{0,16},{1,17},{2,18},{3,19},{4,20},{5,21},{6,22},{7,23},{8,24},{9,... | collective-permute-start | bytes 196616 | tf_op jit(solution)/shard_map/ppermute | solution.py:23
  6.3 0.9 %shard_map.46 = (bf16[64,512]{1,0:T(8,128)(2,1)S(1)}, bf16[16,2048]{1,0:T(8,128)(2,1)S(1)}, f32[16,128]{1,0:T(8,128)S(1)}) custom-call(bf16[64,512]{1,0:T(8,128)(2,1)} %sources.1, bf16[16,2048]{1,0:T(8,128)(2,1)} %targets.1, f32[16,128]{1,0:T(8,128)} %bitcast.5, f32[16,128]{1,0:T(8,128)} %bitcast.6), custom_call_target="tpu_custom_call" | custom-call | tf_op jit(solution)/shard_map/pallas_call | solution.py:52
  7.2 0.0 collective-permute-done.3
  7.3 1.9 %collective-permute-start.5 = (bf16[16,2048]{1,0:T(8,128)(2,1)S(1)}, bf16[16,2048]{1,0:T(8,128)(2,1)S(1)}, u32[]{:S(2)}, u32[]{:S(2)}) collective-permute-start(bf16[16,2048]{1,0:T(8,128)(2,1)S(1)} %collective-permute-done.3), channel_id=1, source_target_pairs={{0,16},{1,17},{2,18},{3,19},{4,20},{5,21},{6,22},{7,23},{8,24},{9,... | collective-permute-start | bytes 196616 | tf_op jit(solution)/shard_map/ppermute | solution.py:23
  9.2 0.0 collective-permute-done.refs_1_
  9.2 0.9 %collective-permute-start.2 = (bf16[64,1024]{1,0:T(8,128)(2,1)S(1)}, bf16[64,1024]{1,0:T(8,128)(2,1)S(1)}, u32[]{:S(2)}, u32[]{:S(2)}) collective-permute-start(bf16[64,1024]{1,0:T(8,128)(2,1)S(1)} %pad_maximum_fusion), channel_id=1, source_target_pairs={{0,9},{1,8},{2,11},{3,10},{4,13},{5,12},{6,15},{7,14},{8,1},{9,0},... | collective-permute-start | bytes 393224 | tf_op jit(solution)/shard_map/ppermute | solution.py:23
  10.1 0.9 %collective-permute-start.1 = (f32[16,128]{1,0:T(8,128)S(1)}, f32[16,128]{1,0:T(8,128)S(1)}, u32[]{:S(2)}, u32[]{:S(2)}) collective-permute-start(f32[16,128]{1,0:T(8,128)S(1)} %get-tuple-element.18), channel_id=1, source_target_pairs={{0,4},{1,5},{2,6},{3,7},{4,0},{5,1},{6,2},{7,3},{8,12},{9,13},{10,... | collective-permute-start | bytes 24584 | tf_op jit(solution)/shard_map/ppermute | solution.py:23
  11.1 0.9 %collective-permute-done.5 = bf16[16,2048]{1,0:T(8,128)(2,1)S(1)} collective-permute-done((bf16[16,2048]{1,0:T(8,128)(2,1)S(1)}, bf16[16,2048]{1,0:T(8,128)(2,1)S(1)}, u32[]{:S(2)}, u32[]{:S(2)}) %collective-permute-start.5) | collective-permute-done | bytes 65568 | tf_op jit(solution)/shard_map/ppermute | solution.py:23
  12.0 0.4 collective-permute-start.6
  12.4 0.4 copy-done
  12.9 1.8 %collective-permute-done.1 = f32[16,128]{1,0:T(8,128)S(1)} collective-permute-done((f32[16,128]{1,0:T(8,128)S(1)}, f32[16,128]{1,0:T(8,128)S(1)}, u32[]{:S(2)}, u32[]{:S(2)}) %collective-permute-start.1) | collective-permute-done | bytes 8224 | tf_op jit(solution)/shard_map/ppermute | solution.py:23
  14.7 0.3 collective-permute-done.2.refs_2_
  15.0 0.1 shard_map.47
  15.1 0.0 collective-permute-done.6.tgt_far
  15.1 18.5 %shard_map.48 = (f32[1,1024]{1,0:T(1,128)S(1)}, bf16[4096,128]{1,0:T(8,128)(2,1)S(1)}) custom-call(bf16[128,1024]{1,0:T(8,128)(2,1)S(1)} %get-tuple-element.21.placed, bf16[32,4096]{1,0:T(8,128)(2,1)S(1)} %maximum_maximum_fusion.tgt_own, bf16[32,4096]{1,0:T(8,128)(2,1)S(1)} %collective-permute-done.6.tgt_far, f32[1,4096]{1,0:T(1,128)S(1)} %bitcast.4), custom_call_target="tpu_custom_call" | custom-call | flops 1073741824 | bytes 1048576 | tf_op jit(solution)/shard_map/pallas_call | solution.py:182
  33.7 0.1 collective-permute-start.7
  33.8 9.3 %shard_map.50 = f32[1,512]{1,0:T(1,128)S(1)} custom-call(bf16[128,512]{1,0:T(8,128)(2,1)S(1)} %get-tuple-element.26.placed, bf16[4096,128]{1,0:T(8,128)(2,1)S(1)} %get-tuple-element.24.lhs), custom_call_target="tpu_custom_call" | custom-call | flops 536870912 | bytes 1048576 | tf_op jit(solution)/shard_map/pallas_call | solution.py:195
  43.1 0.0 collective-permute-done.7
  43.1 2.1 %collective-permute-start.8 = (f32[1,512]{1,0:T(1,128)S(1)}, f32[1,512]{1,0:T(1,128)S(1)}, u32[]{:S(2)}, u32[]{:S(2)}) collective-permute-start(f32[1,512]{1,0:T(1,128)S(1)} %multiply_add_fusion), channel_id=1, source_target_pairs={{0,10},{1,11},{2,8},{3,9},{4,14},{5,15},{6,12},{7,13},{8,2},{9,3},... | collective-permute-start | bytes 6152 | tf_op jit(solution)/shard_map/ppermute | solution.py:23
  45.2 9.3 %shard_map.49 = f32[1,512]{1,0:T(1,128)S(1)} custom-call(bf16[128,512]{1,0:T(8,128)(2,1)S(1)} %get-tuple-element.20.placed, bf16[4096,128]{1,0:T(8,128)(2,1)S(1)} %get-tuple-element.24.lhs), custom_call_target="tpu_custom_call" | custom-call | flops 536870912 | bytes 1048576 | tf_op jit(solution)/shard_map/pallas_call | solution.py:195
  54.5 0.0 collective-permute-done.8
  54.5 0.6 %multiply_subtract_fusion = f32[512]{0:T(512)} fusion(f32[512]{0:T(512)S(1)} %bitcast.7, f32[512]{0:T(512)S(1)} %multiply_reduce_fusion), kind=kLoop, calls=%fused_computation.6 | loop fusion | flops 1024 | bytes 6144 | tf_op jit(solution)/shard_map/sub | solution.py:261
  (8 shorter events, 0.1 us)
Async XLA Ops:
  0.0 7.3 %collective-permute-start.3 = (bf16[16,2048]{1,0:T(8,128)(2,1)}, bf16[16,2048]{1,0:T(8,128)(2,1)S(1)}, u32[]{:S(2)}, u32[]{:S(2)}) collective-permute-start(bf16[16,2048]{1,0:T(8,128)(2,1)} %targets.1), channel_id=1, source_target_pairs={{0,4},{1,5},{2,6},{3,7},{4,0},{5,1},{6,2},{7,3},{8,12},{9,13},{10,... | collective-permute-start | bytes 196616 | tf_op jit(solution)/shard_map/ppermute | solution.py:23
  4.0 5.2 %collective-permute-start = (bf16[64,512]{1,0:T(8,128)(2,1)}, bf16[64,512]{1,0:T(8,128)(2,1)S(1)}, u32[]{:S(2)}, u32[]{:S(2)}) collective-permute-start(bf16[64,512]{1,0:T(8,128)(2,1)} %sources.1), channel_id=1, source_target_pairs={{0,10},{1,11},{2,8},{3,9},{4,14},{5,15},{6,12},{7,13},{8,2},{9,3},... | collective-permute-start | bytes 196616 | tf_op jit(solution)/shard_map/ppermute | solution.py:23
  4.8 6.3 %collective-permute-start.4 = (bf16[16,2048]{1,0:T(8,128)(2,1)}, bf16[16,2048]{1,0:T(8,128)(2,1)S(1)}, u32[]{:S(2)}, u32[]{:S(2)}) collective-permute-start(bf16[16,2048]{1,0:T(8,128)(2,1)} %targets.1), channel_id=1, source_target_pairs={{0,16},{1,17},{2,18},{3,19},{4,20},{5,21},{6,22},{7,23},{8,24},{9,... | collective-permute-start | bytes 196616 | tf_op jit(solution)/shard_map/ppermute | solution.py:23
  7.3 4.7 %collective-permute-start.5 = (bf16[16,2048]{1,0:T(8,128)(2,1)S(1)}, bf16[16,2048]{1,0:T(8,128)(2,1)S(1)}, u32[]{:S(2)}, u32[]{:S(2)}) collective-permute-start(bf16[16,2048]{1,0:T(8,128)(2,1)S(1)} %collective-permute-done.3), channel_id=1, source_target_pairs={{0,16},{1,17},{2,18},{3,19},{4,20},{5,21},{6,22},{7,23},{8,24},{9,... | collective-permute-start | bytes 196616 | tf_op jit(solution)/shard_map/ppermute | solution.py:23
  9.2 5.8 %collective-permute-start.2 = (bf16[64,1024]{1,0:T(8,128)(2,1)S(1)}, bf16[64,1024]{1,0:T(8,128)(2,1)S(1)}, u32[]{:S(2)}, u32[]{:S(2)}) collective-permute-start(bf16[64,1024]{1,0:T(8,128)(2,1)S(1)} %pad_maximum_fusion), channel_id=1, source_target_pairs={{0,9},{1,8},{2,11},{3,10},{4,13},{5,12},{6,15},{7,14},{8,1},{9,0},... | collective-permute-start | bytes 393224 | tf_op jit(solution)/shard_map/ppermute | solution.py:23
  10.1 4.5 %collective-permute-start.1 = (f32[16,128]{1,0:T(8,128)S(1)}, f32[16,128]{1,0:T(8,128)S(1)}, u32[]{:S(2)}, u32[]{:S(2)}) collective-permute-start(f32[16,128]{1,0:T(8,128)S(1)} %get-tuple-element.18), channel_id=1, source_target_pairs={{0,4},{1,5},{2,6},{3,7},{4,0},{5,1},{6,2},{7,3},{8,12},{9,13},{10,... | collective-permute-start | bytes 24584 | tf_op jit(solution)/shard_map/ppermute | solution.py:23
  12.0 0.8 %copy-start = (bf16[64,512]{1,0:T(8,128)(2,1)S(1)}, bf16[64,512]{1,0:T(8,128)(2,1)}, u32[]{:S(2)}) copy-start(bf16[64,512]{1,0:T(8,128)(2,1)} %sources.1) | copy-start | bytes 196612
  12.0 3.1 %collective-permute-start.6 = (bf16[32,4096]{1,0:T(8,128)(2,1)S(1)}, bf16[32,4096]{1,0:T(8,128)(2,1)S(1)}, u32[]{:S(2)}, u32[]{:S(2)}) collective-permute-start(bf16[32,4096]{1,0:T(8,128)(2,1)S(1)} %maximum_maximum_fusion.tgt_own), channel_id=1, source_target_pairs={{0,8},{1,9},{2,10},{3,11},{4,12},{5,13},{6,14},{7,15},{8,0},{9,1},... | collective-permute-start | bytes 786440 | tf_op jit(solution)/shard_map/ppermute | solution.py:23
  33.7 9.4 %collective-permute-start.7 = (f32[1,1024]{1,0:T(1,128)S(1)}, f32[1,1024]{1,0:T(1,128)S(1)}, u32[]{:S(2)}, u32[]{:S(2)}) collective-permute-start(f32[1,1024]{1,0:T(1,128)S(1)} %get-tuple-element.25), channel_id=1, source_target_pairs={{0,9},{1,8},{2,11},{3,10},{4,13},{5,12},{6,15},{7,14},{8,1},{9,0},... | collective-permute-start | bytes 12296 | tf_op jit(solution)/shard_map/ppermute | solution.py:23
  43.1 11.4 %collective-permute-start.8 = (f32[1,512]{1,0:T(1,128)S(1)}, f32[1,512]{1,0:T(1,128)S(1)}, u32[]{:S(2)}, u32[]{:S(2)}) collective-permute-start(f32[1,512]{1,0:T(1,128)S(1)} %multiply_add_fusion), channel_id=1, source_target_pairs={{0,10},{1,11},{2,8},{3,9},{4,14},{5,15},{6,12},{7,13},{8,2},{9,3},... | collective-permute-start | bytes 6152 | tf_op jit(solution)/shard_map/ppermute | solution.py:23

commit v8 on v7

--- a/solution.py
+++ b/solution.py
@@ -112,41 +112,43 @@
     )(*held)
 
 
-def log_sums(width, lhs, rhs, out_ref):
-    count, rows = lhs.shape[0], rhs.shape[1]
+def references(width, lhs, placed, out_ref):
+    chunk = lhs[:CHUNK, :]
+    for start in range(0, placed.shape[1], WIDE):
+        cols = slice(start, start + WIDE)
+        found = jnp.dot(chunk, placed[:, cols], preferred_element_type=jnp.float32)
+        out_ref[:, cols] = jnp.max(jnp.max(found.reshape(CHUNK // 8, 8, WIDE), axis=0), axis=0, keepdims=True)
+
+
+def log_sums(width, lhs, placed, high_ref, out_ref):
+    count, rows = lhs.shape[0], placed.shape[1]
+    place = lax.broadcasted_iota(jnp.int32, (LANES - width, WIDE), 0)
 
     def product(j, block):
         chunk = pl.ds(pl.multiple_of(j * CHUNK, CHUNK), CHUNK)
         found = jnp.dot(lhs[chunk, :], block, preferred_element_type=jnp.float32)
         return found.reshape(CHUNK // 8, 8, found.shape[1])
 
-    place = lax.broadcasted_iota(jnp.int32, (LANES - width, WIDE), 0)
+    worst = jnp.zeros((1, WIDE), jnp.float32)
     for start in range(0, rows, WIDE):
         cols = slice(start, start + WIDE)
-        high = jnp.max(jnp.max(product(0, rhs[:, cols]), axis=0), axis=0, keepdims=True)
+        high = high_ref[:, cols]
         extra = jnp.where(place < 3, 1.0, 0.0)
         for k, part in enumerate(split3(-high)):
             extra = jnp.where(place == 3 + k, part, extra)
-        rhs[width:, cols] = extra.astype(jnp.bfloat16)
-        out_ref[:, cols] = high * RATE
-    worst = jnp.zeros((1, WIDE), jnp.float32)
-    for start in range(0, rows, WIDE):
-        cols = slice(start, start + WIDE)
-        block = rhs[:, cols]
+        block = jnp.concatenate([placed[:width, cols], extra.astype(jnp.bfloat16)], axis=0)
         total = jnp.zeros((8, WIDE), jnp.float32)
         for j in range(count // CHUNK):
             total = total + jnp.sum(jnp.exp2(product(j, block) * RATE), axis=0)
         row_sum = jnp.sum(total, axis=0, keepdims=True)
-        out_ref[:, cols] += jnp.log2(row_sum)
+        out_ref[:, cols] = high * RATE + jnp.log2(row_sum)
         worst = jnp.maximum(worst, row_sum)
 
     @pl.when(jnp.logical_not(jnp.max(worst) < jnp.inf))
     def _():
         for start in range(0, rows, WIDE):
             cols = slice(start, start + WIDE)
-            extra = jnp.where(place < 3, 1.0, 0.0)
-            rhs[width:, cols] = extra.astype(jnp.bfloat16)
-            block = rhs[:, cols]
+            block = placed[:, cols]
 
             def step(j, carry):
                 top, total = carry
@@ -162,15 +164,16 @@
             out_ref[:, cols] = row_top + jnp.log2(row_sum)
 
 
-def first_kernel(placed, tgt_own, tgt_far, bias_ref, out_ref, lhs, rhs):
+def first_kernel(placed, tgt_own, tgt_far, bias_ref, out_ref, lhs, high):
     place_targets(tgt_own, tgt_far, bias_ref, lhs)
-    rhs[...] = placed[...]
-    log_sums(tgt_own.shape[0] + tgt_far.shape[0], lhs, rhs, out_ref)
-
-
-def next_kernel(width, placed, lhs, out_ref, rhs):
-    rhs[...] = placed[...]
-    log_sums(width, lhs, rhs, out_ref)
+    width = tgt_own.shape[0] + tgt_far.shape[0]
+    references(width, lhs, placed, high)
+    log_sums(width, lhs, placed, high, out_ref)
+
+
+def next_kernel(width, placed, lhs, out_ref, high):
+    references(width, lhs, placed, high)
+    log_sums(width, lhs, placed, high, out_ref)
 
 
 def estimate(rows, count):
@@ -184,7 +187,7 @@
         out_shape=(pltpu.VMEM((1, rows), jnp.float32), pltpu.VMEM((count, LANES), jnp.bfloat16)),
         in_specs=[VMEM] * 4,
         out_specs=(VMEM, VMEM),
-        scratch_shapes=[pltpu.VMEM((LANES, rows), jnp.bfloat16)],
+        scratch_shapes=[pltpu.VMEM((1, rows), jnp.float32)],
         cost_estimate=estimate(rows, count),
         compiler_params=pltpu.CompilerParams(vmem_limit_bytes=48 << 20),
     )(placed, tgt_own, tgt_far, bias)
@@ -197,7 +200,7 @@
         out_shape=pltpu.VMEM((1, rows), jnp.float32),
         in_specs=[VMEM] * 2,
         out_specs=VMEM,
-        scratch_shapes=[pltpu.VMEM((LANES, rows), jnp.bfloat16)],
+        scratch_shapes=[pltpu.VMEM((1, rows), jnp.float32)],
         cost_estimate=estimate(rows, count),
         compiler_params=pltpu.CompilerParams(vmem_limit_bytes=48 << 20),
     )(placed, lhs)

time: 55.3 us -> 55.4 us (level)
  no operation moved by 1% of the time
where the time goes in v8:
time: 55.4 us; the launch traced here: 55.2 us
  Pallas kernels  38.2 us (69%)
  starting transfers between devices  12.7 us (23%)
  waiting for transfers between devices  3.06 us (6%)
  other arithmetic  0.7 us (1%)
    pallas_call x2, Pallas kernels, next_logs(): pl.pallas_call(functools.partial(next_kernel, width), out_shape=pltpu.VME...  18.6 us
    pallas_call x1, Pallas kernels, first_logs(): pl.pallas_call(first_kernel, out_shape=(pltpu.VMEM((1, rows), jnp.float32...  18.5 us
    ppermute x9, starting transfers between devices, flip(): return lax.ppermute(value, AXES, [(i, i ^ mask) for i in range(n)])  12.7 us
    ppermute x9, waiting for transfers between devices, flip(): return lax.ppermute(value, AXES, [(i, i ^ mask) for i in range(n)])  3.06 us
  transfers between devices with their start and end apart: 9, of which 3 were waited for; matrix products, arithmetic and copies ran while one was open for 0% of the time, Pallas kernels for 36%

profile of v8, /device:TPU:0, one launch (start us, length us, event | category | flops | bytes accessed | tf_op | source)
XLA Modules:
  0.0 55.2 jit_solution(16684409758603195829)
XLA Ops:
  0.0 4.0 %collective-permute-start.3 = (bf16[16,2048]{1,0:T(8,128)(2,1)}, bf16[16,2048]{1,0:T(8,128)(2,1)S(1)}, u32[]{:S(2)}, u32[]{:S(2)}) collective-permute-start(bf16[16,2048]{1,0:T(8,128)(2,1)} %targets.1), channel_id=1, source_target_pairs={{0,4},{1,5},{2,6},{3,7},{4,0},{5,1},{6,2},{7,3},{8,12},{9,13},{10,... | collective-permute-start | bytes 196616 | tf_op jit(solution)/shard_map/ppermute | solution.py:23
  4.0 0.7 %collective-permute-start = (bf16[64,512]{1,0:T(8,128)(2,1)}, bf16[64,512]{1,0:T(8,128)(2,1)S(1)}, u32[]{:S(2)}, u32[]{:S(2)}) collective-permute-start(bf16[64,512]{1,0:T(8,128)(2,1)} %sources.1), channel_id=1, source_target_pairs={{0,10},{1,11},{2,8},{3,9},{4,14},{5,15},{6,12},{7,13},{8,2},{9,3},... | collective-permute-start | bytes 196616 | tf_op jit(solution)/shard_map/ppermute | solution.py:23
  4.8 1.5 %collective-permute-start.4 = (bf16[16,2048]{1,0:T(8,128)(2,1)}, bf16[16,2048]{1,0:T(8,128)(2,1)S(1)}, u32[]{:S(2)}, u32[]{:S(2)}) collective-permute-start(bf16[16,2048]{1,0:T(8,128)(2,1)} %targets.1), channel_id=1, source_target_pairs={{0,16},{1,17},{2,18},{3,19},{4,20},{5,21},{6,22},{7,23},{8,24},{9,... | collective-permute-start | bytes 196616 | tf_op jit(solution)/shard_map/ppermute | solution.py:23
  6.3 0.9 %shard_map.46 = (bf16[64,512]{1,0:T(8,128)(2,1)S(1)}, bf16[16,2048]{1,0:T(8,128)(2,1)S(1)}, f32[16,128]{1,0:T(8,128)S(1)}) custom-call(bf16[64,512]{1,0:T(8,128)(2,1)} %sources.1, bf16[16,2048]{1,0:T(8,128)(2,1)} %targets.1, f32[16,128]{1,0:T(8,128)} %bitcast.5, f32[16,128]{1,0:T(8,128)} %bitcast.6), custom_call_target="tpu_custom_call" | custom-call | tf_op jit(solution)/shard_map/pallas_call | solution.py:52
  7.2 0.0 collective-permute-done.3
  7.3 1.9 %collective-permute-start.5 = (bf16[16,2048]{1,0:T(8,128)(2,1)S(1)}, bf16[16,2048]{1,0:T(8,128)(2,1)S(1)}, u32[]{:S(2)}, u32[]{:S(2)}) collective-permute-start(bf16[16,2048]{1,0:T(8,128)(2,1)S(1)} %collective-permute-done.3), channel_id=1, source_target_pairs={{0,16},{1,17},{2,18},{3,19},{4,20},{5,21},{6,22},{7,23},{8,24},{9,... | collective-permute-start | bytes 196616 | tf_op jit(solution)/shard_map/ppermute | solution.py:23
  9.2 0.0 collective-permute-done.refs_1_
  9.2 0.9 %collective-permute-start.2 = (bf16[64,1024]{1,0:T(8,128)(2,1)S(1)}, bf16[64,1024]{1,0:T(8,128)(2,1)S(1)}, u32[]{:S(2)}, u32[]{:S(2)}) collective-permute-start(bf16[64,1024]{1,0:T(8,128)(2,1)S(1)} %pad_maximum_fusion), channel_id=1, source_target_pairs={{0,9},{1,8},{2,11},{3,10},{4,13},{5,12},{6,15},{7,14},{8,1},{9,0},... | collective-permute-start | bytes 393224 | tf_op jit(solution)/shard_map/ppermute | solution.py:23
  10.1 0.9 %collective-permute-start.1 = (f32[16,128]{1,0:T(8,128)S(1)}, f32[16,128]{1,0:T(8,128)S(1)}, u32[]{:S(2)}, u32[]{:S(2)}) collective-permute-start(f32[16,128]{1,0:T(8,128)S(1)} %get-tuple-element.18), channel_id=1, source_target_pairs={{0,4},{1,5},{2,6},{3,7},{4,0},{5,1},{6,2},{7,3},{8,12},{9,13},{10,... | collective-permute-start | bytes 24584 | tf_op jit(solution)/shard_map/ppermute | solution.py:23
  11.1 0.9 %collective-permute-done.5 = bf16[16,2048]{1,0:T(8,128)(2,1)S(1)} collective-permute-done((bf16[16,2048]{1,0:T(8,128)(2,1)S(1)}, bf16[16,2048]{1,0:T(8,128)(2,1)S(1)}, u32[]{:S(2)}, u32[]{:S(2)}) %collective-permute-start.5) | collective-permute-done | bytes 65568 | tf_op jit(solution)/shard_map/ppermute | solution.py:23
  12.0 0.4 collective-permute-start.6
  12.4 0.4 copy-done
  12.9 1.8 %collective-permute-done.1 = f32[16,128]{1,0:T(8,128)S(1)} collective-permute-done((f32[16,128]{1,0:T(8,128)S(1)}, f32[16,128]{1,0:T(8,128)S(1)}, u32[]{:S(2)}, u32[]{:S(2)}) %collective-permute-start.1) | collective-permute-done | bytes 8224 | tf_op jit(solution)/shard_map/ppermute | solution.py:23
  14.7 0.3 collective-permute-done.2.refs_2_
  15.0 0.1 shard_map.47
  15.1 0.0 collective-permute-done.6.tgt_far
  15.1 18.5 %shard_map.48 = (f32[1,1024]{1,0:T(1,128)S(1)}, bf16[4096,128]{1,0:T(8,128)(2,1)S(1)}) custom-call(bf16[128,1024]{1,0:T(8,128)(2,1)S(1)} %get-tuple-element.21.placed, bf16[32,4096]{1,0:T(8,128)(2,1)S(1)} %maximum_maximum_fusion.tgt_own, bf16[32,4096]{1,0:T(8,128)(2,1)S(1)} %collective-permute-done.6.tgt_far, f32[1,4096]{1,0:T(1,128)S(1)} %bitcast.4), custom_call_target="tpu_custom_call" | custom-call | flops 1073741824 | bytes 1048576 | tf_op jit(solution)/shard_map/pallas_call | solution.py:185
  33.7 0.1 collective-permute-start.7
  33.8 9.3 %shard_map.50 = f32[1,512]{1,0:T(1,128)S(1)} custom-call(bf16[128,512]{1,0:T(8,128)(2,1)S(1)} %get-tuple-element.26.placed, bf16[4096,128]{1,0:T(8,128)(2,1)S(1)} %get-tuple-element.24.lhs), custom_call_target="tpu_custom_call" | custom-call | flops 536870912 | bytes 1048576 | tf_op jit(solution)/shard_map/pallas_call | solution.py:198
  43.1 0.0 collective-permute-done.7
  43.1 2.1 %collective-permute-start.8 = (f32[1,512]{1,0:T(1,128)S(1)}, f32[1,512]{1,0:T(1,128)S(1)}, u32[]{:S(2)}, u32[]{:S(2)}) collective-permute-start(f32[1,512]{1,0:T(1,128)S(1)} %multiply_add_fusion), channel_id=1, source_target_pairs={{0,10},{1,11},{2,8},{3,9},{4,14},{5,15},{6,12},{7,13},{8,2},{9,3},... | collective-permute-start | bytes 6152 | tf_op jit(solution)/shard_map/ppermute | solution.py:23
  45.2 9.3 %shard_map.49 = f32[1,512]{1,0:T(1,128)S(1)} custom-call(bf16[128,512]{1,0:T(8,128)(2,1)S(1)} %get-tuple-element.20.placed, bf16[4096,128]{1,0:T(8,128)(2,1)S(1)} %get-tuple-element.24.lhs), custom_call_target="tpu_custom_call" | custom-call | flops 536870912 | bytes 1048576 | tf_op jit(solution)/shard_map/pallas_call | solution.py:198
  54.5 0.0 collective-permute-done.8
  54.6 0.6 %multiply_subtract_fusion = f32[512]{0:T(512)} fusion(f32[512]{0:T(512)S(1)} %bitcast.7, f32[512]{0:T(512)S(1)} %multiply_reduce_fusion), kind=kLoop, calls=%fused_computation.6 | loop fusion | flops 1024 | bytes 6144 | tf_op jit(solution)/shard_map/sub | solution.py:264
  (8 shorter events, 0.1 us)
Async XLA Ops:
  0.0 7.3 %collective-permute-start.3 = (bf16[16,2048]{1,0:T(8,128)(2,1)}, bf16[16,2048]{1,0:T(8,128)(2,1)S(1)}, u32[]{:S(2)}, u32[]{:S(2)}) collective-permute-start(bf16[16,2048]{1,0:T(8,128)(2,1)} %targets.1), channel_id=1, source_target_pairs={{0,4},{1,5},{2,6},{3,7},{4,0},{5,1},{6,2},{7,3},{8,12},{9,13},{10,... | collective-permute-start | bytes 196616 | tf_op jit(solution)/shard_map/ppermute | solution.py:23
  4.0 5.2 %collective-permute-start = (bf16[64,512]{1,0:T(8,128)(2,1)}, bf16[64,512]{1,0:T(8,128)(2,1)S(1)}, u32[]{:S(2)}, u32[]{:S(2)}) collective-permute-start(bf16[64,512]{1,0:T(8,128)(2,1)} %sources.1), channel_id=1, source_target_pairs={{0,10},{1,11},{2,8},{3,9},{4,14},{5,15},{6,12},{7,13},{8,2},{9,3},... | collective-permute-start | bytes 196616 | tf_op jit(solution)/shard_map/ppermute | solution.py:23
  4.8 6.3 %collective-permute-start.4 = (bf16[16,2048]{1,0:T(8,128)(2,1)}, bf16[16,2048]{1,0:T(8,128)(2,1)S(1)}, u32[]{:S(2)}, u32[]{:S(2)}) collective-permute-start(bf16[16,2048]{1,0:T(8,128)(2,1)} %targets.1), channel_id=1, source_target_pairs={{0,16},{1,17},{2,18},{3,19},{4,20},{5,21},{6,22},{7,23},{8,24},{9,... | collective-permute-start | bytes 196616 | tf_op jit(solution)/shard_map/ppermute | solution.py:23
  7.3 4.7 %collective-permute-start.5 = (bf16[16,2048]{1,0:T(8,128)(2,1)S(1)}, bf16[16,2048]{1,0:T(8,128)(2,1)S(1)}, u32[]{:S(2)}, u32[]{:S(2)}) collective-permute-start(bf16[16,2048]{1,0:T(8,128)(2,1)S(1)} %collective-permute-done.3), channel_id=1, source_target_pairs={{0,16},{1,17},{2,18},{3,19},{4,20},{5,21},{6,22},{7,23},{8,24},{9,... | collective-permute-start | bytes 196616 | tf_op jit(solution)/shard_map/ppermute | solution.py:23
  9.2 5.8 %collective-permute-start.2 = (bf16[64,1024]{1,0:T(8,128)(2,1)S(1)}, bf16[64,1024]{1,0:T(8,128)(2,1)S(1)}, u32[]{:S(2)}, u32[]{:S(2)}) collective-permute-start(bf16[64,1024]{1,0:T(8,128)(2,1)S(1)} %pad_maximum_fusion), channel_id=1, source_target_pairs={{0,9},{1,8},{2,11},{3,10},{4,13},{5,12},{6,15},{7,14},{8,1},{9,0},... | collective-permute-start | bytes 393224 | tf_op jit(solution)/shard_map/ppermute | solution.py:23
  10.1 4.5 %collective-permute-start.1 = (f32[16,128]{1,0:T(8,128)S(1)}, f32[16,128]{1,0:T(8,128)S(1)}, u32[]{:S(2)}, u32[]{:S(2)}) collective-permute-start(f32[16,128]{1,0:T(8,128)S(1)} %get-tuple-element.18), channel_id=1, source_target_pairs={{0,4},{1,5},{2,6},{3,7},{4,0},{5,1},{6,2},{7,3},{8,12},{9,13},{10,... | collective-permute-start | bytes 24584 | tf_op jit(solution)/shard_map/ppermute | solution.py:23
  12.0 0.8 %copy-start = (bf16[64,512]{1,0:T(8,128)(2,1)S(1)}, bf16[64,512]{1,0:T(8,128)(2,1)}, u32[]{:S(2)}) copy-start(bf16[64,512]{1,0:T(8,128)(2,1)} %sources.1) | copy-start | bytes 196612
  12.0 3.1 %collective-permute-start.6 = (bf16[32,4096]{1,0:T(8,128)(2,1)S(1)}, bf16[32,4096]{1,0:T(8,128)(2,1)S(1)}, u32[]{:S(2)}, u32[]{:S(2)}) collective-permute-start(bf16[32,4096]{1,0:T(8,128)(2,1)S(1)} %maximum_maximum_fusion.tgt_own), channel_id=1, source_target_pairs={{0,8},{1,9},{2,10},{3,11},{4,12},{5,13},{6,14},{7,15},{8,0},{9,1},... | collective-permute-start | bytes 786440 | tf_op jit(solution)/shard_map/ppermute | solution.py:23
  33.7 9.4 %collective-permute-start.7 = (f32[1,1024]{1,0:T(1,128)S(1)}, f32[1,1024]{1,0:T(1,128)S(1)}, u32[]{:S(2)}, u32[]{:S(2)}) collective-permute-start(f32[1,1024]{1,0:T(1,128)S(1)} %get-tuple-element.25), channel_id=1, source_target_pairs={{0,9},{1,8},{2,11},{3,10},{4,13},{5,12},{6,15},{7,14},{8,1},{9,0},... | collective-permute-start | bytes 12296 | tf_op jit(solution)/shard_map/ppermute | solution.py:23
  43.1 11.4 %collective-permute-start.8 = (f32[1,512]{1,0:T(1,128)S(1)}, f32[1,512]{1,0:T(1,128)S(1)}, u32[]{:S(2)}, u32[]{:S(2)}) collective-permute-start(f32[1,512]{1,0:T(1,128)S(1)} %multiply_add_fusion), channel_id=1, source_target_pairs={{0,10},{1,11},{2,8},{3,9},{4,14},{5,15},{6,12},{7,13},{8,2},{9,3},... | collective-permute-start | bytes 6152 | tf_op jit(solution)/shard_map/ppermute | solution.py:23

commit v9 on v7

--- a/solution.py
+++ b/solution.py
@@ -255,8 +255,9 @@
             logs = join(logs, other[:, owned << (k - 1) : owned << k])
         arrived.append(flip(logs, masks[k - 1]))
         logs = next_logs(sources.shape[0], placed[k - 1], lhs)
-    for other in arrived:
-        logs = join(logs, other[:, :owned])
+    parts = [logs, *(other[:, :owned] for other in arrived)]
+    top = functools.reduce(jnp.maximum, parts)
+    logs = top + jnp.log2(sum(jnp.exp2(part - top) for part in parts))
     wide = sources.astype(jnp.float32)
     return 0.5 * jnp.sum(wide * wide, axis=0) - (1.0 / RATE) * logs[0]
 

time: 55.3 us -> 55.3 us (level)
  no operation moved by 1% of the time
where the time goes in v9:
time: 55.3 us; the launch traced here: 55.1 us
  Pallas kernels  38.2 us (69%)
  starting transfers between devices  12.7 us (23%)
  waiting for transfers between devices  3.06 us (6%)
  other arithmetic  0.7 us (1%)
    pallas_call x2, Pallas kernels, next_logs(): pl.pallas_call(functools.partial(next_kernel, width), out_shape=pltpu.VME...  18.6 us
    pallas_call x1, Pallas kernels, first_logs(): pl.pallas_call(first_kernel, out_shape=(pltpu.VMEM((1, rows), jnp.float32...  18.5 us
    ppermute x9, starting transfers between devices, flip(): return lax.ppermute(value, AXES, [(i, i ^ mask) for i in range(n)])  12.7 us
    ppermute x9, waiting for transfers between devices, flip(): return lax.ppermute(value, AXES, [(i, i ^ mask) for i in range(n)])  3.06 us
  transfers between devices with their start and end apart: 9, of which 3 were waited for; matrix products, arithmetic and copies ran while one was open for 0% of the time, Pallas kernels for 36%

profile of v9, /device:TPU:0, one launch (start us, length us, event | category | flops | bytes accessed | tf_op | source)
XLA Modules:
  0.0 55.1 jit_solution(13256766826127297354)
XLA Ops:
  0.0 4.0 %collective-permute-start.3 = (bf16[16,2048]{1,0:T(8,128)(2,1)}, bf16[16,2048]{1,0:T(8,128)(2,1)S(1)}, u32[]{:S(2)}, u32[]{:S(2)}) collective-permute-start(bf16[16,2048]{1,0:T(8,128)(2,1)} %targets.1), channel_id=1, source_target_pairs={{0,4},{1,5},{2,6},{3,7},{4,0},{5,1},{6,2},{7,3},{8,12},{9,13},{10,... | collective-permute-start | bytes 196616 | tf_op jit(solution)/shard_map/ppermute | solution.py:23
  4.0 0.7 %collective-permute-start = (bf16[64,512]{1,0:T(8,128)(2,1)}, bf16[64,512]{1,0:T(8,128)(2,1)S(1)}, u32[]{:S(2)}, u32[]{:S(2)}) collective-permute-start(bf16[64,512]{1,0:T(8,128)(2,1)} %sources.1), channel_id=1, source_target_pairs={{0,10},{1,11},{2,8},{3,9},{4,14},{5,15},{6,12},{7,13},{8,2},{9,3},... | collective-permute-start | bytes 196616 | tf_op jit(solution)/shard_map/ppermute | solution.py:23
  4.8 1.5 %collective-permute-start.4 = (bf16[16,2048]{1,0:T(8,128)(2,1)}, bf16[16,2048]{1,0:T(8,128)(2,1)S(1)}, u32[]{:S(2)}, u32[]{:S(2)}) collective-permute-start(bf16[16,2048]{1,0:T(8,128)(2,1)} %targets.1), channel_id=1, source_target_pairs={{0,16},{1,17},{2,18},{3,19},{4,20},{5,21},{6,22},{7,23},{8,24},{9,... | collective-permute-start | bytes 196616 | tf_op jit(solution)/shard_map/ppermute | solution.py:23
  6.3 0.9 %shard_map.46 = (bf16[64,512]{1,0:T(8,128)(2,1)S(1)}, bf16[16,2048]{1,0:T(8,128)(2,1)S(1)}, f32[16,128]{1,0:T(8,128)S(1)}) custom-call(bf16[64,512]{1,0:T(8,128)(2,1)} %sources.1, bf16[16,2048]{1,0:T(8,128)(2,1)} %targets.1, f32[16,128]{1,0:T(8,128)} %bitcast.5, f32[16,128]{1,0:T(8,128)} %bitcast.6), custom_call_target="tpu_custom_call" | custom-call | tf_op jit(solution)/shard_map/pallas_call | solution.py:52
  7.2 0.0 collective-permute-done.3
  7.3 1.9 %collective-permute-start.5 = (bf16[16,2048]{1,0:T(8,128)(2,1)S(1)}, bf16[16,2048]{1,0:T(8,128)(2,1)S(1)}, u32[]{:S(2)}, u32[]{:S(2)}) collective-permute-start(bf16[16,2048]{1,0:T(8,128)(2,1)S(1)} %collective-permute-done.3), channel_id=1, source_target_pairs={{0,16},{1,17},{2,18},{3,19},{4,20},{5,21},{6,22},{7,23},{8,24},{9,... | collective-permute-start | bytes 196616 | tf_op jit(solution)/shard_map/ppermute | solution.py:23
  9.2 0.0 collective-permute-done.refs_1_
  9.2 0.9 %collective-permute-start.2 = (bf16[64,1024]{1,0:T(8,128)(2,1)S(1)}, bf16[64,1024]{1,0:T(8,128)(2,1)S(1)}, u32[]{:S(2)}, u32[]{:S(2)}) collective-permute-start(bf16[64,1024]{1,0:T(8,128)(2,1)S(1)} %pad_maximum_fusion), channel_id=1, source_target_pairs={{0,9},{1,8},{2,11},{3,10},{4,13},{5,12},{6,15},{7,14},{8,1},{9,0},... | collective-permute-start | bytes 393224 | tf_op jit(solution)/shard_map/ppermute | solution.py:23
  10.1 0.9 %collective-permute-start.1 = (f32[16,128]{1,0:T(8,128)S(1)}, f32[16,128]{1,0:T(8,128)S(1)}, u32[]{:S(2)}, u32[]{:S(2)}) collective-permute-start(f32[16,128]{1,0:T(8,128)S(1)} %get-tuple-element.18), channel_id=1, source_target_pairs={{0,4},{1,5},{2,6},{3,7},{4,0},{5,1},{6,2},{7,3},{8,12},{9,13},{10,... | collective-permute-start | bytes 24584 | tf_op jit(solution)/shard_map/ppermute | solution.py:23
  11.1 0.9 %collective-permute-done.5 = bf16[16,2048]{1,0:T(8,128)(2,1)S(1)} collective-permute-done((bf16[16,2048]{1,0:T(8,128)(2,1)S(1)}, bf16[16,2048]{1,0:T(8,128)(2,1)S(1)}, u32[]{:S(2)}, u32[]{:S(2)}) %collective-permute-start.5) | collective-permute-done | bytes 65568 | tf_op jit(solution)/shard_map/ppermute | solution.py:23
  12.0 0.4 collective-permute-start.6
  12.4 0.4 copy-done
  12.9 1.8 %collective-permute-done.1 = f32[16,128]{1,0:T(8,128)S(1)} collective-permute-done((f32[16,128]{1,0:T(8,128)S(1)}, f32[16,128]{1,0:T(8,128)S(1)}, u32[]{:S(2)}, u32[]{:S(2)}) %collective-permute-start.1) | collective-permute-done | bytes 8224 | tf_op jit(solution)/shard_map/ppermute | solution.py:23
  14.7 0.3 collective-permute-done.2.refs_2_
  15.0 0.1 shard_map.47
  15.1 0.0 collective-permute-done.6.tgt_far
  15.1 18.5 %shard_map.48 = (f32[1,1024]{1,0:T(1,128)S(1)}, bf16[4096,128]{1,0:T(8,128)(2,1)S(1)}) custom-call(bf16[128,1024]{1,0:T(8,128)(2,1)S(1)} %get-tuple-element.21.placed, bf16[32,4096]{1,0:T(8,128)(2,1)S(1)} %maximum_maximum_fusion.tgt_own, bf16[32,4096]{1,0:T(8,128)(2,1)S(1)} %collective-permute-done.6.tgt_far, f32[1,4096]{1,0:T(1,128)S(1)} %bitcast.4), custom_call_target="tpu_custom_call" | custom-call | flops 1073741824 | bytes 1048576 | tf_op jit(solution)/shard_map/pallas_call | solution.py:182
  33.7 0.1 collective-permute-start.7
  33.8 9.3 %shard_map.50 = f32[1,512]{1,0:T(1,128)S(1)} custom-call(bf16[128,512]{1,0:T(8,128)(2,1)S(1)} %get-tuple-element.26.placed, bf16[4096,128]{1,0:T(8,128)(2,1)S(1)} %get-tuple-element.24.lhs), custom_call_target="tpu_custom_call" | custom-call | flops 536870912 | bytes 1048576 | tf_op jit(solution)/shard_map/pallas_call | solution.py:195
  43.1 0.0 collective-permute-done.7
  43.1 2.1 %collective-permute-start.8 = (f32[1,512]{1,0:T(1,128)S(1)}, f32[1,512]{1,0:T(1,128)S(1)}, u32[]{:S(2)}, u32[]{:S(2)}) collective-permute-start(f32[1,512]{1,0:T(1,128)S(1)} %multiply_add_fusion), channel_id=1, source_target_pairs={{0,10},{1,11},{2,8},{3,9},{4,14},{5,15},{6,12},{7,13},{8,2},{9,3},... | collective-permute-start | bytes 6152 | tf_op jit(solution)/shard_map/ppermute | solution.py:23
  45.2 9.3 %shard_map.49 = f32[1,512]{1,0:T(1,128)S(1)} custom-call(bf16[128,512]{1,0:T(8,128)(2,1)S(1)} %get-tuple-element.20.placed, bf16[4096,128]{1,0:T(8,128)(2,1)S(1)} %get-tuple-element.24.lhs), custom_call_target="tpu_custom_call" | custom-call | flops 536870912 | bytes 1048576 | tf_op jit(solution)/shard_map/pallas_call | solution.py:195
  54.5 0.0 collective-permute-done.8
  54.5 0.6 %multiply_subtract_fusion = f32[512]{0:T(512)} fusion(f32[512]{0:T(512)S(1)} %bitcast.7, f32[512]{0:T(512)S(1)} %multiply_reduce_fusion), kind=kLoop, calls=%fused_computation.6 | loop fusion | flops 1024 | bytes 6144 | tf_op jit(solution)/shard_map/sub | solution.py:262
  (8 shorter events, 0.1 us)
Async XLA Ops:
  0.0 7.3 %collective-permute-start.3 = (bf16[16,2048]{1,0:T(8,128)(2,1)}, bf16[16,2048]{1,0:T(8,128)(2,1)S(1)}, u32[]{:S(2)}, u32[]{:S(2)}) collective-permute-start(bf16[16,2048]{1,0:T(8,128)(2,1)} %targets.1), channel_id=1, source_target_pairs={{0,4},{1,5},{2,6},{3,7},{4,0},{5,1},{6,2},{7,3},{8,12},{9,13},{10,... | collective-permute-start | bytes 196616 | tf_op jit(solution)/shard_map/ppermute | solution.py:23
  4.0 5.2 %collective-permute-start = (bf16[64,512]{1,0:T(8,128)(2,1)}, bf16[64,512]{1,0:T(8,128)(2,1)S(1)}, u32[]{:S(2)}, u32[]{:S(2)}) collective-permute-start(bf16[64,512]{1,0:T(8,128)(2,1)} %sources.1), channel_id=1, source_target_pairs={{0,10},{1,11},{2,8},{3,9},{4,14},{5,15},{6,12},{7,13},{8,2},{9,3},... | collective-permute-start | bytes 196616 | tf_op jit(solution)/shard_map/ppermute | solution.py:23
  4.8 6.3 %collective-permute-start.4 = (bf16[16,2048]{1,0:T(8,128)(2,1)}, bf16[16,2048]{1,0:T(8,128)(2,1)S(1)}, u32[]{:S(2)}, u32[]{:S(2)}) collective-permute-start(bf16[16,2048]{1,0:T(8,128)(2,1)} %targets.1), channel_id=1, source_target_pairs={{0,16},{1,17},{2,18},{3,19},{4,20},{5,21},{6,22},{7,23},{8,24},{9,... | collective-permute-start | bytes 196616 | tf_op jit(solution)/shard_map/ppermute | solution.py:23
  7.3 4.7 %collective-permute-start.5 = (bf16[16,2048]{1,0:T(8,128)(2,1)S(1)}, bf16[16,2048]{1,0:T(8,128)(2,1)S(1)}, u32[]{:S(2)}, u32[]{:S(2)}) collective-permute-start(bf16[16,2048]{1,0:T(8,128)(2,1)S(1)} %collective-permute-done.3), channel_id=1, source_target_pairs={{0,16},{1,17},{2,18},{3,19},{4,20},{5,21},{6,22},{7,23},{8,24},{9,... | collective-permute-start | bytes 196616 | tf_op jit(solution)/shard_map/ppermute | solution.py:23
  9.2 5.8 %collective-permute-start.2 = (bf16[64,1024]{1,0:T(8,128)(2,1)S(1)}, bf16[64,1024]{1,0:T(8,128)(2,1)S(1)}, u32[]{:S(2)}, u32[]{:S(2)}) collective-permute-start(bf16[64,1024]{1,0:T(8,128)(2,1)S(1)} %pad_maximum_fusion), channel_id=1, source_target_pairs={{0,9},{1,8},{2,11},{3,10},{4,13},{5,12},{6,15},{7,14},{8,1},{9,0},... | collective-permute-start | bytes 393224 | tf_op jit(solution)/shard_map/ppermute | solution.py:23
  10.1 4.5 %collective-permute-start.1 = (f32[16,128]{1,0:T(8,128)S(1)}, f32[16,128]{1,0:T(8,128)S(1)}, u32[]{:S(2)}, u32[]{:S(2)}) collective-permute-start(f32[16,128]{1,0:T(8,128)S(1)} %get-tuple-element.18), channel_id=1, source_target_pairs={{0,4},{1,5},{2,6},{3,7},{4,0},{5,1},{6,2},{7,3},{8,12},{9,13},{10,... | collective-permute-start | bytes 24584 | tf_op jit(solution)/shard_map/ppermute | solution.py:23
  12.0 0.8 %copy-start = (bf16[64,512]{1,0:T(8,128)(2,1)S(1)}, bf16[64,512]{1,0:T(8,128)(2,1)}, u32[]{:S(2)}) copy-start(bf16[64,512]{1,0:T(8,128)(2,1)} %sources.1) | copy-start | bytes 196612
  12.0 3.1 %collective-permute-start.6 = (bf16[32,4096]{1,0:T(8,128)(2,1)S(1)}, bf16[32,4096]{1,0:T(8,128)(2,1)S(1)}, u32[]{:S(2)}, u32[]{:S(2)}) collective-permute-start(bf16[32,4096]{1,0:T(8,128)(2,1)S(1)} %maximum_maximum_fusion.tgt_own), channel_id=1, source_target_pairs={{0,8},{1,9},{2,10},{3,11},{4,12},{5,13},{6,14},{7,15},{8,0},{9,1},... | collective-permute-start | bytes 786440 | tf_op jit(solution)/shard_map/ppermute | solution.py:23
  33.7 9.4 %collective-permute-start.7 = (f32[1,1024]{1,0:T(1,128)S(1)}, f32[1,1024]{1,0:T(1,128)S(1)}, u32[]{:S(2)}, u32[]{:S(2)}) collective-permute-start(f32[1,1024]{1,0:T(1,128)S(1)} %get-tuple-element.25), channel_id=1, source_target_pairs={{0,9},{1,8},{2,11},{3,10},{4,13},{5,12},{6,15},{7,14},{8,1},{9,0},... | collective-permute-start | bytes 12296 | tf_op jit(solution)/shard_map/ppermute | solution.py:23
  43.1 11.4 %collective-permute-start.8 = (f32[1,512]{1,0:T(1,128)S(1)}, f32[1,512]{1,0:T(1,128)S(1)}, u32[]{:S(2)}, u32[]{:S(2)}) collective-permute-start(f32[1,512]{1,0:T(1,128)S(1)} %multiply_add_fusion), channel_id=1, source_target_pairs={{0,10},{1,11},{2,8},{3,9},{4,14},{5,15},{6,12},{7,13},{8,2},{9,3},... | collective-permute-start | bytes 6152 | tf_op jit(solution)/shard_map/ppermute | solution.py:23
